TPU v7x, 1024 devices: a whole 8x8x8 slice. The times are simulated.
1024 devices in a mesh: node: 64 (over z, y), local: 16 (over x, core).
Axes of the slice: x: 8, y: 8, z: 8, core: 2. Of those that a mesh axis runs over, the one named last changes fastest.
Arguments:
- grad_out: bfloat16 [8192, 7168], P('node', 'local'), may hold values from -6 to 6
- route_expert: int32 [8192, 2], P('node'), may hold values from 0 to 31, all different within a row; in each aligned block of 128 rows (0 to 127, 128 to 255, ...) at most 10 rows name the same one
- gate_prob: float32 [8192, 2], P('node'), may hold values from 0.05 to 1
- saved_gate: bfloat16 [64, 1024, 640], P('node'), may hold values from -6 to 6
- saved_up: bfloat16 [64, 1024, 640], P('node'), may hold values from -6 to 6
- w_gate: bfloat16 [64, 7168, 1024], P('node', 'local'), may hold values from -0.125 to 0.125
- w_up: bfloat16 [64, 7168, 1024], P('node', 'local'), may hold values from -0.125 to 0.125
- w_down: bfloat16 [64, 1024, 7168], P('node', None, 'local'), may hold values from -0.03125 to 0.03125
Outputs:
- grad_in: bfloat16 [8192, 7168], P('node', 'local')
- grad_prob: bfloat16 [8192, 2], P('node')
Inputs may be any that keep to these rules, and one draw needn't show every extreme that they name: `route_expert`: A token names 2 different experts. Among the 128 tokens of one node group no expert is named more than 10 times, a bound that some block reaches.
All inputs are finite; a program needn't handle non-finite values.
Results may differ from a plain program's by a relative error of at most 0.027.
Values may be sent and summed in bfloat16 or wider, within the bound.
No kernel may reach another device: no remote copies, remote signals or barrier semaphores. Data moves between devices by JAX's collectives and lax.ppermute only.
A program may use at most 32 MiB of HBM per device.

v0:
```python
import jax
import jax.numpy as jnp
from jax import lax
from jax.sharding import PartitionSpec as P

FULL_PRECISION = lax.Precision.HIGHEST


def slot_table(routes, experts, capacity):
    tokens = routes.shape[0]
    labels = jnp.arange(experts, dtype=jnp.int32)
    named = routes[:, :, None] == labels[None, None, :]
    onehot = jnp.sum(named.astype(jnp.float32), axis=1)
    positions = jnp.arange(tokens, dtype=jnp.int32)
    earlier_mask = (positions[:, None] > positions[None, :]).astype(jnp.float32)
    before = jnp.dot(earlier_mask, onehot, precision=FULL_PRECISION)
    picked = jnp.sum(jnp.where(named, before[:, None, :], 0.0), axis=2)
    slot_index = routes * capacity + picked.astype(jnp.int32)
    places = jnp.arange(experts * capacity, dtype=jnp.int32)
    return slot_index[None, :, :] == places[:, None, None]


def unit_grads(grad_units, gate_saved, up_saved):
    gate_value = gate_saved.astype(jnp.float32)
    up_value = up_saved.astype(jnp.float32)
    sigmoid_gate = jax.nn.sigmoid(gate_value)
    activation = gate_value * sigmoid_gate
    prob_part = jnp.sum(activation * up_value * grad_units, axis=0)
    grad_gate = (
        grad_units * up_value * sigmoid_gate * (1.0 + gate_value * (1.0 - sigmoid_gate))
    ).astype(jnp.bfloat16)
    grad_upper = (grad_units * activation).astype(jnp.bfloat16)
    return (grad_gate, grad_upper, prob_part)


def shards(grad_out, route_expert, gate_prob, saved_gate, saved_up, w_gate, w_up, w_down):
    groups = lax.axis_size("node")
    experts = groups // 2
    slots_all = saved_gate.shape[2]
    capacity = slots_all // groups
    feat_width = grad_out.shape[1]
    slot_match = slot_table(route_expert, experts, capacity)
    dispatch_mask = jnp.any(slot_match, axis=2).astype(jnp.bfloat16)
    outgoing = jnp.dot(dispatch_mask, grad_out, preferred_element_type=jnp.float32).astype(
        jnp.bfloat16
    )
    outgoing = jnp.repeat(outgoing.reshape(experts, capacity, feat_width), 2, axis=0).reshape(
        groups * capacity, feat_width
    )
    arrived = lax.all_to_all(outgoing, "node", split_axis=0, concat_axis=0, tiled=True)
    down_local = w_down[0]
    gate_local = w_gate[0]
    up_local = w_up[0]
    grad_units = lax.psum_scatter(
        lax.dot_general(
            down_local, arrived, (((1,), (1,)), ((), ())), preferred_element_type=jnp.float32
        ).astype(jnp.bfloat16),
        "local",
        scatter_dimension=0,
        tiled=True,
    ).astype(jnp.float32)
    unit_share = grad_units.shape[0]
    unit_start = lax.axis_index("local") * unit_share
    gate_slice = lax.dynamic_slice_in_dim(saved_gate[0], unit_start, unit_share, 0)
    up_slice = lax.dynamic_slice_in_dim(saved_up[0], unit_start, unit_share, 0)
    grad_gate, grad_upper, prob_part = unit_grads(grad_units, gate_slice, up_slice)
    prob_grad = lax.psum(prob_part, "local")
    running = jnp.dot(
        gate_local,
        lax.all_gather(grad_gate, "local", axis=0, tiled=True),
        preferred_element_type=jnp.float32,
    )
    route_grad = running + jnp.dot(
        up_local,
        lax.all_gather(grad_upper, "local", axis=0, tiled=True),
        preferred_element_type=jnp.float32,
    )
    returned, prob_back = (
        lax.all_to_all(
            route_grad.astype(jnp.bfloat16), "node", split_axis=1, concat_axis=1, tiled=True
        ),
        lax.all_to_all(
            prob_grad.astype(jnp.bfloat16)[None, :], "node", split_axis=1, concat_axis=1, tiled=True
        ),
    )
    summed_rows = jnp.sum(
        returned.astype(jnp.float32).reshape(feat_width, experts, 2, capacity), axis=2
    ).reshape(feat_width, experts * capacity)
    summed_probs = jnp.sum(
        prob_back[0].astype(jnp.float32).reshape(experts, 2, capacity), axis=1
    ).reshape(experts * capacity)
    weights = jnp.sum(jnp.where(slot_match, gate_prob[None, :, :], 0.0), axis=2)
    grad_in = lax.dot_general(
        weights, summed_rows, (((0,), (1,)), ((), ())), precision=FULL_PRECISION
    )
    grad_prob = jnp.sum(jnp.where(slot_match, summed_probs[:, None, None], 0.0), axis=0)
    return (grad_in.astype(jnp.bfloat16), grad_prob.astype(jnp.bfloat16))


def solution(mesh):
    return jax.shard_map(
        shards,
        mesh=mesh,
        in_specs=(
            P("node", "local"),
            P("node", None),
            P("node", None),
            P("node", None, None),
            P("node", None, None),
            P("node", "local", None),
            P("node", "local", None),
            P("node", None, "local"),
        ),
        out_specs=(P("node", "local"), P("node", None)),
        check_vma=False,
    )
```

profile of v0, /device:TPU:6, one launch (start us, length us, event | category | flops | bytes accessed | tf_op | source)
XLA Modules:
  0.0 274.0 jit_solution(254205678381474667)
XLA Ops:
  7.2 0.8 convert_reduce_fusion.1
  8.1 0.8 select_reduce_fusion.2
  8.9 0.7 convert_add_fusion
  9.6 1.1 convolution_convert_fusion.1
  11.0 53.0 %all_to_all.31 = bf16[64,10,448]{2,1,0:T(8,128)(2,1)S(1)} all-to-all(bf16[64,10,448]{2,1,0:T(8,128)(2,1)S(1)} %bitcast.43), channel_id=1, replica_groups=mesh['node'=64,'local'=16] {'node'}, dimensions={0} | all-to-all | bytes 1146880 | tf_op jit(solution)/shard_map/all_to_all | solution.py:50
  64.0 0.4 all_to_all.22
  64.4 0.9 fusion
  65.3 1.5 copy.42
  66.8 53.9 %reduce-scatter.4.cloned.1.call-done = bf16[64,640]{1,0:T(8,128)(2,1)} async-done(((bf16[1024,640]{1,0:T(8,128)(2,1)}), bf16[64,640]{1,0:T(8,128)(2,1)}) %reduce-scatter.4.cloned.1.call-update) | async-done | bytes 81936 | tf_op jit(solution)/shard_map/reduce_scatter | solution.py:54
  120.8 1.7 fusion.10
  122.6 0.7 all-gather.5.cloned.1.call-update
  123.3 25.3 %psum.7 = bf16[640]{0:T(1024)(128)(2,1)S(1)} all-reduce(f32[640]{0:T(1024)S(1)} %get-tuple-element.5), channel_id=1, replica_groups=mesh['node'=64,'local'=16] {'local'}, use_global_device_ids=true, to_apply=%region_7.8 | all-reduce | flops 640 | bytes 3840 | tf_op jit(solution)/shard_map/psum | solution.py:67
  148.6 0.8 all_to_all.27
  149.3 13.9 %all-to-all-start.2 = ((bf16[1,64,10]{2,0,1:T(2,128)(2,1)}), bf16[1,64,10]{2,0,1:T(2,128)(2,1)S(1)}, u32[]{:S(2)}, u32[]{:S(2)}) async-start(bf16[1,64,10]{2,0,1:T(2,128)(2,1)} %all_to_all.27), calls=%async_computation.2 | async-start | bytes 65536 | tf_op jit(solution)/shard_map/all_to_all | solution.py:82
  163.2 7.3 %all-gather.3.cloned.1.call-done = bf16[1024,640]{1,0:T(8,128)(2,1)} async-done(((bf16[64,640]{1,0:T(8,128)(2,1)}), bf16[1024,640]{1,0:T(8,128)(2,1)}) %all-gather.3.cloned.1.call-update) | async-done | bytes 1310736 | tf_op jit(solution)/shard_map/all_gather | solution.py:70
  170.6 3.2 %fusion.4 = f32[640,448]{0,1:T(8,128)} fusion(bf16[1024,640]{1,0:T(8,128)(2,1)} %all-gather.3.cloned.1.call-done, bf16[1,448,1024]{2,1,0:T(8,128)(2,1)S(1)} %copy-done.2), kind=kOutput, calls=%fused_computation.9 | convolution fusion | flops 587202560 | bytes 3375104 | tf_op jit(solution)/shard_map/dot_general | solution.py:68
  173.8 42.9 %all-gather.5.cloned.1.call-done = bf16[1024,640]{1,0:T(8,128)(2,1)} async-done(((bf16[64,640]{1,0:T(8,128)(2,1)}), bf16[1024,640]{1,0:T(8,128)(2,1)}) %all-gather.5.cloned.1.call-update) | async-done | bytes 1310736 | tf_op jit(solution)/shard_map/all_gather | solution.py:75
  216.7 2.5 fusion.2
  219.6 1.3 all_to_all.23
  220.8 14.2 %all-to-all-start.1 = ((bf16[448,64,10]{0,2,1:T(8,128)(2,1)}), bf16[448,64,10]{0,2,1:T(8,128)(2,1)S(1)}, u32[]{:S(2)}, u32[]{:S(2)}) async-start(bf16[448,64,10]{0,2,1:T(8,128)(2,1)} %all_to_all.23), calls=%async_computation.1 | async-start | bytes 2097152 | tf_op jit(solution)/shard_map/all_to_all | solution.py:79
  235.3 0.6 select_reduce_fusion
  235.9 29.1 %all-to-all-done.1 = bf16[448,64,10]{0,2,1:T(8,128)(2,1)S(1)} async-done(((bf16[448,64,10]{0,2,1:T(8,128)(2,1)}), bf16[448,64,10]{0,2,1:T(8,128)(2,1)S(1)}, u32[]{:S(2)}, u32[]{:S(2)}) %all-to-all-start.1) | async-done | bytes 573472 | tf_op jit(solution)/shard_map/all_to_all | solution.py:79
  265.1 0.3 convert_reduce_fusion
  265.4 2.0 convolution_convert_fusion.2
  (23 shorter events, 1.1 us)
Async XLA Ops:
  7.2 57.3 %copy-start = (bf16[1,1024,448]{1,2,0:T(8,128)(2,1)S(1)}, bf16[1,1024,448]{1,2,0:T(8,128)(2,1)}, u32[]{:S(2)}) copy-start(bf16[1,1024,448]{1,2,0:T(8,128)(2,1)} %param.15) | copy-start | bytes 2752516
  7.2 113.6 %reduce-scatter.4.cloned.1.call-start = ((), (), s32[]{:S(2)}) async-start(), calls=%async_computation.6 | async-start | bytes 1392640 | tf_op jit(solution)/shard_map/reduce_scatter | solution.py:54
  66.8 103.8 %copy-start.2 = (bf16[1,448,1024]{2,1,0:T(8,128)(2,1)S(1)}, bf16[1,448,1024]{2,1,0:T(8,128)(2,1)}, u32[]{:S(2)}) copy-start(bf16[1,448,1024]{2,1,0:T(8,128)(2,1)} %param.13) | copy-start | bytes 2752516
  66.8 103.8 %all-gather.3.cloned.1.call-start = ((), (), s32[]{:S(2)}) async-start(), calls=%async_computation.4 | async-start | bytes 1392640 | tf_op jit(solution)/shard_map/all_gather | solution.py:70
  122.6 94.2 %all-gather.5.cloned.1.call-start = ((), (), s32[]{:S(2)}) async-start(), calls=%async_computation.5 | async-start | bytes 1392640 | tf_op jit(solution)/shard_map/all_gather | solution.py:75
  149.3 71.5 %all-to-all-start.2 = ((bf16[1,64,10]{2,0,1:T(2,128)(2,1)}), bf16[1,64,10]{2,0,1:T(2,128)(2,1)S(1)}, u32[]{:S(2)}, u32[]{:S(2)}) async-start(bf16[1,64,10]{2,0,1:T(2,128)(2,1)} %all_to_all.27), calls=%async_computation.2 | async-start | bytes 65536 | tf_op jit(solution)/shard_map/all_to_all | solution.py:82
  163.2 53.5 %copy-start.3 = (bf16[1,448,1024]{2,1,0:T(8,128)(2,1)S(1)}, bf16[1,448,1024]{2,1,0:T(8,128)(2,1)}, u32[]{:S(2)}) copy-start(bf16[1,448,1024]{2,1,0:T(8,128)(2,1)} %param.14) | copy-start | bytes 2752516
  220.8 14.5 %copy-start.1 = (f32[128,2]{0,1:T(2,128)S(1)}, f32[128,2]{0,1:T(2,128)}, u32[]{:S(2)}) copy-start(f32[128,2]{0,1:T(2,128)} %param.10) | copy-start | bytes 3076
  220.8 44.2 %all-to-all-start.1 = ((bf16[448,64,10]{0,2,1:T(8,128)(2,1)}), bf16[448,64,10]{0,2,1:T(8,128)(2,1)S(1)}, u32[]{:S(2)}, u32[]{:S(2)}) async-start(bf16[448,64,10]{0,2,1:T(8,128)(2,1)} %all_to_all.23), calls=%async_computation.1 | async-start | bytes 2097152 | tf_op jit(solution)/shard_map/all_to_all | solution.py:79
Sparse Core Ops, SparseCore 0:
  66.9 53.8 reduce-scatter.3
  124.1 46.4 all-gather.2
  173.3 43.4 all-gather.4
where the time goes:
time: 274 us
  waiting for transfers between devices  134 us (49%)
  blocking collectives  78.3 us (29%)
  starting transfers between devices  28.2 us (10%)
  between operations  13.9 us (5%)
  matrix products  9.95 us (4%)
  other arithmetic  4.98 us (2%)
  local copies, waits for them, and re-layouts  4.63 us (2%)
    reduce_scatter x1, waiting for transfers between devices, shards(): lax.psum_scatter(lax.dot_general(down_local, arrived, (((1,), (1,)), ((),...  53.9 us
    all_to_all x1, blocking collectives, shards(): lax.all_to_all(outgoing, 'node', split_axis=0, concat_axis=0, tiled=True)  53 us
    all_gather x1, waiting for transfers between devices, shards(): lax.all_gather(grad_upper, 'local', axis=0, tiled=True)  42.9 us
    all_to_all x1, waiting for transfers between devices, shards(): lax.all_to_all(route_grad.astype(jnp.bfloat16), 'node', split_axis=1, con...  29.1 us
    psum x1, blocking collectives, shards(): prob_grad = lax.psum(prob_part, 'local')  25.3 us
    all_to_all x1, starting transfers between devices, shards(): lax.all_to_all(route_grad.astype(jnp.bfloat16), 'node', split_axis=1, con...  14.2 us
    all_to_all x1, starting transfers between devices, shards(): lax.all_to_all(prob_grad.astype(jnp.bfloat16)[None, :], 'node', split_axi...  13.9 us
    all_gather x1, waiting for transfers between devices, shards(): lax.all_gather(grad_gate, 'local', axis=0, tiled=True)  7.34 us
  transfers between devices with their start and end apart: 5, of which 4 were waited for; matrix products, arithmetic and copies ran while one was open for 3% of the time, Pallas kernels for 0%

commit v1 on v0

v1 whole, which is shorter than its diff:
```python
import jax
import jax.numpy as jnp
from jax import lax
from jax.sharding import Mesh
from jax.sharding import PartitionSpec as P

FULL_PRECISION = lax.Precision.HIGHEST
NODE = ("z", "y")


def slot_table(routes, experts, capacity):
    tokens = routes.shape[0]
    labels = jnp.arange(experts, dtype=jnp.int32)
    named = routes[:, :, None] == labels[None, None, :]
    onehot = jnp.sum(named.astype(jnp.float32), axis=1)
    positions = jnp.arange(tokens, dtype=jnp.int32)
    earlier_mask = (positions[:, None] > positions[None, :]).astype(jnp.float32)
    before = jnp.dot(earlier_mask, onehot, precision=FULL_PRECISION)
    picked = jnp.sum(jnp.where(named, before[:, None, :], 0.0), axis=2)
    slot_index = routes * capacity + picked.astype(jnp.int32)
    places = jnp.arange(experts * capacity, dtype=jnp.int32)
    return slot_index[None, :, :] == places[:, None, None]


def unit_grads(grad_units, gate_saved, up_saved):
    gate_value = gate_saved.astype(jnp.float32)
    up_value = up_saved.astype(jnp.float32)
    sigmoid_gate = jax.nn.sigmoid(gate_value)
    activation = gate_value * sigmoid_gate
    prob_part = jnp.sum(activation * up_value * grad_units, axis=0)
    grad_gate = (
        grad_units * up_value * sigmoid_gate * (1.0 + gate_value * (1.0 - sigmoid_gate))
    ).astype(jnp.bfloat16)
    grad_upper = (grad_units * activation).astype(jnp.bfloat16)
    return (grad_gate, grad_upper, prob_part)


def shards(grad_out, route_expert, gate_prob, saved_gate, saved_up, w_gate, w_up, w_down):
    groups = lax.axis_size(NODE)
    experts = groups // 2
    slots_all = saved_gate.shape[2]
    capacity = slots_all // groups
    feat_width = grad_out.shape[1]
    block_rows = capacity * feat_width // 128
    slot_match = slot_table(route_expert, experts, capacity)
    dispatch_mask = jnp.any(slot_match, axis=2).astype(jnp.bfloat16)
    outgoing = jnp.dot(dispatch_mask, grad_out, preferred_element_type=jnp.float32).astype(
        jnp.bfloat16
    )
    outgoing = jnp.repeat(outgoing.reshape(experts, block_rows, 128), 2, axis=0)
    arrived = lax.all_to_all(outgoing, NODE, split_axis=0, concat_axis=0, tiled=True)
    arrived = arrived.reshape(slots_all, feat_width)
    partial = lax.dot_general(
        w_down[0], arrived, (((1,), (1,)), ((), ())), preferred_element_type=jnp.float32
    ).astype(jnp.bfloat16)
    halves = lax.psum_scatter(partial, "c", scatter_dimension=0, tiled=True)
    halves = lax.psum(halves, "x")
    grad_units = lax.all_gather(halves, "c", axis=0, tiled=True).astype(jnp.float32)
    grad_gate, grad_upper, prob_grad = unit_grads(grad_units, saved_gate[0], saved_up[0])
    route_grad = jnp.dot(w_gate[0], grad_gate, preferred_element_type=jnp.float32) + jnp.dot(
        w_up[0], grad_upper, preferred_element_type=jnp.float32
    )
    packed = route_grad.astype(jnp.bfloat16).T.reshape(groups, block_rows, 128)
    probs = jnp.pad(
        prob_grad.astype(jnp.bfloat16).reshape(groups, 1, capacity),
        ((0, 0), (0, 0), (0, 128 - capacity)),
    )
    returned = lax.all_to_all(
        jnp.concatenate([packed, probs], axis=1), NODE, split_axis=0, concat_axis=0, tiled=True
    )
    rows = returned[:, :block_rows].reshape(experts, 2, capacity, feat_width)
    summed_rows = jnp.sum(rows.astype(jnp.float32), axis=1).reshape(
        experts * capacity, feat_width
    )
    prob_rows = returned[:, block_rows, :capacity].reshape(experts, 2, capacity)
    summed_probs = jnp.sum(prob_rows.astype(jnp.float32), axis=1).reshape(experts * capacity)
    weights = jnp.sum(jnp.where(slot_match, gate_prob[None, :, :], 0.0), axis=2)
    grad_in = lax.dot_general(
        weights, summed_rows, (((0,), (0,)), ((), ())), precision=FULL_PRECISION
    )
    grad_prob = jnp.sum(jnp.where(slot_match, summed_probs[:, None, None], 0.0), axis=0)
    return (grad_in.astype(jnp.bfloat16), grad_prob.astype(jnp.bfloat16))


def solution(mesh):
    nodes, local = mesh.devices.shape
    rows = 8
    fine = Mesh(
        mesh.devices.reshape(nodes // rows, rows, local // 2, 2), ("z", "y", "x", "c")
    )
    node, feats = NODE, ("x", "c")
    return jax.shard_map(
        shards,
        mesh=fine,
        in_specs=(
            P(node, feats),
            P(node, None),
            P(node, None),
            P(node, None, None),
            P(node, None, None),
            P(node, feats, None),
            P(node, feats, None),
            P(node, None, feats),
        ),
        out_specs=(P(node, feats), P(node, None)),
        check_vma=False,
    )
```

time: 274 us -> 245 us (0.89)
  the two profiles are of different devices: /device:TPU:6 before, /device:TPU:16 now
where the time goes in v1:
time: 245 us
  waiting for transfers between devices  123 us (50%)
  blocking collectives  80.9 us (33%)
  between operations  13.9 us (6%)
  matrix products  9.76 us (4%)
  local copies, waits for them, and re-layouts  8.84 us (4%)
  other arithmetic  7.93 us (3%)
    psum x1, waiting for transfers between devices, shards(): halves = lax.psum(halves, 'x')  89.5 us
    all_to_all x1, blocking collectives, shards(): lax.all_to_all(outgoing, NODE, split_axis=0, concat_axis=0, tiled=True)  44.9 us
    all_to_all x1, blocking collectives, shards(): lax.all_to_all(jnp.concatenate([packed, probs], axis=1), NODE, split_axis...  36 us
    all_gather x1, waiting for transfers between devices, shards(): lax.all_gather(halves, 'c', axis=0, tiled=True).astype(jnp.float32)  20.3 us
    reduce_scatter x1, waiting for transfers between devices, shards(): halves = lax.psum_scatter(partial, 'c', scatter_dimension=0, tiled=True)  13.3 us
  transfers between devices with their start and end apart: 3, of which 3 were waited for; matrix products, arithmetic and copies ran while one was open for 1% of the time, Pallas kernels for 0%

profile of v1, /device:TPU:16, one launch (start us, length us, event | category | flops | bytes accessed | tf_op | source)
XLA Modules:
  0.0 244.6 jit_solution(906316386486284896)
XLA Ops:
  7.2 0.8 convert_reduce_fusion
  8.1 0.8 select_reduce_fusion.2
  8.9 0.7 convert_add_fusion
  9.6 1.1 convolution_convert_fusion.1
  11.3 44.9 %all_to_all.10 = bf16[64,35,128]{2,1,0:T(8,128)(2,1)S(1)} all-to-all(bf16[64,35,128]{2,1,0:T(8,128)(2,1)S(1)} %bitcast.34), channel_id=1, replica_groups=mesh['z'=8,'y'=8,'x'=8,'c'=2] {'z','y'}, dimensions={0} | all-to-all | bytes 1146880 | tf_op jit(solution)/shard_map/all_to_all | solution.py:51
  56.2 0.6 reshape.47
  56.8 1.9 fusion.9
  58.8 13.3 %reduce-scatter.2.cloned.1.call-done = bf16[512,640]{0,1:T(8,128)(2,1)} async-done(((bf16[1024,640]{0,1:T(8,128)(2,1)}), bf16[512,640]{0,1:T(8,128)(2,1)}) %reduce-scatter.2.cloned.1.call-update) | async-done | bytes 655376 | tf_op jit(solution)/shard_map/reduce_scatter | solution.py:56
  72.1 89.5 %all-reduce.3.cloned.1.call-done = bf16[512,640]{0,1:T(8,128)(2,1)} async-done(((bf16[512,640]{0,1:T(8,128)(2,1)}), bf16[512,640]{0,1:T(8,128)(2,1)}) %all-reduce.3.cloned.1.call-update) | async-done | bytes 655376 | tf_op jit(solution)/shard_map/psum | solution.py:57
  161.7 0.7 copy.25
  162.4 1.6 copy.24
  164.0 20.3 %all-gather.2.cloned.1.call-done = bf16[1024,640]{0,1:T(8,128)(2,1)} async-done(((bf16[512,640]{0,1:T(8,128)(2,1)}), bf16[1024,640]{0,1:T(8,128)(2,1)}) %all-gather.2.cloned.1.call-update) | async-done | bytes 1310736 | tf_op jit(solution)/shard_map/all_gather | solution.py:58
  184.3 2.3 fusion.4
  186.6 0.8 convert_element_type.104
  187.4 3.3 %fusion.13 = f32[640,448]{0,1:T(8,128)S(1)} fusion(bf16[1024,640]{0,1:T(8,128)(2,1)} %all-gather.2.cloned.1.call-done, bf16[1,1024,640]{1,2,0:T(8,128)(2,1)S(1)} %copy.24, bf16[1,1024,640]{1,2,0:T(8,128)(2,1)S(1)} %copy.25, bf16[1,448,1024]{2,1,0:T(8,128)(2,1)} %param.13), kind=kOutput, calls=%fused_computation.22 | convolution fusion | flops 595722240 | bytes 5996544 | tf_op jit(solution)/shard_map/dot_general | solution.py:60
  190.7 1.2 fusion.10
  192.3 0.9 reshape.48
  193.3 36.0 %all_to_all.11 = bf16[64,36,128]{2,1,0:T(8,128)(2,1)S(1)} all-to-all(bf16[64,36,128]{2,1,0:T(8,128)(2,1)S(1)} %fusion.18), channel_id=1, replica_groups=mesh['z'=8,'y'=8,'x'=8,'c'=2] {'z','y'}, dimensions={0} | all-to-all | bytes 1179648 | tf_op jit(solution)/shard_map/all_to_all | solution.py:68
  229.6 1.2 slice_convert_fusion
  230.7 2.0 reshape.52
  232.7 1.4 reduce_sum.67
  234.1 1.3 reshape.49
  235.4 0.6 select_reduce_fusion
  236.1 2.0 convolution_convert_fusion.2
  (27 shorter events, 1.5 us)
Async XLA Ops:
  7.2 49.7 %copy-start = (bf16[1,1024,448]{1,2,0:T(8,128)(2,1)S(1)}, bf16[1,1024,448]{1,2,0:T(8,128)(2,1)}, u32[]{:S(2)}) copy-start(bf16[1,1024,448]{1,2,0:T(8,128)(2,1)} %param.15) | copy-start | bytes 2752516
  7.2 64.9 %reduce-scatter.2.cloned.1.call-start = ((), (), s32[]{:S(2)}) async-start(), calls=%async_computation.3 | async-start | bytes 1966080 | tf_op jit(solution)/shard_map/reduce_scatter | solution.py:56
  58.7 103.0 %copy-start.2 = (bf16[1,1024,640]{2,1,0:T(8,128)(2,1)S(1)}, bf16[1,1024,640]{2,1,0:T(8,128)(2,1)}, u32[]{:S(2)}) copy-start(bf16[1,1024,640]{2,1,0:T(8,128)(2,1)} %param.11) | copy-start | bytes 3932164
  58.8 102.9 %all-reduce.3.cloned.1.call-start = ((), (), s32[]{:S(2)}) async-start(), calls=%async_computation.4 | async-start | bytes 1310720 | tf_op jit(solution)/shard_map/psum | solution.py:57
  72.1 112.2 %all-gather.2.cloned.1.call-start = ((), (), s32[]{:S(2)}) async-start(), calls=%async_computation.5 | async-start | bytes 1966080 | tf_op jit(solution)/shard_map/all_gather | solution.py:58
  187.4 3.3 %copy-start.1 = (bf16[1024,640]{0,1:T(8,128)(2,1)S(1)}, bf16[1024,640]{0,1:T(8,128)(2,1)}, u32[]{:S(2)}) copy-start(bf16[1024,640]{0,1:T(8,128)(2,1)} %all-gather.2.cloned.1.call-done) | copy-start | bytes 3932164
  187.4 3.4 %copy-start.5 = (bf16[1,448,1024]{2,1,0:T(8,128)(2,1)S(1)}, bf16[1,448,1024]{2,1,0:T(8,128)(2,1)}, u32[]{:S(2)}) copy-start(bf16[1,448,1024]{2,1,0:T(8,128)(2,1)} %param.14) | copy-start | bytes 2752516
  192.0 1.2 copy-start.3
  232.7 2.7 %copy-start.4 = (f32[128,2]{0,1:T(2,128)S(1)}, f32[128,2]{0,1:T(2,128)}, u32[]{:S(2)}) copy-start(f32[128,2]{0,1:T(2,128)} %param.10) | copy-start | bytes 3076
Sparse Core Ops, SparseCore 0:
  58.9 13.1 reduce-scatter.1
  74.5 87.0 all-reduce.2
  164.7 19.5 all-gather.1

commit v2 on v1

v2 whole, which is shorter than its diff:
```python
import jax
import jax.numpy as jnp
from jax import lax
from jax.sharding import Mesh
from jax.sharding import PartitionSpec as P

FULL_PRECISION = lax.Precision.HIGHEST
PAIR = ("z", "yh")


def slot_table(routes, experts, capacity):
    tokens = routes.shape[0]
    labels = jnp.arange(experts, dtype=jnp.int32)
    named = routes[:, :, None] == labels[None, None, :]
    onehot = jnp.sum(named.astype(jnp.float32), axis=1)
    positions = jnp.arange(tokens, dtype=jnp.int32)
    earlier_mask = (positions[:, None] > positions[None, :]).astype(jnp.float32)
    before = jnp.dot(earlier_mask, onehot, precision=FULL_PRECISION)
    picked = jnp.sum(jnp.where(named, before[:, None, :], 0.0), axis=2)
    slot_index = routes * capacity + picked.astype(jnp.int32)
    places = jnp.arange(experts * capacity, dtype=jnp.int32)
    return slot_index[None, :, :] == places[:, None, None]


def unit_grads(grad_units, gate_saved, up_saved):
    gate_value = gate_saved.astype(jnp.float32)
    up_value = up_saved.astype(jnp.float32)
    sigmoid_gate = jax.nn.sigmoid(gate_value)
    activation = gate_value * sigmoid_gate
    prob_part = jnp.sum(activation * up_value * grad_units, axis=0)
    grad_gate = (
        grad_units * up_value * sigmoid_gate * (1.0 + gate_value * (1.0 - sigmoid_gate))
    ).astype(jnp.bfloat16)
    grad_upper = (grad_units * activation).astype(jnp.bfloat16)
    return (grad_gate, grad_upper, prob_part)


def swap(value, axis):
    return lax.ppermute(value, axis, ((0, 1), (1, 0)))


def shards(grad_out, route_expert, gate_prob, saved_gate, saved_up, w_gate, w_up, w_down):
    experts = lax.axis_size(PAIR)
    slots_all = saved_gate.shape[2]
    hidden = saved_gate.shape[1]
    capacity = slots_all // (2 * experts)
    feat_width = grad_out.shape[1]
    block_rows = capacity * feat_width // 128
    chips = lax.axis_size("x")
    core = lax.axis_index("c")
    side = lax.axis_index("yl")
    slot_match = slot_table(route_expert, experts, capacity)
    dispatch_mask = jnp.any(slot_match, axis=2).astype(jnp.bfloat16)
    outgoing = jnp.dot(dispatch_mask, grad_out, preferred_element_type=jnp.float32).astype(
        jnp.bfloat16
    )
    outgoing = outgoing.reshape(experts, block_rows, 128)
    own_rows = lax.all_to_all(outgoing, PAIR, split_axis=0, concat_axis=0, tiled=True)
    pair_rows = swap(own_rows, "yl")
    first = jnp.where(side == 0, own_rows, pair_rows)
    second = jnp.where(side == 0, pair_rows, own_rows)
    arrived = jnp.stack([first, second], axis=1).reshape(slots_all, feat_width)
    partial = lax.dot_general(
        w_down[0], arrived, (((1,), (1,)), ((), ())), preferred_element_type=jnp.float32
    ).astype(jnp.bfloat16)
    half = hidden // 2
    kept = lax.dynamic_slice_in_dim(partial, core * half, half, 0)
    other = swap(lax.dynamic_slice_in_dim(partial, (1 - core) * half, half, 0), "c")
    on_chip = (kept.astype(jnp.float32) + other.astype(jnp.float32)).astype(jnp.bfloat16)
    pieces = lax.all_to_all(
        on_chip.reshape(chips, half // chips, slots_all), "x", split_axis=0, concat_axis=0, tiled=True
    )
    summed = jnp.sum(pieces.astype(jnp.float32), axis=0).astype(jnp.bfloat16)
    spread = lax.all_to_all(
        jnp.broadcast_to(summed[None], pieces.shape), "x", split_axis=0, concat_axis=0, tiled=True
    ).reshape(half, slots_all)
    partner = swap(spread, "c")
    grad_units = jnp.concatenate(
        [jnp.where(core == 0, spread, partner), jnp.where(core == 0, partner, spread)], axis=0
    ).astype(jnp.float32)
    grad_gate, grad_upper, prob_grad = unit_grads(grad_units, saved_gate[0], saved_up[0])
    route_grad = jnp.dot(w_gate[0], grad_gate, preferred_element_type=jnp.float32) + jnp.dot(
        w_up[0], grad_upper, preferred_element_type=jnp.float32
    )
    packed = route_grad.astype(jnp.bfloat16).T.reshape(experts, 2, block_rows, 128)
    probs = jnp.pad(
        prob_grad.astype(jnp.bfloat16).reshape(experts, 2, 1, capacity),
        ((0, 0), (0, 0), (0, 0), (0, 128 - capacity)),
    )
    packed = jnp.concatenate([packed, probs], axis=2)
    kept_back = jnp.where(side == 0, packed[:, 0], packed[:, 1])
    pair_back = swap(jnp.where(side == 0, packed[:, 1], packed[:, 0]), "yl")
    both = (kept_back.astype(jnp.float32) + pair_back.astype(jnp.float32)).astype(jnp.bfloat16)
    returned = lax.all_to_all(both, PAIR, split_axis=0, concat_axis=0, tiled=True)
    summed_rows = returned[:, :block_rows].reshape(experts * capacity, feat_width)
    summed_probs = returned[:, block_rows, :capacity].reshape(experts * capacity)
    weights = jnp.sum(jnp.where(slot_match, gate_prob[None, :, :], 0.0), axis=2)
    grad_in = lax.dot_general(
        weights,
        summed_rows.astype(jnp.float32),
        (((0,), (0,)), ((), ())),
        precision=FULL_PRECISION,
    )
    grad_prob = jnp.sum(
        jnp.where(slot_match, summed_probs.astype(jnp.float32)[:, None, None], 0.0), axis=0
    )
    return (grad_in.astype(jnp.bfloat16), grad_prob.astype(jnp.bfloat16))


def solution(mesh):
    nodes, local = mesh.devices.shape
    rows = 8
    fine = Mesh(
        mesh.devices.reshape(nodes // rows, rows // 2, 2, local // 2, 2),
        ("z", "yh", "yl", "x", "c"),
    )
    node, feats = ("z", "yh", "yl"), ("x", "c")
    return jax.shard_map(
        shards,
        mesh=fine,
        in_specs=(
            P(node, feats),
            P(node, None),
            P(node, None),
            P(node, None, None),
            P(node, None, None),
            P(node, feats, None),
            P(node, feats, None),
            P(node, None, feats),
        ),
        out_specs=(P(node, feats), P(node, None)),
        check_vma=False,
    )
```

time: 245 us -> 153 us (0.62)
  waiting for transfers between devices: 123 us -> 17.7 us
  blocking collectives: 80.9 us -> 108 us
  between operations: 13.9 us -> 0.92 us
  starting transfers between devices: 0.12 us -> 10.8 us
  local copies, waits for them, and re-layouts: 8.84 us -> 3.53 us
  matrix products: 9.76 us -> 6.17 us
  other arithmetic: 7.93 us -> 4.8 us
    psum x1 -> x0, waiting for transfers between devices: 89.5 us -> none  [shards(): halves = lax.psum(halves, 'x')]
    all_to_all x2 -> x4, blocking collectives: 80.9 us -> 108 us  [the longest x1 36.7 us: shards(): lax.all_to_all(outgoing, PAIR, split_axis=0, concat_axis=0, tiled=True)]
    all_gather x1 -> x0, waiting for transfers between devices: 20.3 us -> none  [shards(): lax.all_gather(halves, 'c', axis=0, tiled=True).astype(jnp.float32)]
    ppermute x0 -> x4, waiting for transfers between devices: none -> 17.7 us  [swap(): return lax.ppermute(value, axis, ((0, 1), (1, 0)))]
    reduce_scatter x1 -> x0, waiting for transfers between devices: 13.3 us -> none  [shards(): halves = lax.psum_scatter(partial, 'c', scatter_dimension=0, tiled=True)]
    ppermute x0 -> x4, starting transfers between devices: none -> 10.8 us  [swap(): return lax.ppermute(value, axis, ((0, 1), (1, 0)))]
  transfers between devices with their start and end apart: 3 -> 4, of which waited for: 3 -> 4; matrix products, arithmetic and copies ran while one was open for 1% -> 0% of each run, Pallas kernels for 0% -> 0%
where the time goes in v2:
time: 153 us; the launch traced here: 152 us
  blocking collectives  108 us (71%)
  waiting for transfers between devices  17.7 us (12%)
  starting transfers between devices  10.8 us (7%)
  matrix products  6.17 us (4%)
  other arithmetic  4.8 us (3%)
  local copies, waits for them, and re-layouts  3.53 us (2%)
    all_to_all x1, blocking collectives, shards(): lax.all_to_all(outgoing, PAIR, split_axis=0, concat_axis=0, tiled=True)  36.7 us
    all_to_all x1, blocking collectives, shards(): lax.all_to_all(on_chip.reshape(chips, half // chips, slots_all), 'x', spl...  27.2 us
    all_to_all x1, blocking collectives, shards(): lax.all_to_all(both, PAIR, split_axis=0, concat_axis=0, tiled=True)  22.4 us
    all_to_all x1, blocking collectives, shards(): lax.all_to_all(jnp.broadcast_to(summed[None], pieces.shape), 'x', split_a...  21.9 us
    ppermute x4, waiting for transfers between devices, swap(): return lax.ppermute(value, axis, ((0, 1), (1, 0)))  17.7 us
    ppermute x4, starting transfers between devices, swap(): return lax.ppermute(value, axis, ((0, 1), (1, 0)))  10.8 us
  transfers between devices with their start and end apart: 4, of which 4 were waited for; matrix products, arithmetic and copies ran while one was open for 0% of the time, Pallas kernels for 0%

profile of v2, /device:TPU:16, one launch (start us, length us, event | category | flops | bytes accessed | tf_op | source)
XLA Modules:
  0.0 152.2 jit_solution(5880228303577411567)
XLA Ops:
  0.6 0.8 convert_reduce_fusion
  1.5 0.8 select_reduce_fusion.2
  2.3 0.7 convert_add_fusion.1
  3.0 1.1 convolution_convert_fusion.1
  4.7 36.7 %all_to_all.20 = bf16[32,35,128]{2,1,0:T(8,128)(2,1)S(1)} all-to-all(bf16[32,35,128]{2,1,0:T(8,128)(2,1)S(1)} %reshape.89), channel_id=1, replica_groups=mesh['z'=8,'yh'=4,'yl'=2,'x'=8,'c'=2] {'z','yh'}, dimensions={0} | all-to-all | bytes 573440 | tf_op jit(solution)/shard_map/all_to_all | solution.py:58
  41.4 3.5 %collective-permute-start = (bf16[32,35,128]{2,1,0:T(8,128)(2,1)S(1)}, bf16[32,35,128]{2,1,0:T(8,128)(2,1)S(1)}, u32[]{:S(2)}, u32[]{:S(2)}) collective-permute-start(bf16[32,35,128]{2,1,0:T(8,128)(2,1)S(1)} %all_to_all.20), channel_id=1, source_target_pairs={{0,16},{16,0},{1,17},{17,1},{2,18},{18,2},{3,19},{19,3},{4,20},{20... | collective-permute-start | bytes 860168 | tf_op jit(solution)/shard_map/ppermute | solution.py:39
  44.9 5.5 %collective-permute-done = bf16[32,35,128]{2,1,0:T(8,128)(2,1)S(1)} collective-permute-done((bf16[32,35,128]{2,1,0:T(8,128)(2,1)S(1)}, bf16[32,35,128]{2,1,0:T(8,128)(2,1)S(1)}, u32[]{:S(2)}, u32[]{:S(2)}) %collective-permute-start) | collective-permute-done | bytes 286752 | tf_op jit(solution)/shard_map/ppermute | solution.py:39
  50.5 0.6 reshape.90
  51.2 0.8 convolution_convert_fusion
  52.1 1.9 %collective-permute-start.1 = (bf16[512,640]{0,1:T(8,128)(2,1)S(1)}, bf16[512,640]{0,1:T(8,128)(2,1)S(1)}, u32[]{:S(2)}, u32[]{:S(2)}) collective-permute-start(bf16[512,640]{0,1:T(8,128)(2,1)S(1)} %dynamic-slice_bitcast_fusion), channel_id=1, source_target_pairs={{0,1},{1,0},{2,3},{3,2},{4,5},{5,4},{6,7},{7,6},{8,9},{9,8},{10,11... | collective-permute-start | bytes 1966088 | tf_op jit(solution)/shard_map/ppermute | solution.py:39
  54.0 2.1 %collective-permute-done.1 = bf16[512,640]{0,1:T(8,128)(2,1)S(1)} collective-permute-done((bf16[512,640]{0,1:T(8,128)(2,1)S(1)}, bf16[512,640]{0,1:T(8,128)(2,1)S(1)}, u32[]{:S(2)}, u32[]{:S(2)}) %collective-permute-start.1) | collective-permute-done | bytes 655392 | tf_op jit(solution)/shard_map/ppermute | solution.py:39
  56.6 27.2 %all_to_all.21 = bf16[8,64,640]{2,1,0:T(8,128)(2,1)S(1)} all-to-all(bf16[8,64,640]{2,1,0:T(8,128)(2,1)S(1)} %bitcast.87), channel_id=1, replica_groups=mesh['z'=8,'yh'=4,'yl'=2,'x'=8,'c'=2] {'x'}, dimensions={0} | all-to-all | bytes 1310720 | tf_op jit(solution)/shard_map/all_to_all | solution.py:70
  83.9 21.9 %all_to_all.22 = bf16[8,64,640]{2,1,0:T(8,128)(2,1)S(1)} all-to-all(bf16[8,64,640]{2,1,0:T(8,128)(2,1)S(1)} %broadcast_in_dim.53), channel_id=1, replica_groups=mesh['z'=8,'yh'=4,'yl'=2,'x'=8,'c'=2] {'x'}, dimensions={0} | all-to-all | bytes 1310720 | tf_op jit(solution)/shard_map/all_to_all | solution.py:74
  105.9 1.9 %collective-permute-start.2 = (bf16[512,640]{1,0:T(8,128)(2,1)S(1)}, bf16[512,640]{1,0:T(8,128)(2,1)S(1)}, u32[]{:S(2)}, u32[]{:S(2)}) collective-permute-start(bf16[512,640]{1,0:T(8,128)(2,1)S(1)} %bitcast.88), channel_id=1, source_target_pairs={{0,1},{1,0},{2,3},{3,2},{4,5},{5,4},{6,7},{7,6},{8,9},{9,8},{10,11... | collective-permute-start | bytes 1966088 | tf_op jit(solution)/shard_map/ppermute | solution.py:39
  107.8 2.0 %collective-permute-done.2 = bf16[512,640]{1,0:T(8,128)(2,1)S(1)} collective-permute-done((bf16[512,640]{1,0:T(8,128)(2,1)S(1)}, bf16[512,640]{1,0:T(8,128)(2,1)S(1)}, u32[]{:S(2)}, u32[]{:S(2)}) %collective-permute-start.2) | collective-permute-done | bytes 655392 | tf_op jit(solution)/shard_map/ppermute | solution.py:39
  110.1 1.0 fusion.8
  111.2 1.6 %fusion.18 = f32[640,448]{0,1:T(8,128)S(1)} fusion(bf16[1,1024,640]{2,1,0:T(8,128)(2,1)S(1)} %copy-done.1, bf16[1,1024,640]{2,1,0:T(8,128)(2,1)S(1)} %copy-done.2, bf16[1,448,1024]{2,1,0:T(8,128)(2,1)S(1)} %copy-done.4, bf16[1,512,640]{2,1,0:T(8,128)(2,1)S(1)} %bitcast.85, bf16[1,512,640]{2,1,0:T(8,128)(2,1)S(1)} %bitcast.83), kind=kOutput, calls=%fused_computation.29 | convolution fusion | flops 597688320 | bytes 5996544 | tf_op jit(solution)/shard_map/dot_general | solution.py:82
  112.9 1.2 fusion.16
  114.4 0.9 reshape.93
  115.6 3.5 %collective-permute-start.3 = (bf16[32,36,128]{2,1,0:T(8,128)(2,1)S(1)}, bf16[32,36,128]{2,1,0:T(8,128)(2,1)S(1)}, u32[]{:S(2)}, u32[]{:S(2)}) collective-permute-start(bf16[32,36,128]{2,1,0:T(8,128)(2,1)S(1)} %fusion.29), channel_id=1, source_target_pairs={{0,16},{16,0},{1,17},{17,1},{2,18},{18,2},{3,19},{19,3},{4,20},{20... | collective-permute-start | bytes 884744 | tf_op jit(solution)/shard_map/ppermute | solution.py:39
  119.1 8.1 %collective-permute-done.3 = bf16[32,36,128]{2,1,0:T(8,128)(2,1)S(1)} collective-permute-done((bf16[32,36,128]{2,1,0:T(8,128)(2,1)S(1)}, bf16[32,36,128]{2,1,0:T(8,128)(2,1)S(1)}, u32[]{:S(2)}, u32[]{:S(2)}) %collective-permute-start.3) | collective-permute-done | bytes 294944 | tf_op jit(solution)/shard_map/ppermute | solution.py:39
  127.4 22.4 %all_to_all.23 = bf16[32,36,128]{2,1,0:T(8,128)(2,1)S(1)} all-to-all(bf16[32,36,128]{2,1,0:T(8,128)(2,1)S(1)} %fusion.28), channel_id=1, replica_groups=mesh['z'=8,'yh'=4,'yl'=2,'x'=8,'c'=2] {'z','yh'}, dimensions={0} | all-to-all | bytes 589824 | tf_op jit(solution)/shard_map/all_to_all | solution.py:94
  150.3 0.6 select_reduce_fusion
  151.0 1.2 convolution_convert_fusion.2
  (32 shorter events, 3.1 us)
Async XLA Ops:
  0.6 50.5 %copy-start = (bf16[1,1024,448]{1,2,0:T(8,128)(2,1)S(1)}, bf16[1,1024,448]{1,2,0:T(8,128)(2,1)}, u32[]{:S(2)}) copy-start(bf16[1,1024,448]{1,2,0:T(8,128)(2,1)} %param.15) | copy-start | bytes 2752516
  41.4 9.0 %collective-permute-start = (bf16[32,35,128]{2,1,0:T(8,128)(2,1)S(1)}, bf16[32,35,128]{2,1,0:T(8,128)(2,1)S(1)}, u32[]{:S(2)}, u32[]{:S(2)}) collective-permute-start(bf16[32,35,128]{2,1,0:T(8,128)(2,1)S(1)} %all_to_all.20), channel_id=1, source_target_pairs={{0,16},{16,0},{1,17},{17,1},{2,18},{18,2},{3,19},{19,3},{4,20},{20... | collective-permute-start | bytes 860168 | tf_op jit(solution)/shard_map/ppermute | solution.py:39
  52.1 4.0 %collective-permute-start.1 = (bf16[512,640]{0,1:T(8,128)(2,1)S(1)}, bf16[512,640]{0,1:T(8,128)(2,1)S(1)}, u32[]{:S(2)}, u32[]{:S(2)}) collective-permute-start(bf16[512,640]{0,1:T(8,128)(2,1)S(1)} %dynamic-slice_bitcast_fusion), channel_id=1, source_target_pairs={{0,1},{1,0},{2,3},{3,2},{4,5},{5,4},{6,7},{7,6},{8,9},{9,8},{10,11... | collective-permute-start | bytes 1966088 | tf_op jit(solution)/shard_map/ppermute | solution.py:39
  105.9 4.0 %collective-permute-start.2 = (bf16[512,640]{1,0:T(8,128)(2,1)S(1)}, bf16[512,640]{1,0:T(8,128)(2,1)S(1)}, u32[]{:S(2)}, u32[]{:S(2)}) collective-permute-start(bf16[512,640]{1,0:T(8,128)(2,1)S(1)} %bitcast.88), channel_id=1, source_target_pairs={{0,1},{1,0},{2,3},{3,2},{4,5},{5,4},{6,7},{7,6},{8,9},{9,8},{10,11... | collective-permute-start | bytes 1966088 | tf_op jit(solution)/shard_map/ppermute | solution.py:39
  107.8 2.2 %copy-start.1 = (bf16[1,1024,640]{2,1,0:T(8,128)(2,1)S(1)}, bf16[1,1024,640]{2,1,0:T(8,128)(2,1)}, u32[]{:S(2)}) copy-start(bf16[1,1024,640]{2,1,0:T(8,128)(2,1)} %param.12) | copy-start | bytes 3932164
  107.8 2.2 %copy-start.2 = (bf16[1,1024,640]{2,1,0:T(8,128)(2,1)S(1)}, bf16[1,1024,640]{2,1,0:T(8,128)(2,1)}, u32[]{:S(2)}) copy-start(bf16[1,1024,640]{2,1,0:T(8,128)(2,1)} %param.11) | copy-start | bytes 3932164
  110.1 1.2 copy-start.4
  111.2 1.6 %copy-start.5 = (bf16[1,448,1024]{2,1,0:T(8,128)(2,1)S(1)}, bf16[1,448,1024]{2,1,0:T(8,128)(2,1)}, u32[]{:S(2)}) copy-start(bf16[1,448,1024]{2,1,0:T(8,128)(2,1)} %param.14) | copy-start | bytes 2752516
  115.6 34.7 %copy-start.3 = (f32[128,2]{0,1:T(2,128)S(1)}, f32[128,2]{0,1:T(2,128)}, u32[]{:S(2)}) copy-start(f32[128,2]{0,1:T(2,128)} %param.10) | copy-start | bytes 3076
  115.6 11.6 %collective-permute-start.3 = (bf16[32,36,128]{2,1,0:T(8,128)(2,1)S(1)}, bf16[32,36,128]{2,1,0:T(8,128)(2,1)S(1)}, u32[]{:S(2)}, u32[]{:S(2)}) collective-permute-start(bf16[32,36,128]{2,1,0:T(8,128)(2,1)S(1)} %fusion.29), channel_id=1, source_target_pairs={{0,16},{16,0},{1,17},{17,1},{2,18},{18,2},{3,19},{19,3},{4,20},{20... | collective-permute-start | bytes 884744 | tf_op jit(solution)/shard_map/ppermute | solution.py:39

commit v3 on v2

--- a/solution.py
+++ b/solution.py
@@ -27,7 +27,7 @@
     up_value = up_saved.astype(jnp.float32)
     sigmoid_gate = jax.nn.sigmoid(gate_value)
     activation = gate_value * sigmoid_gate
-    prob_part = jnp.sum(activation * up_value * grad_units, axis=0)
+    prob_part = jnp.sum(activation * up_value * grad_units, axis=1)
     grad_gate = (
         grad_units * up_value * sigmoid_gate * (1.0 + gate_value * (1.0 - sigmoid_gate))
     ).astype(jnp.bfloat16)
@@ -39,14 +39,73 @@
     return lax.ppermute(value, axis, ((0, 1), (1, 0)))
 
 
+def times_transposed(left, right):
+    return lax.dot_general(
+        left, right, (((1,), (1,)), ((), ())), preferred_element_type=jnp.float32
+    )
+
+
+def chip_sum(rows, down, core):
+    partial = times_transposed(rows, down).astype(jnp.bfloat16)
+    half = partial.shape[1] // 2
+    kept = lax.dynamic_slice_in_dim(partial, core * half, half, 1)
+    other = swap(lax.dynamic_slice_in_dim(partial, (1 - core) * half, half, 1), "c")
+    return (kept.astype(jnp.float32) + other.astype(jnp.float32)).astype(jnp.bfloat16)
+
+
+def over_x(blocks):
+    return lax.all_to_all(blocks, "x", split_axis=0, concat_axis=0, tiled=True)
+
+
+def to_sum(on_chip):
+    chips = lax.axis_size("x")
+    return over_x(on_chip.reshape(chips, on_chip.shape[0] // chips, -1))
+
+
+def add_up(pieces):
+    return jnp.sum(pieces.astype(jnp.float32), axis=0).astype(jnp.bfloat16)
+
+
+def spread(piece):
+    chips = lax.axis_size("x")
+    return over_x(jnp.broadcast_to(piece[None], (chips, *piece.shape))).reshape(
+        chips * piece.shape[0], -1
+    )
+
+
+def chip_gather(spread_half, core):
+    partner = swap(spread_half, "c")
+    return jnp.concatenate(
+        [
+            jnp.where(core == 0, spread_half, partner),
+            jnp.where(core == 0, partner, spread_half),
+        ],
+        axis=1,
+    )
+
+
+def routes_back(grad_units, gate_saved, up_saved, gate_weight, up_weight, experts, capacity):
+    grad_gate, grad_upper, prob_grad = unit_grads(
+        grad_units.astype(jnp.float32), gate_saved, up_saved
+    )
+    route_grad = times_transposed(grad_gate, gate_weight) + times_transposed(
+        grad_upper, up_weight
+    )
+    packed = route_grad.astype(jnp.bfloat16).reshape(experts, -1, 128)
+    probs = jnp.pad(
+        prob_grad.astype(jnp.bfloat16).reshape(experts, 1, capacity),
+        ((0, 0), (0, 0), (0, 128 - capacity)),
+    )
+    return jnp.concatenate([packed, probs], axis=1)
+
+
 def shards(grad_out, route_expert, gate_prob, saved_gate, saved_up, w_gate, w_up, w_down):
     experts = lax.axis_size(PAIR)
     slots_all = saved_gate.shape[2]
-    hidden = saved_gate.shape[1]
-    capacity = slots_all // (2 * experts)
+    slots_side = slots_all // 2
+    capacity = slots_side // experts
     feat_width = grad_out.shape[1]
     block_rows = capacity * feat_width // 128
-    chips = lax.axis_size("x")
     core = lax.axis_index("c")
     side = lax.axis_index("yl")
     slot_match = slot_table(route_expert, experts, capacity)
@@ -57,40 +116,43 @@
     outgoing = outgoing.reshape(experts, block_rows, 128)
     own_rows = lax.all_to_all(outgoing, PAIR, split_axis=0, concat_axis=0, tiled=True)
     pair_rows = swap(own_rows, "yl")
-    first = jnp.where(side == 0, own_rows, pair_rows)
-    second = jnp.where(side == 0, pair_rows, own_rows)
-    arrived = jnp.stack([first, second], axis=1).reshape(slots_all, feat_width)
-    partial = lax.dot_general(
-        w_down[0], arrived, (((1,), (1,)), ((), ())), preferred_element_type=jnp.float32
-    ).astype(jnp.bfloat16)
-    half = hidden // 2
-    kept = lax.dynamic_slice_in_dim(partial, core * half, half, 0)
-    other = swap(lax.dynamic_slice_in_dim(partial, (1 - core) * half, half, 0), "c")
-    on_chip = (kept.astype(jnp.float32) + other.astype(jnp.float32)).astype(jnp.bfloat16)
-    pieces = lax.all_to_all(
-        on_chip.reshape(chips, half // chips, slots_all), "x", split_axis=0, concat_axis=0, tiled=True
+    row = jnp.arange(slots_side, dtype=jnp.int32)[:, None]
+    place = jnp.arange(slots_all, dtype=jnp.int32)[None, :]
+
+    def picked(saved, which):
+        source = (row // capacity * 2 + which) * capacity + row % capacity
+        pick = (place == source).astype(jnp.bfloat16)
+        return times_transposed(pick, saved).astype(jnp.bfloat16)
+
+    own_chip = chip_sum(own_rows.reshape(slots_side, feat_width), w_down[0], core)
+    own_pieces = to_sum(own_chip)
+    pair_chip = chip_sum(pair_rows.reshape(slots_side, feat_width), w_down[0], core)
+    pair_chip, own_pieces = lax.optimization_barrier((pair_chip, own_pieces))
+    pair_pieces = to_sum(pair_chip)
+    pair_half = spread(add_up(pair_pieces))
+    own_piece, pair_half = lax.optimization_barrier((add_up(own_pieces), pair_half))
+    own_half = spread(own_piece)
+    pair_routes = routes_back(
+        chip_gather(pair_half, core),
+        picked(saved_gate[0], 1 - side),
+        picked(saved_up[0], 1 - side),
+        w_gate[0],
+        w_up[0],
+        experts,
+        capacity,
     )
-    summed = jnp.sum(pieces.astype(jnp.float32), axis=0).astype(jnp.bfloat16)
-    spread = lax.all_to_all(
-        jnp.broadcast_to(summed[None], pieces.shape), "x", split_axis=0, concat_axis=0, tiled=True
-    ).reshape(half, slots_all)
-    partner = swap(spread, "c")
-    grad_units = jnp.concatenate(
-        [jnp.where(core == 0, spread, partner), jnp.where(core == 0, partner, spread)], axis=0
-    ).astype(jnp.float32)
-    grad_gate, grad_upper, prob_grad = unit_grads(grad_units, saved_gate[0], saved_up[0])
-    route_grad = jnp.dot(w_gate[0], grad_gate, preferred_element_type=jnp.float32) + jnp.dot(
-        w_up[0], grad_upper, preferred_element_type=jnp.float32
+    pair_back = swap(pair_routes, "yl")
+    own_half, _ = lax.optimization_barrier((own_half, pair_routes))
+    own_routes = routes_back(
+        chip_gather(own_half, core),
+        picked(saved_gate[0], side),
+        picked(saved_up[0], side),
+        w_gate[0],
+        w_up[0],
+        experts,
+        capacity,
     )
-    packed = route_grad.astype(jnp.bfloat16).T.reshape(experts, 2, block_rows, 128)
-    probs = jnp.pad(
-        prob_grad.astype(jnp.bfloat16).reshape(experts, 2, 1, capacity),
-        ((0, 0), (0, 0), (0, 0), (0, 128 - capacity)),
-    )
-    packed = jnp.concatenate([packed, probs], axis=2)
-    kept_back = jnp.where(side == 0, packed[:, 0], packed[:, 1])
-    pair_back = swap(jnp.where(side == 0, packed[:, 1], packed[:, 0]), "yl")
-    both = (kept_back.astype(jnp.float32) + pair_back.astype(jnp.float32)).astype(jnp.bfloat16)
+    both = (own_routes.astype(jnp.float32) + pair_back.astype(jnp.float32)).astype(jnp.bfloat16)
     returned = lax.all_to_all(both, PAIR, split_axis=0, concat_axis=0, tiled=True)
     summed_rows = returned[:, :block_rows].reshape(experts * capacity, feat_width)
     summed_probs = returned[:, block_rows, :capacity].reshape(experts * capacity)

time: 153 us -> 172 us (1.12)
  blocking collectives: 108 us -> 38 us
  starting transfers between devices: 10.8 us -> 49.8 us
  waiting for transfers between devices: 17.7 us -> 53.5 us
  matrix products: 6.17 us -> 14.1 us
  local copies, waits for them, and re-layouts: 3.53 us -> 8.75 us
    all_to_all x3 -> x1, blocking collectives: 85.8 us -> 13.6 us  [over_x(): return lax.all_to_all(blocks, 'x', split_axis=0, concat_axis=0, tiled=True)]
    all_to_all x0 -> x4, waiting for transfers between devices: none -> 43.9 us  [the longest x3 28.8 us: over_x(): return lax.all_to_all(blocks, 'x', split_axis=0, concat_axis=0, tiled=True)]
    all_to_all x0 -> x4, starting transfers between devices: none -> 35.5 us  [the longest x1 21.9 us: shards(): lax.all_to_all(outgoing, PAIR, split_axis=0, concat_axis=0, tiled=True)]
    ppermute x4 -> x6, waiting for transfers between devices: 17.7 us -> 9.64 us  [swap(): return lax.ppermute(value, axis, ((0, 1), (1, 0)))]
    dot_general x3 -> x10, matrix products: 3.69 us -> 11.6 us  [times_transposed(): lax.dot_general(left, right, (((1,), (1,)), ((), ())), preferred_element_...]
    ppermute x4 -> x6, starting transfers between devices: 10.8 us -> 14.3 us  [swap(): return lax.ppermute(value, axis, ((0, 1), (1, 0)))]
    all_to_all x1, blocking collectives: 22.4 us -> 24.4 us  [shards(): lax.all_to_all(both, PAIR, split_axis=0, concat_axis=0, tiled=True)]
    reshape x2 -> x4, local copies, waits for them, and re-layouts: 1.54 us -> 3.26 us  [the longest x1 2.02 us: shards(): pair_rows.reshape(slots_side, feat_width)]
  transfers between devices with their start and end apart: 4 -> 10, of which waited for: 4 -> 7; matrix products, arithmetic and copies ran while one was open for 0% -> 10% of each run, Pallas kernels for 0% -> 0%
where the time goes in v3:
time: 172 us; the launch traced here: 170 us
  waiting for transfers between devices  53.5 us (31%)
  starting transfers between devices  49.8 us (29%)
  blocking collectives  38 us (22%)
  matrix products  14.1 us (8%)
  local copies, waits for them, and re-layouts  8.75 us (5%)
  other arithmetic  5.34 us (3%)
    all_to_all x3, waiting for transfers between devices, over_x(): return lax.all_to_all(blocks, 'x', split_axis=0, concat_axis=0, tiled=True)  28.8 us
    all_to_all x1, blocking collectives, shards(): lax.all_to_all(both, PAIR, split_axis=0, concat_axis=0, tiled=True)  24.4 us
    all_to_all x1, starting transfers between devices, shards(): lax.all_to_all(outgoing, PAIR, split_axis=0, concat_axis=0, tiled=True)  21.9 us
    all_to_all x1, waiting for transfers between devices, shards(): lax.all_to_all(outgoing, PAIR, split_axis=0, concat_axis=0, tiled=True)  15 us
    ppermute x6, starting transfers between devices, swap(): return lax.ppermute(value, axis, ((0, 1), (1, 0)))  14.3 us
    all_to_all x3, starting transfers between devices, over_x(): return lax.all_to_all(blocks, 'x', split_axis=0, concat_axis=0, tiled=True)  13.6 us
    all_to_all x1, blocking collectives, over_x(): return lax.all_to_all(blocks, 'x', split_axis=0, concat_axis=0, tiled=True)  13.6 us
    dot_general x10, matrix products, times_transposed(): lax.dot_general(left, right, (((1,), (1,)), ((), ())), preferred_element_...  11.6 us
  transfers between devices with their start and end apart: 10, of which 7 were waited for; matrix products, arithmetic and copies ran while one was open for 10% of the time, Pallas kernels for 0%

profile of v3, /device:TPU:16, one launch (start us, length us, event | category | flops | bytes accessed | tf_op | source)
XLA Modules:
  0.0 170.4 jit_solution(12173944393707942321)
XLA Ops:
  5.5 21.9 %all-to-all-start = ((bf16[32,35,128]{2,1,0:T(8,128)(2,1)}), bf16[32,35,128]{2,1,0:T(8,128)(2,1)S(1)}, u32[]{:S(2)}, u32[]{:S(2)}) async-start(bf16[32,35,128]{2,1,0:T(8,128)(2,1)} %reshape.120), calls=%async_computation | async-start | bytes 655360 | tf_op jit(solution)/shard_map/all_to_all | solution.py:117
  27.4 15.0 %all-to-all-done = bf16[32,35,128]{2,1,0:T(8,128)(2,1)S(1)} async-done(((bf16[32,35,128]{2,1,0:T(8,128)(2,1)}), bf16[32,35,128]{2,1,0:T(8,128)(2,1)S(1)}, u32[]{:S(2)}, u32[]{:S(2)}) %all-to-all-start) | async-done | bytes 286752 | tf_op jit(solution)/shard_map/all_to_all | solution.py:117
  42.7 3.5 %collective-permute-start = (bf16[32,35,128]{2,1,0:T(8,128)(2,1)S(1)}, bf16[32,35,128]{2,1,0:T(8,128)(2,1)}, u32[]{:S(2)}, u32[]{:S(2)}) collective-permute-start(bf16[32,35,128]{2,1,0:T(8,128)(2,1)S(1)} %all-to-all-done), channel_id=1, source_target_pairs={{0,16},{16,0},{1,17},{17,1},{2,18},{18,2},{3,19},{19,3},{4,20},{20... | collective-permute-start | bytes 860168 | tf_op jit(solution)/shard_map/ppermute | solution.py:39
  47.5 1.9 %collective-permute-start.2 = (bf16[320,512]{1,0:T(8,128)(2,1)}, bf16[320,512]{1,0:T(8,128)(2,1)}, u32[]{:S(2)}, u32[]{:S(2)}) collective-permute-start(bf16[320,512]{1,0:T(8,128)(2,1)} %constant_dynamic-slice_fusion), channel_id=1, source_target_pairs={{0,1},{1,0},{2,3},{3,2},{4,5},{5,4},{6,7},{7,6},{8,9},{9,8},{10,11... | collective-permute-start | bytes 983048 | tf_op jit(solution)/shard_map/ppermute | solution.py:39
  49.4 2.4 %collective-permute-done = bf16[32,35,128]{2,1,0:T(8,128)(2,1)} collective-permute-done((bf16[32,35,128]{2,1,0:T(8,128)(2,1)S(1)}, bf16[32,35,128]{2,1,0:T(8,128)(2,1)}, u32[]{:S(2)}, u32[]{:S(2)}) %collective-permute-start) | collective-permute-done | bytes 286752 | tf_op jit(solution)/shard_map/ppermute | solution.py:39
  51.8 2.0 %reshape.121 = bf16[320,448]{1,0:T(8,128)(2,1)} reshape(bf16[32,35,128]{2,1,0:T(8,128)(2,1)} %collective-permute-done) | data formatting | bytes 573440 | tf_op jit(solution)/shard_map/reshape | solution.py:129
  53.8 1.5 convolution_convert_fusion.5
  55.3 1.8 %add_convert_fusion.1 = bf16[320,512]{1,0:T(8,128)(2,1)} fusion(bf16[320,512]{1,0:T(8,128)(2,1)} %collective-permute-done.2, bf16[320,1024]{1,0:T(8,128)(2,1)S(1)} %convolution_convert_fusion.4, s32[]{:T(128)S(6)} %select_n.84), kind=kLoop, calls=%fused_computation.64 | loop fusion | flops 655360 | bytes 983044 | tf_op jit(solution)/shard_map/convert_element_type | solution.py:53
  57.1 6.8 %all-to-all-start.1 = ((bf16[8,40,512]{2,1,0:T(8,128)(2,1)}), bf16[8,40,512]{2,1,0:T(8,128)(2,1)S(1)}, u32[]{:S(2)}, u32[]{:S(2)}) async-start(bf16[8,40,512]{2,1,0:T(8,128)(2,1)} %bitcast.1), calls=%async_computation.1 | async-start | bytes 655360 | tf_op jit(solution)/shard_map/all_to_all | solution.py:57
  63.9 1.9 %collective-permute-start.1 = (bf16[320,512]{1,0:T(8,128)(2,1)S(1)}, bf16[320,512]{1,0:T(8,128)(2,1)S(1)}, u32[]{:S(2)}, u32[]{:S(2)}) collective-permute-start(bf16[320,512]{1,0:T(8,128)(2,1)S(1)} %constant_dynamic-slice_fusion.1), channel_id=1, source_target_pairs={{0,1},{1,0},{2,3},{3,2},{4,5},{5,4},{6,7},{7,6},{8,9},{9,8},{10,11... | collective-permute-start | bytes 983048 | tf_op jit(solution)/shard_map/ppermute | solution.py:39
  65.8 1.6 collective-permute-done.1
  67.5 7.9 %all-to-all-done.1 = bf16[8,40,512]{2,1,0:T(8,128)(2,1)S(1)} async-done(((bf16[8,40,512]{2,1,0:T(8,128)(2,1)}), bf16[8,40,512]{2,1,0:T(8,128)(2,1)S(1)}, u32[]{:S(2)}, u32[]{:S(2)}) %all-to-all-start.1) | async-done | bytes 327712 | tf_op jit(solution)/shard_map/all_to_all | solution.py:57
  75.4 13.6 %all_to_all.30 = bf16[8,40,512]{2,1,0:T(8,128)(2,1)S(1)} all-to-all(bf16[8,40,512]{2,1,0:T(8,128)(2,1)S(1)} %bitcast.42), channel_id=1, replica_groups=mesh['z'=8,'yh'=4,'yl'=2,'x'=8,'c'=2] {'x'}, dimensions={0} | all-to-all | bytes 655360 | tf_op jit(solution)/shard_map/all_to_all | solution.py:57
  89.8 3.4 %all-to-all-start.3 = ((bf16[8,40,512]{2,1,0:T(8,128)(2,1)}), bf16[8,40,512]{2,1,0:T(8,128)(2,1)S(1)}, u32[]{:S(2)}, u32[]{:S(2)}) async-start(bf16[8,40,512]{2,1,0:T(8,128)(2,1)} %broadcast_in_dim.38), calls=%async_computation.3 | async-start | bytes 655360 | tf_op jit(solution)/shard_map/all_to_all | solution.py:57
  93.3 11.0 %all-to-all-done.3 = bf16[8,40,512]{2,1,0:T(8,128)(2,1)S(1)} async-done(((bf16[8,40,512]{2,1,0:T(8,128)(2,1)}), bf16[8,40,512]{2,1,0:T(8,128)(2,1)S(1)}, u32[]{:S(2)}, u32[]{:S(2)}) %all-to-all-start.3) | async-done | bytes 327712 | tf_op jit(solution)/shard_map/all_to_all | solution.py:57
  104.3 1.9 %collective-permute-start.3 = (bf16[320,512]{1,0:T(8,128)(2,1)S(1)}, bf16[320,512]{1,0:T(8,128)(2,1)S(1)}, u32[]{:S(2)}, u32[]{:S(2)}) collective-permute-start(bf16[320,512]{1,0:T(8,128)(2,1)S(1)} %bitcast.45), channel_id=1, source_target_pairs={{0,1},{1,0},{2,3},{3,2},{4,5},{5,4},{6,7},{7,6},{8,9},{9,8},{10,11... | collective-permute-start | bytes 983048 | tf_op jit(solution)/shard_map/ppermute | solution.py:39
  106.3 2.9 %convolution_convert_fusion.2 = bf16[320,1024]{1,0:T(8,128)(2,1)} fusion(bf16[1,1024,640]{2,1,0:T(8,128)(2,1)} %param.11, s32[320]{0:T(512)S(1)} %multiply_add_fusion.1), kind=kOutput, calls=%fused_computation.16 | convolution fusion | flops 419962880 | bytes 1967360 | tf_op jit(solution)/shard_map/dot_general | solution.py:43
  109.9 3.4 %all-to-all-start.4 = ((bf16[8,40,512]{2,1,0:T(8,128)(2,1)}), bf16[8,40,512]{2,1,0:T(8,128)(2,1)S(1)}, u32[]{:S(2)}, u32[]{:S(2)}) async-start(bf16[8,40,512]{2,1,0:T(8,128)(2,1)} %broadcast_in_dim.62), calls=%async_computation.4 | async-start | bytes 655360 | tf_op jit(solution)/shard_map/all_to_all | solution.py:57
  117.6 9.9 %all-to-all-done.4 = bf16[8,40,512]{2,1,0:T(8,128)(2,1)S(1)} async-done(((bf16[8,40,512]{2,1,0:T(8,128)(2,1)}), bf16[8,40,512]{2,1,0:T(8,128)(2,1)S(1)}, u32[]{:S(2)}, u32[]{:S(2)}) %all-to-all-start.4) | async-done | bytes 327712 | tf_op jit(solution)/shard_map/all_to_all | solution.py:57
  127.5 2.0 %collective-permute-start.4 = (bf16[320,512]{1,0:T(8,128)(2,1)S(1)}, bf16[320,512]{1,0:T(8,128)(2,1)S(1)}, u32[]{:S(2)}, u32[]{:S(2)}) collective-permute-start(bf16[320,512]{1,0:T(8,128)(2,1)S(1)} %bitcast.43), channel_id=1, source_target_pairs={{0,1},{1,0},{2,3},{3,2},{4,5},{5,4},{6,7},{7,6},{8,9},{9,8},{10,11... | collective-permute-start | bytes 983048 | tf_op jit(solution)/shard_map/ppermute | solution.py:39
  129.5 2.1 %convolution_convert_fusion = bf16[320,1024]{1,0:T(8,128)(2,1)S(1)} fusion(bf16[1,1024,640]{2,1,0:T(8,128)(2,1)} %param.11, s32[320]{0:T(512)S(1)} %multiply_add_fusion), kind=kOutput, calls=%fused_computation.14 | convolution fusion | flops 419962880 | bytes 1967360 | tf_op jit(solution)/shard_map/dot_general | solution.py:43
  131.6 3.1 %collective-permute-start.5 = (bf16[32,36,128]{2,1,0:T(8,128)(2,1)S(1)}, bf16[32,36,128]{2,1,0:T(8,128)(2,1)S(1)}, u32[]{:S(2)}, u32[]{:S(2)}) collective-permute-start(bf16[32,36,128]{2,1,0:T(8,128)(2,1)S(1)} %fusion.42), channel_id=1, source_target_pairs={{0,16},{16,0},{1,17},{17,1},{2,18},{18,2},{3,19},{19,3},{4,20},{20... | collective-permute-start | bytes 884744 | tf_op jit(solution)/shard_map/ppermute | solution.py:39
  137.9 5.7 %collective-permute-done.5 = bf16[32,36,128]{2,1,0:T(8,128)(2,1)S(1)} collective-permute-done((bf16[32,36,128]{2,1,0:T(8,128)(2,1)S(1)}, bf16[32,36,128]{2,1,0:T(8,128)(2,1)S(1)}, u32[]{:S(2)}, u32[]{:S(2)}) %collective-permute-start.5) | collective-permute-done | bytes 294944 | tf_op jit(solution)/shard_map/ppermute | solution.py:39
  143.7 24.4 %all_to_all.31 = bf16[32,36,128]{2,1,0:T(8,128)(2,1)S(1)} all-to-all(bf16[32,36,128]{2,1,0:T(8,128)(2,1)S(1)} %add_convert_fusion), channel_id=1, replica_groups=mesh['z'=8,'yh'=4,'yl'=2,'x'=8,'c'=2] {'z','yh'}, dimensions={0} | all-to-all | bytes 589824 | tf_op jit(solution)/shard_map/all_to_all | solution.py:156
  (56 shorter events, 17.9 us)
Async XLA Ops:
  0.6 114.4 %copy-start = (bf16[1,1024,640]{2,1,0:T(8,128)(2,1)S(1)}, bf16[1,1024,640]{2,1,0:T(8,128)(2,1)}, u32[]{:S(2)}) copy-start(bf16[1,1024,640]{2,1,0:T(8,128)(2,1)} %param.12) | copy-start | bytes 3932164
  0.6 45.6 %copy-start.1 = (bf16[1,1024,448]{1,2,0:T(8,128)(2,1)S(1)}, bf16[1,1024,448]{1,2,0:T(8,128)(2,1)}, u32[]{:S(2)}) copy-start(bf16[1,1024,448]{1,2,0:T(8,128)(2,1)} %param.15) | copy-start | bytes 2752516
  5.5 36.9 %all-to-all-start = ((bf16[32,35,128]{2,1,0:T(8,128)(2,1)}), bf16[32,35,128]{2,1,0:T(8,128)(2,1)S(1)}, u32[]{:S(2)}, u32[]{:S(2)}) async-start(bf16[32,35,128]{2,1,0:T(8,128)(2,1)} %reshape.120), calls=%async_computation | async-start | bytes 655360 | tf_op jit(solution)/shard_map/all_to_all | solution.py:117
  42.7 9.1 %collective-permute-start = (bf16[32,35,128]{2,1,0:T(8,128)(2,1)S(1)}, bf16[32,35,128]{2,1,0:T(8,128)(2,1)}, u32[]{:S(2)}, u32[]{:S(2)}) collective-permute-start(bf16[32,35,128]{2,1,0:T(8,128)(2,1)S(1)} %all-to-all-done), channel_id=1, source_target_pairs={{0,16},{16,0},{1,17},{17,1},{2,18},{18,2},{3,19},{19,3},{4,20},{20... | collective-permute-start | bytes 860168 | tf_op jit(solution)/shard_map/ppermute | solution.py:39
  47.5 7.8 %collective-permute-start.2 = (bf16[320,512]{1,0:T(8,128)(2,1)}, bf16[320,512]{1,0:T(8,128)(2,1)}, u32[]{:S(2)}, u32[]{:S(2)}) collective-permute-start(bf16[320,512]{1,0:T(8,128)(2,1)} %constant_dynamic-slice_fusion), channel_id=1, source_target_pairs={{0,1},{1,0},{2,3},{3,2},{4,5},{5,4},{6,7},{7,6},{8,9},{9,8},{10,11... | collective-permute-start | bytes 983048 | tf_op jit(solution)/shard_map/ppermute | solution.py:39
  57.1 18.4 %all-to-all-start.1 = ((bf16[8,40,512]{2,1,0:T(8,128)(2,1)}), bf16[8,40,512]{2,1,0:T(8,128)(2,1)S(1)}, u32[]{:S(2)}, u32[]{:S(2)}) async-start(bf16[8,40,512]{2,1,0:T(8,128)(2,1)} %bitcast.1), calls=%async_computation.1 | async-start | bytes 655360 | tf_op jit(solution)/shard_map/all_to_all | solution.py:57
  63.9 3.5 %collective-permute-start.1 = (bf16[320,512]{1,0:T(8,128)(2,1)S(1)}, bf16[320,512]{1,0:T(8,128)(2,1)S(1)}, u32[]{:S(2)}, u32[]{:S(2)}) collective-permute-start(bf16[320,512]{1,0:T(8,128)(2,1)S(1)} %constant_dynamic-slice_fusion.1), channel_id=1, source_target_pairs={{0,1},{1,0},{2,3},{3,2},{4,5},{5,4},{6,7},{7,6},{8,9},{9,8},{10,11... | collective-permute-start | bytes 983048 | tf_op jit(solution)/shard_map/ppermute | solution.py:39
  89.8 14.5 %all-to-all-start.3 = ((bf16[8,40,512]{2,1,0:T(8,128)(2,1)}), bf16[8,40,512]{2,1,0:T(8,128)(2,1)S(1)}, u32[]{:S(2)}, u32[]{:S(2)}) async-start(bf16[8,40,512]{2,1,0:T(8,128)(2,1)} %broadcast_in_dim.38), calls=%async_computation.3 | async-start | bytes 655360 | tf_op jit(solution)/shard_map/all_to_all | solution.py:57
  104.3 9.0 %collective-permute-start.3 = (bf16[320,512]{1,0:T(8,128)(2,1)S(1)}, bf16[320,512]{1,0:T(8,128)(2,1)S(1)}, u32[]{:S(2)}, u32[]{:S(2)}) collective-permute-start(bf16[320,512]{1,0:T(8,128)(2,1)S(1)} %bitcast.45), channel_id=1, source_target_pairs={{0,1},{1,0},{2,3},{3,2},{4,5},{5,4},{6,7},{7,6},{8,9},{9,8},{10,11... | collective-permute-start | bytes 983048 | tf_op jit(solution)/shard_map/ppermute | solution.py:39
  109.1 4.3 %copy-start.3 = (bf16[1,448,1024]{2,1,0:T(8,128)(2,1)S(1)}, bf16[1,448,1024]{2,1,0:T(8,128)(2,1)}, u32[]{:S(2)}) copy-start(bf16[1,448,1024]{2,1,0:T(8,128)(2,1)} %param.14) | copy-start | bytes 2752516
  109.9 17.6 %all-to-all-start.4 = ((bf16[8,40,512]{2,1,0:T(8,128)(2,1)}), bf16[8,40,512]{2,1,0:T(8,128)(2,1)S(1)}, u32[]{:S(2)}, u32[]{:S(2)}) async-start(bf16[8,40,512]{2,1,0:T(8,128)(2,1)} %broadcast_in_dim.62), calls=%async_computation.4 | async-start | bytes 655360 | tf_op jit(solution)/shard_map/all_to_all | solution.py:57
  113.3 1.1 copy-start.7
  115.0 1.2 copy-start.5
  127.5 7.2 %collective-permute-start.4 = (bf16[320,512]{1,0:T(8,128)(2,1)S(1)}, bf16[320,512]{1,0:T(8,128)(2,1)S(1)}, u32[]{:S(2)}, u32[]{:S(2)}) collective-permute-start(bf16[320,512]{1,0:T(8,128)(2,1)S(1)} %bitcast.43), channel_id=1, source_target_pairs={{0,1},{1,0},{2,3},{3,2},{4,5},{5,4},{6,7},{7,6},{8,9},{9,8},{10,11... | collective-permute-start | bytes 983048 | tf_op jit(solution)/shard_map/ppermute | solution.py:39
  129.5 5.3 %copy-start.4 = (bf16[1,448,1024]{2,1,0:T(8,128)(2,1)S(1)}, bf16[1,448,1024]{2,1,0:T(8,128)(2,1)}, u32[]{:S(2)}) copy-start(bf16[1,448,1024]{2,1,0:T(8,128)(2,1)} %param.14) | copy-start | bytes 2752516
  131.6 11.9 %collective-permute-start.5 = (bf16[32,36,128]{2,1,0:T(8,128)(2,1)S(1)}, bf16[32,36,128]{2,1,0:T(8,128)(2,1)S(1)}, u32[]{:S(2)}, u32[]{:S(2)}) collective-permute-start(bf16[32,36,128]{2,1,0:T(8,128)(2,1)S(1)} %fusion.42), channel_id=1, source_target_pairs={{0,16},{16,0},{1,17},{17,1},{2,18},{18,2},{3,19},{19,3},{4,20},{20... | collective-permute-start | bytes 884744 | tf_op jit(solution)/shard_map/ppermute | solution.py:39
  135.3 1.2 copy-start.6
  137.8 30.8 %copy-start.2 = (f32[128,2]{0,1:T(2,128)S(1)}, f32[128,2]{0,1:T(2,128)}, u32[]{:S(2)}) copy-start(f32[128,2]{0,1:T(2,128)} %param.10) | copy-start | bytes 3076

commit v4 on v3

--- a/solution.py
+++ b/solution.py
@@ -6,6 +6,7 @@
 
 FULL_PRECISION = lax.Precision.HIGHEST
 PAIR = ("z", "yh")
+NODE = ("z", "yh", "yl")
 
 
 def slot_table(routes, experts, capacity):
@@ -45,21 +46,8 @@
     )
 
 
-def chip_sum(rows, down, core):
-    partial = times_transposed(rows, down).astype(jnp.bfloat16)
-    half = partial.shape[1] // 2
-    kept = lax.dynamic_slice_in_dim(partial, core * half, half, 1)
-    other = swap(lax.dynamic_slice_in_dim(partial, (1 - core) * half, half, 1), "c")
-    return (kept.astype(jnp.float32) + other.astype(jnp.float32)).astype(jnp.bfloat16)
-
-
 def over_x(blocks):
     return lax.all_to_all(blocks, "x", split_axis=0, concat_axis=0, tiled=True)
-
-
-def to_sum(on_chip):
-    chips = lax.axis_size("x")
-    return over_x(on_chip.reshape(chips, on_chip.shape[0] // chips, -1))
 
 
 def add_up(pieces):
@@ -73,14 +61,10 @@
     )
 
 
-def chip_gather(spread_half, core):
-    partner = swap(spread_half, "c")
+def chip_gather(half, core):
+    partner = swap(half, "c")
     return jnp.concatenate(
-        [
-            jnp.where(core == 0, spread_half, partner),
-            jnp.where(core == 0, partner, spread_half),
-        ],
-        axis=1,
+        [jnp.where(core == 0, half, partner), jnp.where(core == 0, partner, half)], axis=1
     )
 
 
@@ -99,61 +83,83 @@
     return jnp.concatenate([packed, probs], axis=1)
 
 
+def turned(pair):
+    return (pair % lax.axis_size("yh")) // (lax.axis_size("yh") // 2)
+
+
+def over_group(blocks):
+    pairs = lax.axis_size(PAIR)
+    groups = [[2 * p + (g ^ turned(p)) for p in range(pairs)] for g in range(2)]
+    return lax.all_to_all(
+        blocks, NODE, split_axis=0, concat_axis=0, tiled=True, axis_index_groups=groups
+    )
+
+
 def shards(grad_out, route_expert, gate_prob, saved_gate, saved_up, w_gate, w_up, w_down):
     experts = lax.axis_size(PAIR)
+    chips = lax.axis_size("x")
     slots_all = saved_gate.shape[2]
     slots_side = slots_all // 2
     capacity = slots_side // experts
     feat_width = grad_out.shape[1]
+    half = saved_gate.shape[1] // 2
     block_rows = capacity * feat_width // 128
     core = lax.axis_index("c")
-    side = lax.axis_index("yl")
+    group = lax.axis_index("yl") ^ turned(lax.axis_index("yh"))
     slot_match = slot_table(route_expert, experts, capacity)
     dispatch_mask = jnp.any(slot_match, axis=2).astype(jnp.bfloat16)
     outgoing = jnp.dot(dispatch_mask, grad_out, preferred_element_type=jnp.float32).astype(
         jnp.bfloat16
     )
-    outgoing = outgoing.reshape(experts, block_rows, 128)
-    own_rows = lax.all_to_all(outgoing, PAIR, split_axis=0, concat_axis=0, tiled=True)
+    own_rows = over_group(outgoing.reshape(experts, block_rows, 128))
+
+    slot = jnp.arange(slots_all, dtype=jnp.int32)[:, None]
+    place = jnp.arange(slots_all, dtype=jnp.int32)[None, :]
+    pair = slot // capacity % experts
+    member = group ^ turned(pair) ^ (slot // slots_side)
+    source = (2 * pair + member) * capacity + slot % capacity
+    order = (place == source).astype(jnp.bfloat16)
+    gate_rows = times_transposed(order, saved_gate[0]).astype(jnp.bfloat16)
+    up_rows = times_transposed(order, saved_up[0]).astype(jnp.bfloat16)
+    down_kept = lax.dynamic_slice_in_dim(w_down[0], core * half, half, 0)
+    down_other = swap(lax.dynamic_slice_in_dim(w_down[0], (1 - core) * half, half, 0), "c")
+    own_rows, gate_rows, up_rows, down_other = lax.optimization_barrier(
+        (own_rows, gate_rows, up_rows, down_other)
+    )
+
     pair_rows = swap(own_rows, "yl")
-    row = jnp.arange(slots_side, dtype=jnp.int32)[:, None]
-    place = jnp.arange(slots_all, dtype=jnp.int32)[None, :]
-
-    def picked(saved, which):
-        source = (row // capacity * 2 + which) * capacity + row % capacity
-        pick = (place == source).astype(jnp.bfloat16)
-        return times_transposed(pick, saved).astype(jnp.bfloat16)
-
-    own_chip = chip_sum(own_rows.reshape(slots_side, feat_width), w_down[0], core)
-    own_pieces = to_sum(own_chip)
-    pair_chip = chip_sum(pair_rows.reshape(slots_side, feat_width), w_down[0], core)
-    pair_chip, own_pieces = lax.optimization_barrier((pair_chip, own_pieces))
-    pair_pieces = to_sum(pair_chip)
-    pair_half = spread(add_up(pair_pieces))
-    own_piece, pair_half = lax.optimization_barrier((add_up(own_pieces), pair_half))
-    own_half = spread(own_piece)
+    own_other = swap(own_rows, "c")
+    pair_rows, own_other = lax.optimization_barrier((pair_rows, own_other))
+    pair_other = swap(pair_rows, "c")
+    kept_rows = jnp.concatenate([own_rows, pair_rows]).reshape(slots_all, feat_width)
+    other_rows = jnp.concatenate([own_other, pair_other]).reshape(slots_all, feat_width)
+    on_chip = (
+        times_transposed(kept_rows, down_kept) + times_transposed(other_rows, down_other)
+    ).astype(jnp.bfloat16)
+    pieces = over_x(on_chip.reshape(chips, slots_all // chips, half))
+    half_units = spread(add_up(pieces))
     pair_routes = routes_back(
-        chip_gather(pair_half, core),
-        picked(saved_gate[0], 1 - side),
-        picked(saved_up[0], 1 - side),
+        chip_gather(half_units[slots_side:], core),
+        gate_rows[slots_side:],
+        up_rows[slots_side:],
         w_gate[0],
         w_up[0],
         experts,
         capacity,
     )
     pair_back = swap(pair_routes, "yl")
-    own_half, _ = lax.optimization_barrier((own_half, pair_routes))
+    own_units, _ = lax.optimization_barrier((chip_gather(half_units[:slots_side], core), pair_routes))
     own_routes = routes_back(
-        chip_gather(own_half, core),
-        picked(saved_gate[0], side),
-        picked(saved_up[0], side),
+        own_units,
+        gate_rows[:slots_side],
+        up_rows[:slots_side],
         w_gate[0],
         w_up[0],
         experts,
         capacity,
     )
     both = (own_routes.astype(jnp.float32) + pair_back.astype(jnp.float32)).astype(jnp.bfloat16)
-    returned = lax.all_to_all(both, PAIR, split_axis=0, concat_axis=0, tiled=True)
+    returned = over_group(both)
     summed_rows = returned[:, :block_rows].reshape(experts * capacity, feat_width)
     summed_probs = returned[:, block_rows, :capacity].reshape(experts * capacity)
     weights = jnp.sum(jnp.where(slot_match, gate_prob[None, :, :], 0.0), axis=2)
@@ -176,7 +182,7 @@
         mesh.devices.reshape(nodes // rows, rows // 2, 2, local // 2, 2),
         ("z", "yh", "yl", "x", "c"),
     )
-    node, feats = ("z", "yh", "yl"), ("x", "c")
+    node, feats = NODE, ("x", "c")
     return jax.shard_map(
         shards,
         mesh=fine,

time: 172 us -> 163 us (0.948)
  waiting for transfers between devices: 53.5 us -> 19.3 us
  blocking collectives: 38 us -> 69.4 us
  starting transfers between devices: 49.8 us -> 37.1 us
  other arithmetic: 5.34 us -> 10.6 us
  matrix products: 14.1 us -> 16.1 us
    all_to_all x1 -> x2, blocking collectives: 13.6 us -> 50.7 us  [over_x(): return lax.all_to_all(blocks, 'x', split_axis=0, concat_axis=0, tiled=True)]
    all_to_all x4 -> x1, waiting for transfers between devices: 43.9 us -> 8.16 us  [over_group(): lax.all_to_all(blocks, NODE, split_axis=0, concat_axis=0, tiled=True, axi...]
    all_to_all x4 -> x1, starting transfers between devices: 35.5 us -> 21.7 us  [over_group(): lax.all_to_all(blocks, NODE, split_axis=0, concat_axis=0, tiled=True, axi...]
    all_to_all x1, blocking collectives: 24.4 us -> 18.7 us  [over_group(): lax.all_to_all(blocks, NODE, split_axis=0, concat_axis=0, tiled=True, axi...]
    reshape x2, local copies, waits for them, and re-layouts: 0.94 us -> 3.62 us  [routes_back(): packed = route_grad.astype(jnp.bfloat16).reshape(experts, -1, 128)]
    reduce_sum x0 -> x2, other arithmetic: none -> 2.23 us  [unit_grads(): prob_part = jnp.sum(activation * up_value * grad_units, axis=1)]
    concatenate x0 -> x3, other arithmetic: none -> 2.16 us  [the longest x1 1.04 us: shards(): jnp.concatenate([own_rows, pair_rows]).reshape(slots_all, feat_width)]
    dot_general x10 -> x8, matrix products: 11.6 us -> 13.6 us  [times_transposed(): lax.dot_general(left, right, (((1,), (1,)), ((), ())), preferred_element_...]
  transfers between devices with their start and end apart: 10 -> 8, of which waited for: 7 -> 3; matrix products, arithmetic and copies ran while one was open for 10% -> 13% of each run, Pallas kernels for 0% -> 0%
where the time goes in v4:
time: 163 us; the launch traced here: 162 us
  blocking collectives  69.4 us (43%)
  starting transfers between devices  37.1 us (23%)
  waiting for transfers between devices  19.3 us (12%)
  matrix products  16.1 us (10%)
  other arithmetic  10.6 us (7%)
  local copies, waits for them, and re-layouts  8.4 us (5%)
    all_to_all x2, blocking collectives, over_x(): return lax.all_to_all(blocks, 'x', split_axis=0, concat_axis=0, tiled=True)  50.7 us
    all_to_all x1, starting transfers between devices, over_group(): lax.all_to_all(blocks, NODE, split_axis=0, concat_axis=0, tiled=True, axi...  21.7 us
    all_to_all x1, blocking collectives, over_group(): lax.all_to_all(blocks, NODE, split_axis=0, concat_axis=0, tiled=True, axi...  18.7 us
    ppermute x7, starting transfers between devices, swap(): return lax.ppermute(value, axis, ((0, 1), (1, 0)))  15.4 us
    dot_general x8, matrix products, times_transposed(): lax.dot_general(left, right, (((1,), (1,)), ((), ())), preferred_element_...  13.6 us
    ppermute x7, waiting for transfers between devices, swap(): return lax.ppermute(value, axis, ((0, 1), (1, 0)))  11.1 us
    all_to_all x1, waiting for transfers between devices, over_group(): lax.all_to_all(blocks, NODE, split_axis=0, concat_axis=0, tiled=True, axi...  8.16 us
    reshape x2, local copies, waits for them, and re-layouts, routes_back(): packed = route_grad.astype(jnp.bfloat16).reshape(experts, -1, 128)  3.62 us
  transfers between devices with their start and end apart: 8, of which 3 were waited for; matrix products, arithmetic and copies ran while one was open for 13% of the time, Pallas kernels for 0%

profile of v4, /device:TPU:16, one launch (start us, length us, event | category | flops | bytes accessed | tf_op | source)
XLA Modules:
  0.0 161.9 jit_solution(1603768040570648778)
XLA Ops:
  5.5 21.7 %all-to-all-start = ((bf16[32,35,128]{2,1,0:T(8,128)(2,1)}), bf16[32,35,128]{2,1,0:T(8,128)(2,1)S(1)}, u32[]{:S(2)}, u32[]{:S(2)}) async-start(bf16[32,35,128]{2,1,0:T(8,128)(2,1)} %reshape.196), calls=%async_computation | async-start | bytes 655360 | tf_op jit(solution)/shard_map/all_to_all | solution.py:93
  27.2 1.9 %collective-permute-start = (bf16[512,448]{0,1:T(8,128)(2,1)S(1)}, bf16[512,448]{0,1:T(8,128)(2,1)S(1)}, u32[]{:S(2)}, u32[]{:S(2)}) collective-permute-start(bf16[512,448]{0,1:T(8,128)(2,1)S(1)} %dynamic-slice_bitcast_fusion), channel_id=1, source_target_pairs={{0,1},{1,0},{2,3},{3,2},{4,5},{5,4},{6,7},{7,6},{8,9},{9,8},{10,11... | collective-permute-start | bytes 1376264 | tf_op jit(solution)/shard_map/ppermute | solution.py:40
  29.2 2.3 %fusion.3 = bf16[640,1024]{1,0:T(8,128)(2,1)} fusion(bf16[1,1024,640]{2,1,0:T(8,128)(2,1)S(1)} %copy-done, s32[640]{0:T(1024)S(1)} %fusion.62), kind=kOutput, calls=%fused_computation.18 | convolution fusion | flops 839925760 | bytes 2624000 | tf_op jit(solution)/shard_map/dot_general | solution.py:44
  31.5 2.3 %fusion.2 = bf16[640,1024]{1,0:T(8,128)(2,1)} fusion(bf16[1,1024,640]{2,1,0:T(8,128)(2,1)S(1)} %copy-done.9, s32[640]{0:T(1024)S(1)} %fusion.62), kind=kOutput, calls=%fused_computation.17 | convolution fusion | flops 839925760 | bytes 2624000 | tf_op jit(solution)/shard_map/dot_general | solution.py:44
  33.8 8.2 %all-to-all-done = bf16[32,35,128]{2,1,0:T(8,128)(2,1)S(1)} async-done(((bf16[32,35,128]{2,1,0:T(8,128)(2,1)}), bf16[32,35,128]{2,1,0:T(8,128)(2,1)S(1)}, u32[]{:S(2)}, u32[]{:S(2)}) %all-to-all-start) | async-done | bytes 286752 | tf_op jit(solution)/shard_map/all_to_all | solution.py:93
  42.0 1.9 %collective-permute-start.2 = (bf16[32,35,128]{2,1,0:T(8,128)(2,1)S(1)}, bf16[32,35,128]{2,1,0:T(8,128)(2,1)S(1)}, u32[]{:S(2)}, u32[]{:S(2)}) collective-permute-start(bf16[32,35,128]{2,1,0:T(8,128)(2,1)S(1)} %all-to-all-done), channel_id=1, source_target_pairs={{0,1},{1,0},{2,3},{3,2},{4,5},{5,4},{6,7},{7,6},{8,9},{9,8},{10,11... | collective-permute-start | bytes 860168 | tf_op jit(solution)/shard_map/ppermute | solution.py:40
  43.9 2.6 %collective-permute-start.1 = (bf16[32,35,128]{2,1,0:T(8,128)(2,1)S(1)}, bf16[32,35,128]{2,1,0:T(8,128)(2,1)}, u32[]{:S(2)}, u32[]{:S(2)}) collective-permute-start(bf16[32,35,128]{2,1,0:T(8,128)(2,1)S(1)} %all-to-all-done), channel_id=1, source_target_pairs={{0,16},{16,0},{1,17},{17,1},{2,18},{18,2},{3,19},{19,3},{4,20},{20... | collective-permute-start | bytes 860168 | tf_op jit(solution)/shard_map/ppermute | solution.py:40
  46.5 9.5 %collective-permute-done.1 = bf16[32,35,128]{2,1,0:T(8,128)(2,1)} collective-permute-done((bf16[32,35,128]{2,1,0:T(8,128)(2,1)S(1)}, bf16[32,35,128]{2,1,0:T(8,128)(2,1)}, u32[]{:S(2)}, u32[]{:S(2)}) %collective-permute-start.1) | collective-permute-done | bytes 286752 | tf_op jit(solution)/shard_map/ppermute | solution.py:40
  56.0 1.9 %collective-permute-start.3 = (bf16[32,35,128]{2,1,0:T(8,128)(2,1)}, bf16[32,35,128]{2,1,0:T(8,128)(2,1)}, u32[]{:S(2)}, u32[]{:S(2)}) collective-permute-start(bf16[32,35,128]{2,1,0:T(8,128)(2,1)} %collective-permute-done.1), channel_id=1, source_target_pairs={{0,1},{1,0},{2,3},{3,2},{4,5},{5,4},{6,7},{7,6},{8,9},{9,8},{10,11... | collective-permute-start | bytes 860168 | tf_op jit(solution)/shard_map/ppermute | solution.py:40
  59.6 1.6 fusion.45
  62.3 1.5 reshape.198
  63.7 1.7 %fusion.4 = bf16[640,512]{1,0:T(8,128)(2,1)S(1)} fusion(f32[640,512]{1,0:T(8,128)S(1)} %fusion.45, bf16[640,448]{1,0:T(8,128)(2,1)} %reshape.198, bf16[512,448]{0,1:T(8,128)(2,1)} %copy-done.5), kind=kOutput, calls=%fused_computation.20 | convolution fusion | flops 294256640 | bytes 2998272 | tf_op jit(solution)/shard_map/dot_general | solution.py:44
  65.4 27.5 %all_to_all.20 = bf16[8,80,512]{2,1,0:T(8,128)(2,1)S(1)} all-to-all(bf16[8,80,512]{2,1,0:T(8,128)(2,1)S(1)} %bitcast.37), channel_id=1, replica_groups=mesh['z'=8,'yh'=4,'yl'=2,'x'=8,'c'=2] {'x'}, dimensions={0} | all-to-all | bytes 1310720 | tf_op jit(solution)/shard_map/all_to_all | solution.py:50
  93.1 23.2 %all_to_all.21 = bf16[8,80,512]{2,1,0:T(8,128)(2,1)S(1)} all-to-all(bf16[8,80,512]{2,1,0:T(8,128)(2,1)S(1)} %broadcast_in_dim.55), channel_id=1, replica_groups=mesh['z'=8,'yh'=4,'yl'=2,'x'=8,'c'=2] {'x'}, dimensions={0} | all-to-all | bytes 1310720 | tf_op jit(solution)/shard_map/all_to_all | solution.py:50
  116.4 1.9 %collective-permute-start.5 = (bf16[320,512]{1,0:T(8,128)(2,1)S(1)}, bf16[320,512]{1,0:T(8,128)(2,1)S(1)}, u32[]{:S(2)}, u32[]{:S(2)}) collective-permute-start(bf16[320,512]{1,0:T(8,128)(2,1)S(1)} %bitcast.40), channel_id=1, source_target_pairs={{0,1},{1,0},{2,3},{3,2},{4,5},{5,4},{6,7},{7,6},{8,9},{9,8},{10,11... | collective-permute-start | bytes 983048 | tf_op jit(solution)/shard_map/ppermute | solution.py:40
  118.3 2.4 %collective-permute-start.4 = (bf16[320,512]{1,0:T(8,128)(2,1)S(1)}, bf16[320,512]{1,0:T(8,128)(2,1)}, u32[]{:S(2)}, u32[]{:S(2)}) collective-permute-start(bf16[320,512]{1,0:T(8,128)(2,1)S(1)} %bitcast.39), channel_id=1, source_target_pairs={{0,1},{1,0},{2,3},{3,2},{4,5},{5,4},{6,7},{7,6},{8,9},{9,8},{10,11... | collective-permute-start | bytes 983048 | tf_op jit(solution)/shard_map/ppermute | solution.py:40
  120.8 2.1 %fusion.28 = f32[320,448]{1,0:T(8,128)S(1)} fusion(bf16[1,448,1024]{2,1,0:T(8,128)(2,1)} %param.14, bf16[640,1024]{1,0:T(8,128)(2,1)} %fusion.2, bf16[320,512]{1,0:T(8,128)(2,1)S(1)} %get-tuple-element.23, bf16[320,512]{1,0:T(8,128)(2,1)S(1)} %get-tuple-element.22), kind=kOutput, calls=%fused_computation.48 | convolution fusion | flops 297205760 | bytes 2801664 | tf_op jit(solution)/shard_map/dot_general | solution.py:44
  123.2 1.5 fusion.25
  125.5 1.4 reshape.200
  127.7 2.7 %collective-permute-start.6 = (bf16[32,36,128]{2,1,0:T(8,128)(2,1)}, bf16[32,36,128]{2,1,0:T(8,128)(2,1)}, u32[]{:S(2)}, u32[]{:S(2)}) collective-permute-start(bf16[32,36,128]{2,1,0:T(8,128)(2,1)} %fusion.48), channel_id=1, source_target_pairs={{0,16},{16,0},{1,17},{17,1},{2,18},{18,2},{3,19},{19,3},{4,20},{20... | collective-permute-start | bytes 884744 | tf_op jit(solution)/shard_map/ppermute | solution.py:40
  134.1 2.2 %reshape.201 = bf16[32,35,128]{2,1,0:T(8,128)(2,1)} reshape(bf16[320,448]{1,0:T(8,128)(2,1)} %fusion.26) | data formatting | bytes 573440 | tf_op jit(solution)/shard_map/reshape | solution.py:78
  136.3 1.7 %fusion.18 = bf16[320]{0:T(512)(128)(2,1)S(1)} fusion(bf16[320,1024]{1,0:T(8,128)(2,1)S(1)} %pad_maximum_fusion.2, bf16[640,1024]{1,0:T(8,128)(2,1)S(1)} %copy-done.1, bf16[640,1024]{1,0:T(8,128)(2,1)} %fusion.2), kind=kLoop, calls=%fused_computation.34 | loop fusion | flops 3276480 | bytes 1966720 | tf_op jit(solution)/shard_map/reduce_sum | solution.py:31
  138.1 1.6 %collective-permute-done.6 = bf16[32,36,128]{2,1,0:T(8,128)(2,1)} collective-permute-done((bf16[32,36,128]{2,1,0:T(8,128)(2,1)}, bf16[32,36,128]{2,1,0:T(8,128)(2,1)}, u32[]{:S(2)}, u32[]{:S(2)}) %collective-permute-start.6) | collective-permute-done | bytes 294944 | tf_op jit(solution)/shard_map/ppermute | solution.py:40
  140.9 18.7 %all_to_all.22 = bf16[32,36,128]{2,1,0:T(8,128)(2,1)S(1)} all-to-all(bf16[32,36,128]{2,1,0:T(8,128)(2,1)S(1)} %add_convert_fusion), channel_id=1, replica_groups={{0,32,80,112,128,160,208,240,256,288,336,368,384,416,464,496,512,544,59..., dimensions={0} | all-to-all | bytes 589824 | tf_op jit(solution)/shard_map/all_to_all | solution.py:93
  (61 shorter events, 16.9 us)
Async XLA Ops:
  0.6 28.6 %copy-start = (bf16[1,1024,640]{2,1,0:T(8,128)(2,1)S(1)}, bf16[1,1024,640]{2,1,0:T(8,128)(2,1)}, u32[]{:S(2)}) copy-start(bf16[1,1024,640]{2,1,0:T(8,128)(2,1)} %param.12) | copy-start | bytes 3932164
  0.6 26.5 %copy-start.4 = (bf16[1,1024,448]{1,2,0:T(8,128)(2,1)S(1)}, bf16[1,1024,448]{1,2,0:T(8,128)(2,1)}, u32[]{:S(2)}) copy-start(bf16[1,1024,448]{1,2,0:T(8,128)(2,1)} %param.15) | copy-start | bytes 2752516
  5.5 36.5 %all-to-all-start = ((bf16[32,35,128]{2,1,0:T(8,128)(2,1)}), bf16[32,35,128]{2,1,0:T(8,128)(2,1)S(1)}, u32[]{:S(2)}, u32[]{:S(2)}) async-start(bf16[32,35,128]{2,1,0:T(8,128)(2,1)} %reshape.196), calls=%async_computation | async-start | bytes 655360 | tf_op jit(solution)/shard_map/all_to_all | solution.py:93
  27.2 6.6 %collective-permute-start = (bf16[512,448]{0,1:T(8,128)(2,1)S(1)}, bf16[512,448]{0,1:T(8,128)(2,1)S(1)}, u32[]{:S(2)}, u32[]{:S(2)}) collective-permute-start(bf16[512,448]{0,1:T(8,128)(2,1)S(1)} %dynamic-slice_bitcast_fusion), channel_id=1, source_target_pairs={{0,1},{1,0},{2,3},{3,2},{4,5},{5,4},{6,7},{7,6},{8,9},{9,8},{10,11... | collective-permute-start | bytes 1376264 | tf_op jit(solution)/shard_map/ppermute | solution.py:40
  29.2 2.3 %copy-start.9 = (bf16[1,1024,640]{2,1,0:T(8,128)(2,1)S(1)}, bf16[1,1024,640]{2,1,0:T(8,128)(2,1)}, u32[]{:S(2)}) copy-start(bf16[1,1024,640]{2,1,0:T(8,128)(2,1)} %param.11) | copy-start | bytes 3932164
  33.8 24.1 %copy-start.5 = (bf16[512,448]{0,1:T(8,128)(2,1)}, bf16[512,448]{0,1:T(8,128)(2,1)S(1)}, u32[]{:S(2)}) copy-start(bf16[512,448]{0,1:T(8,128)(2,1)S(1)} %collective-permute-done) | copy-start | bytes 1376260
  42.0 4.5 %collective-permute-start.2 = (bf16[32,35,128]{2,1,0:T(8,128)(2,1)S(1)}, bf16[32,35,128]{2,1,0:T(8,128)(2,1)S(1)}, u32[]{:S(2)}, u32[]{:S(2)}) collective-permute-start(bf16[32,35,128]{2,1,0:T(8,128)(2,1)S(1)} %all-to-all-done), channel_id=1, source_target_pairs={{0,1},{1,0},{2,3},{3,2},{4,5},{5,4},{6,7},{7,6},{8,9},{9,8},{10,11... | collective-permute-start | bytes 860168 | tf_op jit(solution)/shard_map/ppermute | solution.py:40
  43.9 12.1 %collective-permute-start.1 = (bf16[32,35,128]{2,1,0:T(8,128)(2,1)S(1)}, bf16[32,35,128]{2,1,0:T(8,128)(2,1)}, u32[]{:S(2)}, u32[]{:S(2)}) collective-permute-start(bf16[32,35,128]{2,1,0:T(8,128)(2,1)S(1)} %all-to-all-done), channel_id=1, source_target_pairs={{0,16},{16,0},{1,17},{17,1},{2,18},{18,2},{3,19},{19,3},{4,20},{20... | collective-permute-start | bytes 860168 | tf_op jit(solution)/shard_map/ppermute | solution.py:40
  46.5 9.5 %copy-start.6 = (bf16[32,35,128]{2,1,0:T(8,128)(2,1)}, bf16[32,35,128]{2,1,0:T(8,128)(2,1)S(1)}, u32[]{:S(2)}) copy-start(bf16[32,35,128]{2,1,0:T(8,128)(2,1)S(1)} %collective-permute-done.2) | copy-start | bytes 860164
  56.0 5.2 %collective-permute-start.3 = (bf16[32,35,128]{2,1,0:T(8,128)(2,1)}, bf16[32,35,128]{2,1,0:T(8,128)(2,1)}, u32[]{:S(2)}, u32[]{:S(2)}) collective-permute-start(bf16[32,35,128]{2,1,0:T(8,128)(2,1)} %collective-permute-done.1), channel_id=1, source_target_pairs={{0,1},{1,0},{2,3},{3,2},{4,5},{5,4},{6,7},{7,6},{8,9},{9,8},{10,11... | collective-permute-start | bytes 860168 | tf_op jit(solution)/shard_map/ppermute | solution.py:40
  59.6 1.6 copy-start.7
  116.4 4.4 %collective-permute-start.5 = (bf16[320,512]{1,0:T(8,128)(2,1)S(1)}, bf16[320,512]{1,0:T(8,128)(2,1)S(1)}, u32[]{:S(2)}, u32[]{:S(2)}) collective-permute-start(bf16[320,512]{1,0:T(8,128)(2,1)S(1)} %bitcast.40), channel_id=1, source_target_pairs={{0,1},{1,0},{2,3},{3,2},{4,5},{5,4},{6,7},{7,6},{8,9},{9,8},{10,11... | collective-permute-start | bytes 983048 | tf_op jit(solution)/shard_map/ppermute | solution.py:40
  118.3 12.2 %collective-permute-start.4 = (bf16[320,512]{1,0:T(8,128)(2,1)S(1)}, bf16[320,512]{1,0:T(8,128)(2,1)}, u32[]{:S(2)}, u32[]{:S(2)}) collective-permute-start(bf16[320,512]{1,0:T(8,128)(2,1)S(1)} %bitcast.39), channel_id=1, source_target_pairs={{0,1},{1,0},{2,3},{3,2},{4,5},{5,4},{6,7},{7,6},{8,9},{9,8},{10,11... | collective-permute-start | bytes 983048 | tf_op jit(solution)/shard_map/ppermute | solution.py:40
  120.8 2.2 %copy-start.1 = (bf16[640,1024]{1,0:T(8,128)(2,1)S(1)}, bf16[640,1024]{1,0:T(8,128)(2,1)}, u32[]{:S(2)}) copy-start(bf16[640,1024]{1,0:T(8,128)(2,1)} %fusion.3) | copy-start | bytes 3932164
  120.8 2.2 %copy-start.2 = (bf16[640,1024]{1,0:T(8,128)(2,1)S(1)}, bf16[640,1024]{1,0:T(8,128)(2,1)}, u32[]{:S(2)}) copy-start(bf16[640,1024]{1,0:T(8,128)(2,1)} %fusion.2) | copy-start | bytes 3932164
  120.8 2.4 %copy-start.10 = (bf16[1,448,1024]{2,1,0:T(8,128)(2,1)S(1)}, bf16[1,448,1024]{2,1,0:T(8,128)(2,1)}, u32[]{:S(2)}) copy-start(bf16[1,448,1024]{2,1,0:T(8,128)(2,1)} %param.13) | copy-start | bytes 2752516
  127.7 3.9 %copy-start.3 = (bf16[640,1024]{1,0:T(8,128)(2,1)S(1)}, bf16[640,1024]{1,0:T(8,128)(2,1)}, u32[]{:S(2)}) copy-start(bf16[640,1024]{1,0:T(8,128)(2,1)} %fusion.2) | copy-start | bytes 3932164
  127.7 3.9 %copy-start.11 = (bf16[1,448,1024]{2,1,0:T(8,128)(2,1)S(1)}, bf16[1,448,1024]{2,1,0:T(8,128)(2,1)}, u32[]{:S(2)}) copy-start(bf16[1,448,1024]{2,1,0:T(8,128)(2,1)} %param.13) | copy-start | bytes 2752516
  127.7 12.0 %collective-permute-start.6 = (bf16[32,36,128]{2,1,0:T(8,128)(2,1)}, bf16[32,36,128]{2,1,0:T(8,128)(2,1)}, u32[]{:S(2)}, u32[]{:S(2)}) collective-permute-start(bf16[32,36,128]{2,1,0:T(8,128)(2,1)} %fusion.48), channel_id=1, source_target_pairs={{0,16},{16,0},{1,17},{17,1},{2,18},{18,2},{3,19},{19,3},{4,20},{20... | collective-permute-start | bytes 884744 | tf_op jit(solution)/shard_map/ppermute | solution.py:40
  131.6 1.2 copy-start.12
  137.9 22.1 %copy-start.8 = (f32[128,2]{0,1:T(2,128)S(1)}, f32[128,2]{0,1:T(2,128)}, u32[]{:S(2)}) copy-start(f32[128,2]{0,1:T(2,128)} %param.10) | copy-start | bytes 3076

commit v5 on v1

v5 whole, which is shorter than its diff:
```python
import functools

import jax
import jax.numpy as jnp
import numpy as np
from jax import lax
from jax.experimental import pallas as pl
from jax.experimental.pallas import tpu as pltpu
from jax.sharding import Mesh
from jax.sharding import PartitionSpec as P

PAIR = ("z", "yh")
NODE = ("z", "yh", "yl")
LANES = 128
PACKED = 40
BATCH = 8


def swap(value, axis):
    return lax.ppermute(value, axis, ((0, 1), (1, 0)))


def times_transposed(left, right):
    return lax.dot_general(
        left, right, (((1,), (1,)), ((), ())), preferred_element_type=jnp.float32
    )


def over_x(blocks):
    return lax.all_to_all(blocks, "x", split_axis=0, concat_axis=0, tiled=True)


def turned(pair):
    return (pair % lax.axis_size("yh")) // (lax.axis_size("yh") // 2)


def over_group(blocks):
    pairs = lax.axis_size(PAIR)
    groups = [[2 * p + (g ^ turned(p)) for p in range(pairs)] for g in range(2)]
    return lax.all_to_all(
        blocks, NODE, split_axis=0, concat_axis=0, tiled=True, axis_index_groups=groups
    )


def packing(capacity):
    kinds = np.zeros((5, BATCH, capacity, BATCH, PACKED), np.float32)
    for block in range(BATCH):
        for slot in range(capacity):
            for kind in range(3):
                kinds[kind, block, slot, block, capacity * kind + slot] = 1
            kinds[3, block, slot, block, 3 * capacity + slot % (capacity // 2)] = 1
            kinds[4, block, slot, block, 3 * capacity + capacity // 2] = 1
    return kinds.reshape(5, BATCH * capacity, BATCH * PACKED)


def tail_lanes(rank, capacity):
    lane = lax.broadcasted_iota(jnp.int32, (rank.shape[0], LANES), 1)
    return (lane < LANES // 2) == (rank < capacity // 2)


def unpacked(block_ref, pick_ref, rank, capacity):
    span = BATCH * capacity
    features, probs = [], []
    for batch in range(block_ref.shape[0] // BATCH):
        rows = block_ref[batch * BATCH : (batch + 1) * BATCH].astype(jnp.float32)
        rows = rows.reshape(BATCH * PACKED, LANES).astype(jnp.bfloat16)
        picked = jnp.dot(pick_ref[...], rows, preferred_element_type=jnp.float32)
        own = rank[batch * span : (batch + 1) * span]
        tail = jnp.where(tail_lanes(own, capacity), picked[3 * span : 4 * span], 0.0)
        groups = [picked[k * span : (k + 1) * span] for k in range(3)] + [tail]
        features.append(jnp.concatenate(groups, axis=1).astype(jnp.bfloat16))
        if picked.shape[0] > 4 * span:
            lane = lax.broadcasted_iota(jnp.int32, (span, LANES), 1)
            prob = jnp.where(lane == own, picked[4 * span :], 0.0)
            probs.append(jnp.sum(prob, axis=1, keepdims=True))
    return features, probs


def pack(rows, probs, put_ref, rank, out_ref, capacity):
    span = BATCH * capacity
    for batch in range(out_ref.shape[0] // BATCH):
        own = rank[batch * span : (batch + 1) * span]
        part = rows[batch * span : (batch + 1) * span]
        tail = part[:, 3 * LANES :]
        tail = jnp.where(
            tail_lanes(own, capacity), jnp.concatenate([tail, tail], axis=1), 0.0
        )
        groups = [part[:, k * LANES : (k + 1) * LANES] for k in range(3)] + [tail]
        if probs is not None:
            lane = lax.broadcasted_iota(jnp.int32, (span, LANES), 1)
            groups.append(jnp.where(lane == own, probs[batch * span : (batch + 1) * span], 0.0))
        stacked = jnp.concatenate(groups, axis=0).astype(jnp.bfloat16)
        packed = jnp.dot(
            put_ref[:, : stacked.shape[0]], stacked, preferred_element_type=jnp.float32
        )
        out_ref[batch * BATCH : (batch + 1) * BATCH] = packed.reshape(
            BATCH, PACKED, LANES
        ).astype(jnp.bfloat16)


def slot_masks(routes, widen, expert, rank):
    experts = widen.shape[1]
    tokens = routes.shape[1]
    label = lax.broadcasted_iota(jnp.int32, (experts, tokens), 0)
    named = (routes[0:1] == label) | (routes[1:2] == label)
    earlier = lax.broadcasted_iota(jnp.int32, (tokens, tokens), 0) < lax.broadcasted_iota(
        jnp.int32, (tokens, tokens), 1
    )
    ones = jnp.where(named, 1.0, 0.0).astype(jnp.bfloat16)
    before = jnp.dot(
        ones, jnp.where(earlier, 1.0, 0.0).astype(jnp.bfloat16), preferred_element_type=jnp.float32
    )
    before = jnp.dot(widen, before.astype(jnp.bfloat16), preferred_element_type=jnp.float32)
    here = before == rank.astype(jnp.float32)
    return [here & (routes[k : k + 1] == expert) for k in range(2)]


def dispatch_kernel(capacity, routes_ref, grad_ref, widen_ref, expert_ref, rank_ref, put_ref, out_ref):
    first, second = slot_masks(routes_ref[...], widen_ref[...], expert_ref[...], rank_ref[...])
    mask = jnp.where(first | second, 1.0, 0.0).astype(jnp.bfloat16)
    rows = times_transposed(mask, grad_ref[...])
    pack(rows, None, put_ref, rank_ref[...], out_ref, capacity)


def down_kernel(
    capacity, core_ref, own_ref, own_far_ref, pair_ref, pair_far_ref, near_ref, far_ref, pick_ref, rank_ref, out_ref
):
    def stretched(weights):
        return jnp.concatenate([weights, weights[3 * LANES :]], axis=0)

    near, far = stretched(near_ref[...]), stretched(far_ref[...])
    span = BATCH * capacity
    done = 0
    for here_ref, there_ref in ((own_ref, own_far_ref), (pair_ref, pair_far_ref)):
        here, _ = unpacked(here_ref, pick_ref, rank_ref[...], capacity)
        there, _ = unpacked(there_ref, pick_ref, rank_ref[...], capacity)
        here, there = jnp.concatenate(here, axis=0), jnp.concatenate(there, axis=0)
        total = jnp.dot(here, near, preferred_element_type=jnp.float32)
        total = total + jnp.dot(there, far, preferred_element_type=jnp.float32)
        out_ref[done : done + total.shape[0]] = total.astype(jnp.bfloat16)
        done += total.shape[0]


def add_kernel(pieces_ref, out_ref):
    total = pieces_ref[0].astype(jnp.float32)
    for piece in range(1, pieces_ref.shape[0]):
        total = total + pieces_ref[piece].astype(jnp.float32)
    total = total.astype(jnp.bfloat16)
    for piece in range(out_ref.shape[0]):
        out_ref[piece] = total


def route_kernel(
    capacity,
    core_ref,
    near_ref,
    far_ref,
    gate_ref,
    up_ref,
    w_gate_ref,
    w_up_ref,
    put_ref,
    rank_ref,
    out_ref,
    total_ref,
    prob_ref,
):
    step = pl.program_id(0)

    @pl.when(step == 0)
    def _():
        total_ref[...] = jnp.zeros_like(total_ref)
        prob_ref[...] = jnp.zeros_like(prob_ref)

    units = jnp.where(step == 0, near_ref[...].astype(jnp.float32), far_ref[...].astype(jnp.float32))
    gate = gate_ref[...].astype(jnp.float32)
    up = up_ref[...].astype(jnp.float32)
    sigmoid = 1.0 / (1.0 + jnp.exp(-gate))
    upper = units * (gate * sigmoid)
    gates = units * up * sigmoid * (1.0 + gate * (1.0 - sigmoid))
    prob_ref[...] += jnp.sum(upper * up, axis=1, keepdims=True)
    total_ref[...] += times_transposed(
        gates.astype(jnp.bfloat16), w_gate_ref[...]
    ) + times_transposed(upper.astype(jnp.bfloat16), w_up_ref[...])

    @pl.when(step == 1)
    def _():
        pack(total_ref[...], prob_ref[...], put_ref, rank_ref[...], out_ref, capacity)


def sum_kernel(left_ref, right_ref, out_ref):
    out_ref[...] = (
        left_ref[...].astype(jnp.float32) + right_ref[...].astype(jnp.float32)
    ).astype(jnp.bfloat16)


def combine_kernel(
    capacity,
    back_ref,
    routes_ref,
    weight_ref,
    widen_ref,
    expert_ref,
    rank_ref,
    pick_ref,
    out_ref,
    prob_ref,
):
    masks = slot_masks(routes_ref[...], widen_ref[...], expert_ref[...], rank_ref[...])
    weights = jnp.where(masks[0], weight_ref[0:1], 0.0) + jnp.where(masks[1], weight_ref[1:2], 0.0)
    features, probs = unpacked(back_ref, pick_ref, rank_ref[...], capacity)
    wide = jnp.concatenate(features, axis=0)
    half = LANES // 2
    tail = wide[:, 3 * LANES : 3 * LANES + half] + wide[:, 3 * LANES + half :]
    rows = jnp.concatenate([wide[:, : 3 * LANES], tail], axis=1)
    total = jnp.zeros(out_ref.shape, jnp.float32)
    rest = weights
    for _ in range(3):
        part = rest.astype(jnp.bfloat16)
        rest = rest - part.astype(jnp.float32)
        total = total + lax.dot_general(
            rows, part, (((0,), (0,)), ((), ())), preferred_element_type=jnp.float32
        )
    out_ref[...] = total.astype(jnp.bfloat16)
    prob = jnp.concatenate(probs, axis=0)
    for k in range(2):
        prob_ref[k : k + 1] = jnp.sum(
            jnp.where(masks[k], prob, 0.0), axis=0, keepdims=True
        ).astype(jnp.bfloat16)


BIG = pltpu.CompilerParams(vmem_limit_bytes=40 * 1024 * 1024)
FULL = pltpu.CompilerParams(vmem_limit_bytes=60 * 1024 * 1024)


def whole(kernel, out_shape, *args, params=BIG):
    return pl.pallas_call(kernel, out_shape=out_shape, compiler_params=params)(*args)


def shards(grad_out, route_expert, gate_prob, saved_gate, saved_up, w_gate, w_up, w_down):
    experts = lax.axis_size(PAIR)
    chips = lax.axis_size("x")
    slots_all = saved_gate.shape[2]
    slots_side = slots_all // 2
    capacity = slots_side // experts
    feats = grad_out.shape[1]
    tokens = grad_out.shape[0]
    half = saved_gate.shape[1] // 2
    bf16 = jnp.bfloat16
    core = lax.axis_index("c")
    group = lax.axis_index("yl") ^ turned(lax.axis_index("yh"))
    numbers = np.arange(slots_side, dtype=np.int32)[:, None]
    expert_of = jnp.asarray(numbers // capacity)
    rank_of = jnp.asarray(numbers % capacity)
    widen = jnp.asarray(numbers // capacity == np.arange(experts)[None, :], bf16)
    kinds = packing(capacity)
    pick_all = jnp.asarray(kinds.reshape(-1, kinds.shape[2]), bf16)
    pick_rows = pick_all[: 4 * kinds.shape[1]]
    put_all = jnp.asarray(kinds.reshape(-1, kinds.shape[2]).T, bf16)
    block = jax.ShapeDtypeStruct((experts, PACKED, LANES), bf16)

    routes = route_expert.T
    outgoing = whole(
        functools.partial(dispatch_kernel, capacity),
        block,
        routes,
        grad_out.T,
        widen,
        expert_of,
        rank_of,
        put_all[:, : 4 * kinds.shape[1]],
        params=FULL,
    )
    own_rows = over_group(outgoing)

    slot = jnp.arange(slots_all, dtype=jnp.int32)[:, None]
    place = jnp.arange(slots_all, dtype=jnp.int32)[None, :]
    pair = slot // capacity % experts
    member = group ^ turned(pair) ^ (slot // slots_side)
    source = (2 * pair + member) * capacity + slot % capacity
    order = (place == source).astype(bf16)
    gate_rows = times_transposed(order, saved_gate[0]).astype(bf16)
    up_rows = times_transposed(order, saved_up[0]).astype(bf16)
    down = w_down[0].T
    down_far = swap(lax.dynamic_slice_in_dim(down, (1 - core) * half, half, 1), "c")
    own_rows, gate_rows, up_rows, down_far = lax.optimization_barrier(
        (own_rows, gate_rows, up_rows, down_far)
    )

    pair_rows = swap(own_rows, "yl")
    own_far = swap(own_rows, "c")
    pair_rows, own_far = lax.optimization_barrier((pair_rows, own_far))
    pair_far = swap(pair_rows, "c")
    cores = core.astype(jnp.int32).reshape(1)
    block_spec = pl.BlockSpec(block.shape, lambda i, c: (0, 0, 0))
    fixed = lambda i, c: (0, 0)
    on_chip = pl.pallas_call(
        functools.partial(down_kernel, capacity),
        out_shape=jax.ShapeDtypeStruct((slots_all, half), bf16),
        grid_spec=pltpu.PrefetchScalarGridSpec(
            num_scalar_prefetch=1,
            grid=(1,),
            in_specs=[block_spec] * 4
            + [
                pl.BlockSpec((feats, half), lambda i, c: (0, c[0])),
                pl.BlockSpec((feats, half), fixed),
                pl.BlockSpec(pick_rows.shape, fixed),
                pl.BlockSpec(rank_of.shape, fixed),
            ],
            out_specs=pl.BlockSpec((slots_all, half), fixed),
        ),
        compiler_params=BIG,
    )(cores, own_rows, own_far, pair_rows, pair_far, down, down_far, pick_rows, rank_of)
    pieces = over_x(on_chip.reshape(chips, slots_all // chips, half))
    near = over_x(
        whole(add_kernel, jax.ShapeDtypeStruct(pieces.shape, bf16), pieces)
    ).reshape(slots_all, half)
    far = swap(near, "c")

    def routes_of(side, near, far):
        rows_of = lambda i, c: (side, 0)
        hidden_of = lambda i, c: (side, c[0] ^ i)
        weights_of = lambda i, c: (0, c[0] ^ i)
        return pl.pallas_call(
            functools.partial(route_kernel, capacity),
            out_shape=block,
            grid_spec=pltpu.PrefetchScalarGridSpec(
                num_scalar_prefetch=1,
                grid=(2,),
                in_specs=[
                    pl.BlockSpec((slots_side, half), rows_of),
                    pl.BlockSpec((slots_side, half), rows_of),
                    pl.BlockSpec((slots_side, half), hidden_of),
                    pl.BlockSpec((slots_side, half), hidden_of),
                    pl.BlockSpec((feats, half), weights_of),
                    pl.BlockSpec((feats, half), weights_of),
                    pl.BlockSpec(put_all.shape, fixed),
                    pl.BlockSpec(rank_of.shape, fixed),
                ],
                out_specs=block_spec,
                scratch_shapes=[
                    pltpu.VMEM((slots_side, feats), jnp.float32),
                    pltpu.VMEM((slots_side, 1), jnp.float32),
                ],
            ),
            compiler_params=BIG,
        )(cores, near, far, gate_rows, up_rows, w_gate[0], w_up[0], put_all, rank_of)

    pair_routes = routes_of(1, near, far)
    pair_back = swap(pair_routes, "yl")
    far, _ = lax.optimization_barrier((far, pair_routes))
    own_routes = routes_of(0, near, far)
    both = whole(sum_kernel, block, own_routes, pair_back)
    returned = over_group(both)
    grad_in, grad_prob = whole(
        functools.partial(combine_kernel, capacity),
        (
            jax.ShapeDtypeStruct((feats, tokens), bf16),
            jax.ShapeDtypeStruct((2, tokens), bf16),
        ),
        returned,
        routes,
        gate_prob.T,
        widen,
        expert_of,
        rank_of,
        pick_all,
    )
    return (grad_in.T, grad_prob.T)


def solution(mesh):
    nodes, local = mesh.devices.shape
    rows = 8
    fine = Mesh(mesh.devices.reshape(nodes // rows, rows // 2, 2, local // 2, 2), (*NODE, "x", "c"))
    node, feats = NODE, ("x", "c")
    return jax.shard_map(
        shards,
        mesh=fine,
        in_specs=(
            P(node, feats),
            P(node, None),
            P(node, None),
            P(node, None, None),
            P(node, None, None),
            P(node, feats, None),
            P(node, feats, None),
            P(node, None, feats),
        ),
        out_specs=(P(node, feats), P(node, None)),
        check_vma=False,
    )
```

time: 245 us -> 150 us (0.61)
  waiting for transfers between devices: 123 us -> 28.1 us
  starting transfers between devices: 0.12 us -> 34.6 us
  between operations: 13.9 us -> 0.9 us
  blocking collectives: 80.9 us -> 68.2 us
  Pallas kernels: 0 us -> 12.3 us
  other arithmetic: 7.93 us -> 0.04 us
  local copies, waits for them, and re-layouts: 8.84 us -> 2.13 us
  matrix products: 9.76 us -> 3.53 us
    psum x1 -> x0, waiting for transfers between devices: 89.5 us -> none  [shards(): halves = lax.psum(halves, 'x')]
    all_to_all x0 -> x1, starting transfers between devices: none -> 21.7 us  [over_group(): lax.all_to_all(blocks, NODE, split_axis=0, concat_axis=0, tiled=True, axi...]
    all_gather x1 -> x0, waiting for transfers between devices: 20.3 us -> none  [shards(): lax.all_gather(halves, 'c', axis=0, tiled=True).astype(jnp.float32)]
    ppermute x0 -> x6, waiting for transfers between devices: none -> 19.7 us  [swap(): return lax.ppermute(value, axis, ((0, 1), (1, 0)))]
    reduce_scatter x1 -> x0, waiting for transfers between devices: 13.3 us -> none  [shards(): halves = lax.psum_scatter(partial, 'c', scatter_dimension=0, tiled=True)]
    ppermute x0 -> x6, starting transfers between devices: none -> 13 us  [swap(): return lax.ppermute(value, axis, ((0, 1), (1, 0)))]
    all_to_all x2 -> x3, blocking collectives: 80.9 us -> 68.2 us  [the longest x2 49.2 us: over_x(): return lax.all_to_all(blocks, 'x', split_axis=0, concat_axis=0, tiled=True)]
    pallas_call x0 -> x7, Pallas kernels: none -> 12.3 us  [the longest x4 4.93 us: whole(): pl.pallas_call(kernel, out_shape=out_shape, compiler_params=params)(*args)]
  transfers between devices with their start and end apart: 3 -> 7, of which waited for: 3 -> 5; matrix products, arithmetic and copies ran while one was open for 1% -> 3% of each run, Pallas kernels for 0% -> 1%
where the time goes in v5:
time: 150 us
  blocking collectives  68.2 us (45%)
  starting transfers between devices  34.6 us (23%)
  waiting for transfers between devices  28.1 us (19%)
  Pallas kernels  12.3 us (8%)
  matrix products  3.53 us (2%)
  local copies, waits for them, and re-layouts  2.13 us (1%)
    all_to_all x2, blocking collectives, over_x(): return lax.all_to_all(blocks, 'x', split_axis=0, concat_axis=0, tiled=True)  49.2 us
    all_to_all x1, starting transfers between devices, over_group(): lax.all_to_all(blocks, NODE, split_axis=0, concat_axis=0, tiled=True, axi...  21.7 us
    ppermute x6, waiting for transfers between devices, swap(): return lax.ppermute(value, axis, ((0, 1), (1, 0)))  19.7 us
    all_to_all x1, blocking collectives, over_group(): lax.all_to_all(blocks, NODE, split_axis=0, concat_axis=0, tiled=True, axi...  19 us
    ppermute x6, starting transfers between devices, swap(): return lax.ppermute(value, axis, ((0, 1), (1, 0)))  13 us
    all_to_all x1, waiting for transfers between devices, over_group(): lax.all_to_all(blocks, NODE, split_axis=0, concat_axis=0, tiled=True, axi...  8.4 us
    pallas_call x4, Pallas kernels, whole(): pl.pallas_call(kernel, out_shape=out_shape, compiler_params=params)(*args)  4.93 us
    pallas_call x2, Pallas kernels, routes_of(): pl.pallas_call(functools.partial(route_kernel, capacity), out_shape=block...  4.41 us
  transfers between devices with their start and end apart: 7, of which 5 were waited for; matrix products, arithmetic and copies ran while one was open for 3% of the time, Pallas kernels for 1%

profile of v5, /device:TPU:16, one launch (start us, length us, event | category | flops | bytes accessed | tf_op | source)
XLA Modules:
  0.0 149.8 jit_solution(6453250185924433477)
XLA Ops:
  0.7 3.0 %shard_map.140 = bf16[32,40,128]{2,1,0:T(8,128)(2,1)} custom-call(s32[2,128]{1,0:T(2,128)} %bitcast.32, bf16[448,128]{1,0:T(8,128)(2,1)} %bitcast.35, bf16[320,32]{1,0:T(8,128)(2,1)} %constant.108.clone.widen_ref, s32[320,1]{1,0:T(8,128)} %constant.106.clone.expert_ref, s32[320,1]{1,0:T(8,128)} %constant.107.clone.rank_ref, bf16[320,320]{1,0:T(8,128)(2,1)} %constant.116.put_ref), custom_call_target="tpu_custom_call" | custom-call | tf_op jit(solution)/shard_map/pallas_call | solution.py:237
  3.6 21.7 %all-to-all-start = ((bf16[32,40,128]{2,1,0:T(8,128)(2,1)}), bf16[32,40,128]{2,1,0:T(8,128)(2,1)S(1)}, u32[]{:S(2)}, u32[]{:S(2)}) async-start(bf16[32,40,128]{2,1,0:T(8,128)(2,1)} %shard_map.140), calls=%async_computation | async-start | bytes 655360 | tf_op jit(solution)/shard_map/all_to_all | solution.py:40
  25.3 0.8 dynamic-slice_bitcast_fusion
  26.1 1.9 %collective-permute-start = (bf16[448,512]{1,0:T(8,128)(2,1)}, bf16[448,512]{1,0:T(8,128)(2,1)}, u32[]{:S(2)}, u32[]{:S(2)}) collective-permute-start(bf16[448,512]{1,0:T(8,128)(2,1)} %dynamic-slice_bitcast_fusion), channel_id=1, source_target_pairs={{0,1},{1,0},{2,3},{3,2},{4,5},{5,4},{6,7},{7,6},{8,9},{9,8},{10,11... | collective-permute-start | bytes 1376264 | tf_op jit(solution)/shard_map/ppermute | solution.py:20
  28.1 1.2 fusion.3.up_ref
  29.4 2.3 %fusion.2.gate_ref = bf16[640,1024]{1,0:T(8,128)(2,1)} fusion(bf16[1,1024,640]{2,1,0:T(8,128)(2,1)S(1)} %copy-done.14, s32[640]{0:T(1024)S(1)} %fusion.17), kind=kOutput, calls=%fused_computation.3 | convolution fusion | flops 839925760 | bytes 2624000 | tf_op jit(solution)/shard_map/dot_general | solution.py:24
  31.7 8.4 %all-to-all-done.own_ref = bf16[32,40,128]{2,1,0:T(8,128)(2,1)S(1)} async-done(((bf16[32,40,128]{2,1,0:T(8,128)(2,1)}), bf16[32,40,128]{2,1,0:T(8,128)(2,1)S(1)}, u32[]{:S(2)}, u32[]{:S(2)}) %all-to-all-start) | async-done | bytes 327712 | tf_op jit(solution)/shard_map/all_to_all | solution.py:40
  40.1 1.9 %collective-permute-start.2 = (bf16[32,40,128]{2,1,0:T(8,128)(2,1)S(1)}, bf16[32,40,128]{2,1,0:T(8,128)(2,1)S(1)}, u32[]{:S(2)}, u32[]{:S(2)}) collective-permute-start(bf16[32,40,128]{2,1,0:T(8,128)(2,1)S(1)} %all-to-all-done.own_ref), channel_id=1, source_target_pairs={{0,1},{1,0},{2,3},{3,2},{4,5},{5,4},{6,7},{7,6},{8,9},{9,8},{10,11... | collective-permute-start | bytes 983048 | tf_op jit(solution)/shard_map/ppermute | solution.py:20
  42.1 2.6 %collective-permute-start.1 = (bf16[32,40,128]{2,1,0:T(8,128)(2,1)S(1)}, bf16[32,40,128]{2,1,0:T(8,128)(2,1)S(1)}, u32[]{:S(2)}, u32[]{:S(2)}) collective-permute-start(bf16[32,40,128]{2,1,0:T(8,128)(2,1)S(1)} %all-to-all-done.own_ref), channel_id=1, source_target_pairs={{0,16},{16,0},{1,17},{17,1},{2,18},{18,2},{3,19},{19,3},{4,20},{20... | collective-permute-start | bytes 983048 | tf_op jit(solution)/shard_map/ppermute | solution.py:20
  44.7 9.4 %collective-permute-done.1.pair_ref = bf16[32,40,128]{2,1,0:T(8,128)(2,1)S(1)} collective-permute-done((bf16[32,40,128]{2,1,0:T(8,128)(2,1)S(1)}, bf16[32,40,128]{2,1,0:T(8,128)(2,1)S(1)}, u32[]{:S(2)}, u32[]{:S(2)}) %collective-permute-start.1) | collective-permute-done | bytes 327712 | tf_op jit(solution)/shard_map/ppermute | solution.py:20
  54.1 1.9 %collective-permute-start.3 = (bf16[32,40,128]{2,1,0:T(8,128)(2,1)S(1)}, bf16[32,40,128]{2,1,0:T(8,128)(2,1)S(1)}, u32[]{:S(2)}, u32[]{:S(2)}) collective-permute-start(bf16[32,40,128]{2,1,0:T(8,128)(2,1)S(1)} %collective-permute-done.1.pair_ref), channel_id=1, source_target_pairs={{0,1},{1,0},{2,3},{3,2},{4,5},{5,4},{6,7},{7,6},{8,9},{9,8},{10,11... | collective-permute-start | bytes 983048 | tf_op jit(solution)/shard_map/ppermute | solution.py:20
  56.0 1.6 %collective-permute-done.3.pair_far_ref = bf16[32,40,128]{2,1,0:T(8,128)(2,1)S(1)} collective-permute-done((bf16[32,40,128]{2,1,0:T(8,128)(2,1)S(1)}, bf16[32,40,128]{2,1,0:T(8,128)(2,1)S(1)}, u32[]{:S(2)}, u32[]{:S(2)}) %collective-permute-start.3) | collective-permute-done | bytes 327712 | tf_op jit(solution)/shard_map/ppermute | solution.py:20
  57.6 1.2 copy-done.6
  58.8 3.0 %shard_map.141 = bf16[640,512]{1,0:T(8,128)(2,1)S(1)} custom-call(s32[1]{0:T(128)} %bitcast.core_ref, bf16[32,40,128]{2,1,0:T(8,128)(2,1)S(1)} %all-to-all-done.own_ref, bf16[32,40,128]{2,1,0:T(8,128)(2,1)S(1)} %collective-permute-done.2.own_far_ref, bf16[32,40,128]{2,1,0:T(8,128)(2,1)S(1)} %collective-permute-done.1.pair_ref, ...), custom_call_target="tpu_custom_call" | custom-call | tf_op jit(solution)/shard_map/pallas_call | solution.py:297
  61.8 27.3 %all_to_all.20.pieces_ref = bf16[8,80,512]{2,1,0:T(8,128)(2,1)S(1)} all-to-all(bf16[8,80,512]{2,1,0:T(8,128)(2,1)S(1)} %bitcast.30), channel_id=1, replica_groups=mesh['z'=8,'yh'=4,'yl'=2,'x'=8,'c'=2] {'x'}, dimensions={0} | all-to-all | bytes 1310720 | tf_op jit(solution)/shard_map/all_to_all | solution.py:30
  89.2 21.9 %all_to_all.21 = bf16[8,80,512]{2,1,0:T(8,128)(2,1)S(1)} all-to-all(bf16[8,80,512]{2,1,0:T(8,128)(2,1)S(1)} %shard_map.142), channel_id=1, replica_groups=mesh['z'=8,'yh'=4,'yl'=2,'x'=8,'c'=2] {'x'}, dimensions={0} | all-to-all | bytes 1310720 | tf_op jit(solution)/shard_map/all_to_all | solution.py:30
  111.0 1.9 %collective-permute-start.4 = (bf16[640,512]{1,0:T(8,128)(2,1)S(1)}, bf16[640,512]{1,0:T(8,128)(2,1)S(1)}, u32[]{:S(2)}, u32[]{:S(2)}) collective-permute-start(bf16[640,512]{1,0:T(8,128)(2,1)S(1)} %bitcast.23), channel_id=1, source_target_pairs={{0,1},{1,0},{2,3},{3,2},{4,5},{5,4},{6,7},{7,6},{8,9},{9,8},{10,11... | collective-permute-start | bytes 1966088 | tf_op jit(solution)/shard_map/ppermute | solution.py:20
  113.0 2.1 %collective-permute-done.4.far_ref = bf16[640,512]{1,0:T(8,128)(2,1)S(1)} collective-permute-done((bf16[640,512]{1,0:T(8,128)(2,1)S(1)}, bf16[640,512]{1,0:T(8,128)(2,1)S(1)}, u32[]{:S(2)}, u32[]{:S(2)}) %collective-permute-start.4) | collective-permute-done | bytes 655392 | tf_op jit(solution)/shard_map/ppermute | solution.py:20
  115.0 2.2 %shard_map.143 = bf16[32,40,128]{2,1,0:T(8,128)(2,1)S(1)} custom-call(s32[1]{0:T(128)} %bitcast.core_ref, bf16[640,512]{1,0:T(8,128)(2,1)S(1)} %bitcast.24, bf16[640,512]{1,0:T(8,128)(2,1)S(1)} %collective-permute-done.4.far_ref, bf16[640,1024]{1,0:T(8,128)(2,1)S(1)} %copy-done.1, bf16[640,1024]{1,0:T(8,128)(2,1)S(1)} %fusion.3.up_ref, ...), custom_call_target="tpu_custom_call" | custom-call | tf_op jit(solution)/shard_map/pallas_call | solution.py:324
  117.3 2.7 %collective-permute-start.5 = (bf16[32,40,128]{2,1,0:T(8,128)(2,1)S(1)}, bf16[32,40,128]{2,1,0:T(8,128)(2,1)S(1)}, u32[]{:S(2)}, u32[]{:S(2)}) collective-permute-start(bf16[32,40,128]{2,1,0:T(8,128)(2,1)S(1)} %shard_map.143), channel_id=1, source_target_pairs={{0,16},{16,0},{1,17},{17,1},{2,18},{18,2},{3,19},{19,3},{4,20},{20... | collective-permute-start | bytes 983048 | tf_op jit(solution)/shard_map/ppermute | solution.py:20
  120.0 2.2 %shard_map.144.left_ref = bf16[32,40,128]{2,1,0:T(8,128)(2,1)S(1)} custom-call(s32[1]{0:T(128)} %bitcast.core_ref, bf16[640,512]{1,0:T(8,128)(2,1)S(1)} %bitcast.25, bf16[640,512]{1,0:T(8,128)(2,1)S(1)} %collective-permute-done.4.far_ref, bf16[640,1024]{1,0:T(8,128)(2,1)S(1)} %copy-done.1, bf16[640,1024]{1,0:T(8,128)(2,1)S(1)} %fusion.3.up_ref, ...), custom_call_target="tpu_custom_call" | custom-call | tf_op jit(solution)/shard_map/pallas_call | solution.py:324
  122.3 6.6 %collective-permute-done.5.right_ref = bf16[32,40,128]{2,1,0:T(8,128)(2,1)S(1)} collective-permute-done((bf16[32,40,128]{2,1,0:T(8,128)(2,1)S(1)}, bf16[32,40,128]{2,1,0:T(8,128)(2,1)S(1)}, u32[]{:S(2)}, u32[]{:S(2)}) %collective-permute-start.5) | collective-permute-done | bytes 327712 | tf_op jit(solution)/shard_map/ppermute | solution.py:20
  129.0 19.0 %all_to_all.22.back_ref = bf16[32,40,128]{2,1,0:T(8,128)(2,1)S(1)} all-to-all(bf16[32,40,128]{2,1,0:T(8,128)(2,1)S(1)} %shard_map.145), channel_id=1, replica_groups={{0,32,80,112,128,160,208,240,256,288,336,368,384,416,464,496,512,544,59..., dimensions={0} | all-to-all | bytes 655360 | tf_op jit(solution)/shard_map/all_to_all | solution.py:40
  148.0 1.8 %shard_map.146 = (bf16[448,128]{1,0:T(8,128)(2,1)}, bf16[2,128]{1,0:T(2,128)(2,1)}) custom-call(bf16[32,40,128]{2,1,0:T(8,128)(2,1)S(1)} %all_to_all.22.back_ref, s32[2,128]{1,0:T(2,128)S(1)} %bitcast.33, f32[2,128]{1,0:T(2,128)S(1)} %bitcast.34, bf16[320,32]{1,0:T(8,128)(2,1)S(1)} %copy-done.9, s32[320,1]{1,0:T(8,128)S(1)} %copy-done.8, ...), custom_call_target="tpu_custom_call" | custom-call | tf_op jit(solution)/shard_map/pallas_call | solution.py:237
  (34 shorter events, 0.4 us)
Async XLA Ops:
  0.6 27.5 %copy-start = (bf16[1,1024,640]{2,1,0:T(8,128)(2,1)S(1)}, bf16[1,1024,640]{2,1,0:T(8,128)(2,1)}, u32[]{:S(2)}) copy-start(bf16[1,1024,640]{2,1,0:T(8,128)(2,1)} %param.17) | copy-start | bytes 3932164
  0.6 24.7 %copy-start.5 = (bf16[1,1024,448]{1,2,0:T(8,128)(2,1)S(1)}, bf16[1,1024,448]{1,2,0:T(8,128)(2,1)}, u32[]{:S(2)}) copy-start(bf16[1,1024,448]{1,2,0:T(8,128)(2,1)} %param.20) | copy-start | bytes 2752516
  3.6 36.5 %all-to-all-start = ((bf16[32,40,128]{2,1,0:T(8,128)(2,1)}), bf16[32,40,128]{2,1,0:T(8,128)(2,1)S(1)}, u32[]{:S(2)}, u32[]{:S(2)}) async-start(bf16[32,40,128]{2,1,0:T(8,128)(2,1)} %shard_map.140), calls=%async_computation | async-start | bytes 655360 | tf_op jit(solution)/shard_map/all_to_all | solution.py:40
  26.1 5.6 %collective-permute-start = (bf16[448,512]{1,0:T(8,128)(2,1)}, bf16[448,512]{1,0:T(8,128)(2,1)}, u32[]{:S(2)}, u32[]{:S(2)}) collective-permute-start(bf16[448,512]{1,0:T(8,128)(2,1)} %dynamic-slice_bitcast_fusion), channel_id=1, source_target_pairs={{0,1},{1,0},{2,3},{3,2},{4,5},{5,4},{6,7},{7,6},{8,9},{9,8},{10,11... | collective-permute-start | bytes 1376264 | tf_op jit(solution)/shard_map/ppermute | solution.py:20
  28.1 1.3 copy-start.14
  29.4 28.2 %copy-start.2 = (s32[320,1]{1,0:T(8,128)S(1)}, s32[320,1]{1,0:T(8,128)}, u32[]{:S(2)}) copy-start(s32[320,1]{1,0:T(8,128)} %constant.107.clone.rank_ref) | copy-start | bytes 3844
  29.4 28.2 %copy-start.11 = (bf16[320,320]{1,0:T(8,128)(2,1)S(1)}, bf16[320,320]{1,0:T(8,128)(2,1)}, u32[]{:S(2)}) copy-start(bf16[320,320]{1,0:T(8,128)(2,1)} %constant.117.pick_ref) | copy-start | bytes 614404
  40.1 4.6 %collective-permute-start.2 = (bf16[32,40,128]{2,1,0:T(8,128)(2,1)S(1)}, bf16[32,40,128]{2,1,0:T(8,128)(2,1)S(1)}, u32[]{:S(2)}, u32[]{:S(2)}) collective-permute-start(bf16[32,40,128]{2,1,0:T(8,128)(2,1)S(1)} %all-to-all-done.own_ref), channel_id=1, source_target_pairs={{0,1},{1,0},{2,3},{3,2},{4,5},{5,4},{6,7},{7,6},{8,9},{9,8},{10,11... | collective-permute-start | bytes 983048 | tf_op jit(solution)/shard_map/ppermute | solution.py:20
  42.1 12.0 %collective-permute-start.1 = (bf16[32,40,128]{2,1,0:T(8,128)(2,1)S(1)}, bf16[32,40,128]{2,1,0:T(8,128)(2,1)S(1)}, u32[]{:S(2)}, u32[]{:S(2)}) collective-permute-start(bf16[32,40,128]{2,1,0:T(8,128)(2,1)S(1)} %all-to-all-done.own_ref), channel_id=1, source_target_pairs={{0,16},{16,0},{1,17},{17,1},{2,18},{18,2},{3,19},{19,3},{4,20},{20... | collective-permute-start | bytes 983048 | tf_op jit(solution)/shard_map/ppermute | solution.py:20
  54.1 3.5 %collective-permute-start.3 = (bf16[32,40,128]{2,1,0:T(8,128)(2,1)S(1)}, bf16[32,40,128]{2,1,0:T(8,128)(2,1)S(1)}, u32[]{:S(2)}, u32[]{:S(2)}) collective-permute-start(bf16[32,40,128]{2,1,0:T(8,128)(2,1)S(1)} %collective-permute-done.1.pair_ref), channel_id=1, source_target_pairs={{0,1},{1,0},{2,3},{3,2},{4,5},{5,4},{6,7},{7,6},{8,9},{9,8},{10,11... | collective-permute-start | bytes 983048 | tf_op jit(solution)/shard_map/ppermute | solution.py:20
  57.6 1.2 copy-start.6
  61.8 53.3 %copy-start.4 = (bf16[1,448,1024]{2,1,0:T(8,128)(2,1)S(1)}, bf16[1,448,1024]{2,1,0:T(8,128)(2,1)}, u32[]{:S(2)}) copy-start(bf16[1,448,1024]{2,1,0:T(8,128)(2,1)} %param.19) | copy-start | bytes 2752516
  89.1 26.0 %copy-start.1 = (bf16[640,1024]{1,0:T(8,128)(2,1)S(1)}, bf16[640,1024]{1,0:T(8,128)(2,1)}, u32[]{:S(2)}) copy-start(bf16[640,1024]{1,0:T(8,128)(2,1)} %fusion.2.gate_ref) | copy-start | bytes 3932164
  89.1 26.0 %copy-start.3 = (bf16[1,448,1024]{2,1,0:T(8,128)(2,1)S(1)}, bf16[1,448,1024]{2,1,0:T(8,128)(2,1)}, u32[]{:S(2)}) copy-start(bf16[1,448,1024]{2,1,0:T(8,128)(2,1)} %param.18) | copy-start | bytes 2752516
  89.1 26.0 %copy-start.7 = (bf16[320,400]{1,0:T(8,128)(2,1)S(1)}, bf16[320,400]{1,0:T(8,128)(2,1)}, u32[]{:S(2)}) copy-start(bf16[320,400]{1,0:T(8,128)(2,1)} %constant.110.clone.put_ref) | copy-start | bytes 768004
  111.0 4.0 %collective-permute-start.4 = (bf16[640,512]{1,0:T(8,128)(2,1)S(1)}, bf16[640,512]{1,0:T(8,128)(2,1)S(1)}, u32[]{:S(2)}, u32[]{:S(2)}) collective-permute-start(bf16[640,512]{1,0:T(8,128)(2,1)S(1)} %bitcast.23), channel_id=1, source_target_pairs={{0,1},{1,0},{2,3},{3,2},{4,5},{5,4},{6,7},{7,6},{8,9},{9,8},{10,11... | collective-permute-start | bytes 1966088 | tf_op jit(solution)/shard_map/ppermute | solution.py:20
  117.3 11.6 %collective-permute-start.5 = (bf16[32,40,128]{2,1,0:T(8,128)(2,1)S(1)}, bf16[32,40,128]{2,1,0:T(8,128)(2,1)S(1)}, u32[]{:S(2)}, u32[]{:S(2)}) collective-permute-start(bf16[32,40,128]{2,1,0:T(8,128)(2,1)S(1)} %shard_map.143), channel_id=1, source_target_pairs={{0,16},{16,0},{1,17},{17,1},{2,18},{18,2},{3,19},{19,3},{4,20},{20... | collective-permute-start | bytes 983048 | tf_op jit(solution)/shard_map/ppermute | solution.py:20
  122.2 25.8 %copy-start.8 = (s32[320,1]{1,0:T(8,128)S(1)}, s32[320,1]{1,0:T(8,128)}, u32[]{:S(2)}) copy-start(s32[320,1]{1,0:T(8,128)} %constant.106.clone.expert_ref) | copy-start | bytes 3844
  122.2 25.8 %copy-start.9 = (bf16[320,32]{1,0:T(8,128)(2,1)S(1)}, bf16[320,32]{1,0:T(8,128)(2,1)}, u32[]{:S(2)}) copy-start(bf16[320,32]{1,0:T(8,128)(2,1)} %constant.108.clone.widen_ref) | copy-start | bytes 61444
  122.2 25.8 %copy-start.10 = (bf16[400,320]{1,0:T(8,128)(2,1)S(1)}, bf16[400,320]{1,0:T(8,128)(2,1)}, u32[]{:S(2)}) copy-start(bf16[400,320]{1,0:T(8,128)(2,1)} %constant.109.clone.pick_ref) | copy-start | bytes 768004
  122.2 25.8 %copy-start.12 = (s32[128,2]{0,1:T(2,128)S(1)}, s32[128,2]{0,1:T(2,128)}, u32[]{:S(2)}) copy-start(s32[128,2]{0,1:T(2,128)} %param.14) | copy-start | bytes 3076
  122.2 25.8 %copy-start.13 = (f32[128,2]{0,1:T(2,128)S(1)}, f32[128,2]{0,1:T(2,128)}, u32[]{:S(2)}) copy-start(f32[128,2]{0,1:T(2,128)} %param.15) | copy-start | bytes 3076

commit v6 on v5

--- a/solution.py
+++ b/solution.py
@@ -122,23 +122,20 @@
     pack(rows, None, put_ref, rank_ref[...], out_ref, capacity)
 
 
+def stretched(weights):
+    return jnp.concatenate([weights, weights[3 * LANES :]], axis=0)
+
+
 def down_kernel(
-    capacity, core_ref, own_ref, own_far_ref, pair_ref, pair_far_ref, near_ref, far_ref, pick_ref, rank_ref, out_ref
+    capacity, core_ref, block_ref, kept_w_ref, sent_w_ref, pick_ref, rank_ref, *refs
 ):
-    def stretched(weights):
-        return jnp.concatenate([weights, weights[3 * LANES :]], axis=0)
-
-    near, far = stretched(near_ref[...]), stretched(far_ref[...])
-    span = BATCH * capacity
-    done = 0
-    for here_ref, there_ref in ((own_ref, own_far_ref), (pair_ref, pair_far_ref)):
-        here, _ = unpacked(here_ref, pick_ref, rank_ref[...], capacity)
-        there, _ = unpacked(there_ref, pick_ref, rank_ref[...], capacity)
-        here, there = jnp.concatenate(here, axis=0), jnp.concatenate(there, axis=0)
-        total = jnp.dot(here, near, preferred_element_type=jnp.float32)
-        total = total + jnp.dot(there, far, preferred_element_type=jnp.float32)
-        out_ref[done : done + total.shape[0]] = total.astype(jnp.bfloat16)
-        done += total.shape[0]
+    kept_ref, sent_ref = refs[-2:]
+    rows, _ = unpacked(block_ref, pick_ref, rank_ref[...], capacity)
+    rows = jnp.concatenate(rows, axis=0)
+    for weights_ref, out_ref in ((sent_w_ref, sent_ref), (kept_w_ref, kept_ref)):
+        out_ref[...] = jnp.dot(
+            rows, stretched(weights_ref[...]), preferred_element_type=jnp.float32
+        ).astype(jnp.bfloat16)
 
 
 def add_kernel(pieces_ref, out_ref):
@@ -233,8 +230,14 @@
 FULL = pltpu.CompilerParams(vmem_limit_bytes=60 * 1024 * 1024)
 
 
-def whole(kernel, out_shape, *args, params=BIG):
-    return pl.pallas_call(kernel, out_shape=out_shape, compiler_params=params)(*args)
+def cost(products, moved):
+    return pl.CostEstimate(flops=2 * products, bytes_accessed=2 * moved, transcendentals=0)
+
+
+def whole(kernel, out_shape, *args, params=BIG, estimate=None):
+    return pl.pallas_call(
+        kernel, out_shape=out_shape, compiler_params=params, cost_estimate=estimate
+    )(*args)
 
 
 def shards(grad_out, route_expert, gate_prob, saved_gate, saved_up, w_gate, w_up, w_down):
@@ -282,35 +285,40 @@
     gate_rows = times_transposed(order, saved_gate[0]).astype(bf16)
     up_rows = times_transposed(order, saved_up[0]).astype(bf16)
     down = w_down[0].T
-    down_far = swap(lax.dynamic_slice_in_dim(down, (1 - core) * half, half, 1), "c")
-    own_rows, gate_rows, up_rows, down_far = lax.optimization_barrier(
-        (own_rows, gate_rows, up_rows, down_far)
-    )
+    own_rows, gate_rows, up_rows = lax.optimization_barrier((own_rows, gate_rows, up_rows))
 
     pair_rows = swap(own_rows, "yl")
-    own_far = swap(own_rows, "c")
-    pair_rows, own_far = lax.optimization_barrier((pair_rows, own_far))
-    pair_far = swap(pair_rows, "c")
     cores = core.astype(jnp.int32).reshape(1)
     block_spec = pl.BlockSpec(block.shape, lambda i, c: (0, 0, 0))
     fixed = lambda i, c: (0, 0)
-    on_chip = pl.pallas_call(
-        functools.partial(down_kernel, capacity),
-        out_shape=jax.ShapeDtypeStruct((slots_all, half), bf16),
-        grid_spec=pltpu.PrefetchScalarGridSpec(
-            num_scalar_prefetch=1,
-            grid=(1,),
-            in_specs=[block_spec] * 4
-            + [
-                pl.BlockSpec((feats, half), lambda i, c: (0, c[0])),
-                pl.BlockSpec((feats, half), fixed),
-                pl.BlockSpec(pick_rows.shape, fixed),
-                pl.BlockSpec(rank_of.shape, fixed),
-            ],
-            out_specs=pl.BlockSpec((slots_all, half), fixed),
-        ),
-        compiler_params=BIG,
-    )(cores, own_rows, own_far, pair_rows, pair_far, down, down_far, pick_rows, rank_of)
+    product = jax.ShapeDtypeStruct((slots_all, half), bf16)
+
+    def products_of(side, rows, *filled):
+        return pl.pallas_call(
+            functools.partial(down_kernel, capacity),
+            out_shape=(product, product),
+            grid_spec=pltpu.PrefetchScalarGridSpec(
+                num_scalar_prefetch=1,
+                grid=(1,),
+                in_specs=[
+                    block_spec,
+                    pl.BlockSpec((feats, half), lambda i, c: (0, c[0])),
+                    pl.BlockSpec((feats, half), lambda i, c: (0, 1 - c[0])),
+                    pl.BlockSpec(pick_rows.shape, fixed),
+                    pl.BlockSpec(rank_of.shape, fixed),
+                ]
+                + [pl.BlockSpec(memory_space=pl.ANY)] * len(filled),
+                out_specs=[pl.BlockSpec((slots_side, half), lambda i, c: (side, 0))] * 2,
+            ),
+            input_output_aliases={6 + i: i for i in range(len(filled))},
+            compiler_params=BIG,
+            cost_estimate=cost(
+                2 * slots_side * feats * half, 2 * feats * half + 3 * slots_side * half
+            ),
+        )(cores, rows, down, down, pick_rows, rank_of, *filled)
+
+    kept, sent = products_of(1, pair_rows, *products_of(0, own_rows))
+    on_chip = whole(sum_kernel, product, kept, swap(sent, "c"))
     pieces = over_x(on_chip.reshape(chips, slots_all // chips, half))
     near = over_x(
         whole(add_kernel, jax.ShapeDtypeStruct(pieces.shape, bf16), pieces)

time: 150 us -> 145 us (0.967)
  starting transfers between devices: 34.6 us -> 30.3 us
  local copies, waits for them, and re-layouts: 2.13 us -> 0.08 us
    ppermute x6 -> x4, starting transfers between devices: 13 us -> 8.63 us  [swap(): return lax.ppermute(value, axis, ((0, 1), (1, 0)))]
    all_to_all x1, waiting for transfers between devices: 8.4 us -> 10.2 us  [over_group(): lax.all_to_all(blocks, NODE, split_axis=0, concat_axis=0, tiled=True, axi...]
    ppermute x6 -> x4, waiting for transfers between devices: 19.7 us -> 18.2 us  [swap(): return lax.ppermute(value, axis, ((0, 1), (1, 0)))]
    pallas_call x5 -> x7, Pallas kernels: 7.93 us -> 6.63 us  [the longest x5 5.04 us: whole(): pl.pallas_call(kernel, out_shape=out_shape, compiler_params=params, cost_...]
  transfers between devices with their start and end apart: 7 -> 5, of which waited for: 5 -> 5; matrix products, arithmetic and copies ran while one was open for 3% -> 3% of each run, Pallas kernels for 1% -> 2%
where the time goes in v6:
time: 145 us
  blocking collectives  69.3 us (48%)
  starting transfers between devices  30.3 us (21%)
  waiting for transfers between devices  28.4 us (20%)
  Pallas kernels  11 us (8%)
  matrix products  4.59 us (3%)
    all_to_all x2, blocking collectives, over_x(): return lax.all_to_all(blocks, 'x', split_axis=0, concat_axis=0, tiled=True)  49.3 us
    all_to_all x1, starting transfers between devices, over_group(): lax.all_to_all(blocks, NODE, split_axis=0, concat_axis=0, tiled=True, axi...  21.7 us
    all_to_all x1, blocking collectives, over_group(): lax.all_to_all(blocks, NODE, split_axis=0, concat_axis=0, tiled=True, axi...  20 us
    ppermute x4, waiting for transfers between devices, swap(): return lax.ppermute(value, axis, ((0, 1), (1, 0)))  18.2 us
    all_to_all x1, waiting for transfers between devices, over_group(): lax.all_to_all(blocks, NODE, split_axis=0, concat_axis=0, tiled=True, axi...  10.2 us
    ppermute x4, starting transfers between devices, swap(): return lax.ppermute(value, axis, ((0, 1), (1, 0)))  8.63 us
    pallas_call x5, Pallas kernels, whole(): pl.pallas_call(kernel, out_shape=out_shape, compiler_params=params, cost_...  5.04 us
    dot_general x2, matrix products, times_transposed(): lax.dot_general(left, right, (((1,), (1,)), ((), ())), preferred_element_...  4.59 us
  transfers between devices with their start and end apart: 5, of which 5 were waited for; matrix products, arithmetic and copies ran while one was open for 3% of the time, Pallas kernels for 2%

profile of v6, /device:TPU:16, one launch (start us, length us, event | category | flops | bytes accessed | tf_op | source)
XLA Modules:
  0.0 144.7 jit_solution(7696854779895739640)
XLA Ops:
  0.6 2.9 %shard_map.140 = bf16[32,40,128]{2,1,0:T(8,128)(2,1)} custom-call(s32[2,128]{1,0:T(2,128)} %bitcast.31, bf16[448,128]{1,0:T(8,128)(2,1)} %bitcast.34, bf16[320,32]{1,0:T(8,128)(2,1)} %constant.101.clone.widen_ref, s32[320,1]{1,0:T(8,128)} %constant.99.clone.expert_ref, s32[320,1]{1,0:T(8,128)} %constant.100.clone.rank_ref, bf16[320,320]{1,0:T(8,128)(2,1)} %constant.109.put_ref), custom_call_target="tpu_custom_call" | custom-call | tf_op jit(solution)/shard_map/pallas_call | solution.py:238
  3.6 21.7 %all-to-all-start = ((bf16[32,40,128]{2,1,0:T(8,128)(2,1)}), bf16[32,40,128]{2,1,0:T(8,128)(2,1)S(1)}, u32[]{:S(2)}, u32[]{:S(2)}) async-start(bf16[32,40,128]{2,1,0:T(8,128)(2,1)} %shard_map.140), calls=%async_computation | async-start | bytes 655360 | tf_op jit(solution)/shard_map/all_to_all | solution.py:40
  25.3 2.3 %fusion.3.up_ref = bf16[640,1024]{1,0:T(8,128)(2,1)} fusion(bf16[1,1024,640]{2,1,0:T(8,128)(2,1)S(1)} %copy-done, s32[640]{0:T(1024)S(1)} %fusion.17), kind=kOutput, calls=%fused_computation.4 | convolution fusion | flops 839925760 | bytes 2624000 | tf_op jit(solution)/shard_map/dot_general | solution.py:24
  27.6 2.3 %fusion.2.gate_ref = bf16[640,1024]{1,0:T(8,128)(2,1)} fusion(bf16[1,1024,640]{2,1,0:T(8,128)(2,1)S(1)} %copy-done.14, s32[640]{0:T(1024)S(1)} %fusion.17), kind=kOutput, calls=%fused_computation.3 | convolution fusion | flops 839925760 | bytes 2624000 | tf_op jit(solution)/shard_map/dot_general | solution.py:24
  29.9 10.2 %all-to-all-done.block_ref = bf16[32,40,128]{2,1,0:T(8,128)(2,1)S(1)} async-done(((bf16[32,40,128]{2,1,0:T(8,128)(2,1)}), bf16[32,40,128]{2,1,0:T(8,128)(2,1)S(1)}, u32[]{:S(2)}, u32[]{:S(2)}) %all-to-all-start) | async-done | bytes 327712 | tf_op jit(solution)/shard_map/all_to_all | solution.py:40
  40.1 2.6 %collective-permute-start = (bf16[32,40,128]{2,1,0:T(8,128)(2,1)S(1)}, bf16[32,40,128]{2,1,0:T(8,128)(2,1)S(1)}, u32[]{:S(2)}, u32[]{:S(2)}) collective-permute-start(bf16[32,40,128]{2,1,0:T(8,128)(2,1)S(1)} %all-to-all-done.block_ref), channel_id=1, source_target_pairs={{0,16},{16,0},{1,17},{17,1},{2,18},{18,2},{3,19},{19,3},{4,20},{20... | collective-permute-start | bytes 983048 | tf_op jit(solution)/shard_map/ppermute | solution.py:20
  42.7 0.8 shard_map.141
  43.6 6.9 %collective-permute-done.block_ref = bf16[32,40,128]{2,1,0:T(8,128)(2,1)S(1)} collective-permute-done((bf16[32,40,128]{2,1,0:T(8,128)(2,1)S(1)}, bf16[32,40,128]{2,1,0:T(8,128)(2,1)S(1)}, u32[]{:S(2)}, u32[]{:S(2)}) %collective-permute-start) | collective-permute-done | bytes 327712 | tf_op jit(solution)/shard_map/ppermute | solution.py:20
  50.5 0.8 shard_map.142
  51.3 1.9 %collective-permute-start.1 = (bf16[640,512]{1,0:T(8,128)(2,1)S(1)}, bf16[640,512]{1,0:T(8,128)(2,1)S(1)}, u32[]{:S(2)}, u32[]{:S(2)}) collective-permute-start(bf16[640,512]{1,0:T(8,128)(2,1)S(1)} %get-tuple-element.16), channel_id=1, source_target_pairs={{0,1},{1,0},{2,3},{3,2},{4,5},{5,4},{6,7},{7,6},{8,9},{9,8},{10,11... | collective-permute-start | bytes 1966088 | tf_op jit(solution)/shard_map/ppermute | solution.py:20
  53.2 2.1 %collective-permute-done.1.right_ref = bf16[640,512]{1,0:T(8,128)(2,1)S(1)} collective-permute-done((bf16[640,512]{1,0:T(8,128)(2,1)S(1)}, bf16[640,512]{1,0:T(8,128)(2,1)S(1)}, u32[]{:S(2)}, u32[]{:S(2)}) %collective-permute-start.1) | collective-permute-done | bytes 655392 | tf_op jit(solution)/shard_map/ppermute | solution.py:20
  55.3 0.2 shard_map.143
  55.4 27.3 %all_to_all.20.pieces_ref = bf16[8,80,512]{2,1,0:T(8,128)(2,1)S(1)} all-to-all(bf16[8,80,512]{2,1,0:T(8,128)(2,1)S(1)} %bitcast.30), channel_id=1, replica_groups=mesh['z'=8,'yh'=4,'yl'=2,'x'=8,'c'=2] {'x'}, dimensions={0} | all-to-all | bytes 1310720 | tf_op jit(solution)/shard_map/all_to_all | solution.py:30
  82.7 0.1 shard_map.144
  82.8 22.0 %all_to_all.21 = bf16[8,80,512]{2,1,0:T(8,128)(2,1)S(1)} all-to-all(bf16[8,80,512]{2,1,0:T(8,128)(2,1)S(1)} %shard_map.144), channel_id=1, replica_groups=mesh['z'=8,'yh'=4,'yl'=2,'x'=8,'c'=2] {'x'}, dimensions={0} | all-to-all | bytes 1310720 | tf_op jit(solution)/shard_map/all_to_all | solution.py:30
  104.9 1.9 %collective-permute-start.2 = (bf16[640,512]{1,0:T(8,128)(2,1)S(1)}, bf16[640,512]{1,0:T(8,128)(2,1)S(1)}, u32[]{:S(2)}, u32[]{:S(2)}) collective-permute-start(bf16[640,512]{1,0:T(8,128)(2,1)S(1)} %bitcast.23), channel_id=1, source_target_pairs={{0,1},{1,0},{2,3},{3,2},{4,5},{5,4},{6,7},{7,6},{8,9},{9,8},{10,11... | collective-permute-start | bytes 1966088 | tf_op jit(solution)/shard_map/ppermute | solution.py:20
  106.8 2.1 %collective-permute-done.2.far_ref = bf16[640,512]{1,0:T(8,128)(2,1)S(1)} collective-permute-done((bf16[640,512]{1,0:T(8,128)(2,1)S(1)}, bf16[640,512]{1,0:T(8,128)(2,1)S(1)}, u32[]{:S(2)}, u32[]{:S(2)}) %collective-permute-start.2) | collective-permute-done | bytes 655392 | tf_op jit(solution)/shard_map/ppermute | solution.py:20
  108.9 2.2 %shard_map.145 = bf16[32,40,128]{2,1,0:T(8,128)(2,1)S(1)} custom-call(s32[1]{0:T(128)} %bitcast.core_ref, bf16[640,512]{1,0:T(8,128)(2,1)S(1)} %bitcast.24, bf16[640,512]{1,0:T(8,128)(2,1)S(1)} %collective-permute-done.2.far_ref, bf16[640,1024]{1,0:T(8,128)(2,1)S(1)} %copy-done.4, bf16[640,1024]{1,0:T(8,128)(2,1)S(1)} %copy-done.3, ...), custom_call_target="tpu_custom_call" | custom-call | tf_op jit(solution)/shard_map/pallas_call | solution.py:332
  111.1 2.2 %collective-permute-start.3 = (bf16[32,40,128]{2,1,0:T(8,128)(2,1)S(1)}, bf16[32,40,128]{2,1,0:T(8,128)(2,1)S(1)}, u32[]{:S(2)}, u32[]{:S(2)}) collective-permute-start(bf16[32,40,128]{2,1,0:T(8,128)(2,1)S(1)} %shard_map.145), channel_id=1, source_target_pairs={{0,16},{16,0},{1,17},{17,1},{2,18},{18,2},{3,19},{19,3},{4,20},{20... | collective-permute-start | bytes 983048 | tf_op jit(solution)/shard_map/ppermute | solution.py:20
  113.3 2.2 %shard_map.146.left_ref = bf16[32,40,128]{2,1,0:T(8,128)(2,1)S(1)} custom-call(s32[1]{0:T(128)} %bitcast.core_ref, bf16[640,512]{1,0:T(8,128)(2,1)S(1)} %bitcast.25, bf16[640,512]{1,0:T(8,128)(2,1)S(1)} %collective-permute-done.2.far_ref, bf16[640,1024]{1,0:T(8,128)(2,1)S(1)} %copy-done.4, bf16[640,1024]{1,0:T(8,128)(2,1)S(1)} %copy-done.3, ...), custom_call_target="tpu_custom_call" | custom-call | tf_op jit(solution)/shard_map/pallas_call | solution.py:332
  115.6 7.2 %collective-permute-done.3.right_ref = bf16[32,40,128]{2,1,0:T(8,128)(2,1)S(1)} collective-permute-done((bf16[32,40,128]{2,1,0:T(8,128)(2,1)S(1)}, bf16[32,40,128]{2,1,0:T(8,128)(2,1)S(1)}, u32[]{:S(2)}, u32[]{:S(2)}) %collective-permute-start.3) | collective-permute-done | bytes 327712 | tf_op jit(solution)/shard_map/ppermute | solution.py:20
  122.7 0.1 shard_map.147
  122.8 20.0 %all_to_all.22.back_ref = bf16[32,40,128]{2,1,0:T(8,128)(2,1)S(1)} all-to-all(bf16[32,40,128]{2,1,0:T(8,128)(2,1)S(1)} %shard_map.147), channel_id=1, replica_groups={{0,32,80,112,128,160,208,240,256,288,336,368,384,416,464,496,512,544,59..., dimensions={0} | all-to-all | bytes 655360 | tf_op jit(solution)/shard_map/all_to_all | solution.py:40
  142.9 1.8 %shard_map.148 = (bf16[448,128]{1,0:T(8,128)(2,1)}, bf16[2,128]{1,0:T(2,128)(2,1)}) custom-call(bf16[32,40,128]{2,1,0:T(8,128)(2,1)S(1)} %all_to_all.22.back_ref, s32[2,128]{1,0:T(2,128)S(1)} %bitcast.32, f32[2,128]{1,0:T(2,128)S(1)} %bitcast.33, bf16[320,32]{1,0:T(8,128)(2,1)S(1)} %copy-done.10, s32[320,1]{1,0:T(8,128)S(1)} %copy-done.9, ...), custom_call_target="tpu_custom_call" | custom-call | tf_op jit(solution)/shard_map/pallas_call | solution.py:238
  (31 shorter events, 0.1 us)
Async XLA Ops:
  0.6 24.7 %copy-start = (bf16[1,1024,640]{2,1,0:T(8,128)(2,1)S(1)}, bf16[1,1024,640]{2,1,0:T(8,128)(2,1)}, u32[]{:S(2)}) copy-start(bf16[1,1024,640]{2,1,0:T(8,128)(2,1)} %param.17) | copy-start | bytes 3932164
  3.6 36.5 %all-to-all-start = ((bf16[32,40,128]{2,1,0:T(8,128)(2,1)}), bf16[32,40,128]{2,1,0:T(8,128)(2,1)S(1)}, u32[]{:S(2)}, u32[]{:S(2)}) async-start(bf16[32,40,128]{2,1,0:T(8,128)(2,1)} %shard_map.140), calls=%async_computation | async-start | bytes 655360 | tf_op jit(solution)/shard_map/all_to_all | solution.py:40
  25.3 2.3 %copy-start.14 = (bf16[1,1024,640]{2,1,0:T(8,128)(2,1)S(1)}, bf16[1,1024,640]{2,1,0:T(8,128)(2,1)}, u32[]{:S(2)}) copy-start(bf16[1,1024,640]{2,1,0:T(8,128)(2,1)} %param.16) | copy-start | bytes 3932164
  27.6 15.1 %copy-start.1 = (bf16[1,1024,448]{1,2,0:T(8,128)(2,1)S(1)}, bf16[1,1024,448]{1,2,0:T(8,128)(2,1)}, u32[]{:S(2)}) copy-start(bf16[1,1024,448]{1,2,0:T(8,128)(2,1)} %param.20) | copy-start | bytes 2752516
  27.6 15.1 %copy-start.2 = (s32[320,1]{1,0:T(8,128)S(1)}, s32[320,1]{1,0:T(8,128)}, u32[]{:S(2)}) copy-start(s32[320,1]{1,0:T(8,128)} %constant.100.clone.rank_ref) | copy-start | bytes 3844
  27.6 15.1 %copy-start.8 = (bf16[320,320]{1,0:T(8,128)(2,1)S(1)}, bf16[320,320]{1,0:T(8,128)(2,1)}, u32[]{:S(2)}) copy-start(bf16[320,320]{1,0:T(8,128)(2,1)} %constant.110.pick_ref) | copy-start | bytes 614404
  40.1 10.4 %collective-permute-start = (bf16[32,40,128]{2,1,0:T(8,128)(2,1)S(1)}, bf16[32,40,128]{2,1,0:T(8,128)(2,1)S(1)}, u32[]{:S(2)}, u32[]{:S(2)}) collective-permute-start(bf16[32,40,128]{2,1,0:T(8,128)(2,1)S(1)} %all-to-all-done.block_ref), channel_id=1, source_target_pairs={{0,16},{16,0},{1,17},{17,1},{2,18},{18,2},{3,19},{19,3},{4,20},{20... | collective-permute-start | bytes 983048 | tf_op jit(solution)/shard_map/ppermute | solution.py:20
  51.3 4.0 %collective-permute-start.1 = (bf16[640,512]{1,0:T(8,128)(2,1)S(1)}, bf16[640,512]{1,0:T(8,128)(2,1)S(1)}, u32[]{:S(2)}, u32[]{:S(2)}) collective-permute-start(bf16[640,512]{1,0:T(8,128)(2,1)S(1)} %get-tuple-element.16), channel_id=1, source_target_pairs={{0,1},{1,0},{2,3},{3,2},{4,5},{5,4},{6,7},{7,6},{8,9},{9,8},{10,11... | collective-permute-start | bytes 1966088 | tf_op jit(solution)/shard_map/ppermute | solution.py:20
  55.3 53.6 %copy-start.6 = (bf16[1,448,1024]{2,1,0:T(8,128)(2,1)S(1)}, bf16[1,448,1024]{2,1,0:T(8,128)(2,1)}, u32[]{:S(2)}) copy-start(bf16[1,448,1024]{2,1,0:T(8,128)(2,1)} %param.19) | copy-start | bytes 2752516
  55.4 53.4 %copy-start.5 = (bf16[1,448,1024]{2,1,0:T(8,128)(2,1)S(1)}, bf16[1,448,1024]{2,1,0:T(8,128)(2,1)}, u32[]{:S(2)}) copy-start(bf16[1,448,1024]{2,1,0:T(8,128)(2,1)} %param.18) | copy-start | bytes 2752516
  55.4 53.4 %copy-start.7 = (bf16[320,400]{1,0:T(8,128)(2,1)S(1)}, bf16[320,400]{1,0:T(8,128)(2,1)}, u32[]{:S(2)}) copy-start(bf16[320,400]{1,0:T(8,128)(2,1)} %constant.103.clone.put_ref) | copy-start | bytes 768004
  82.7 26.1 %copy-start.3 = (bf16[640,1024]{1,0:T(8,128)(2,1)S(1)}, bf16[640,1024]{1,0:T(8,128)(2,1)}, u32[]{:S(2)}) copy-start(bf16[640,1024]{1,0:T(8,128)(2,1)} %fusion.3.up_ref) | copy-start | bytes 3932164
  82.7 26.1 %copy-start.4 = (bf16[640,1024]{1,0:T(8,128)(2,1)S(1)}, bf16[640,1024]{1,0:T(8,128)(2,1)}, u32[]{:S(2)}) copy-start(bf16[640,1024]{1,0:T(8,128)(2,1)} %fusion.2.gate_ref) | copy-start | bytes 3932164
  104.9 4.0 %collective-permute-start.2 = (bf16[640,512]{1,0:T(8,128)(2,1)S(1)}, bf16[640,512]{1,0:T(8,128)(2,1)S(1)}, u32[]{:S(2)}, u32[]{:S(2)}) collective-permute-start(bf16[640,512]{1,0:T(8,128)(2,1)S(1)} %bitcast.23), channel_id=1, source_target_pairs={{0,1},{1,0},{2,3},{3,2},{4,5},{5,4},{6,7},{7,6},{8,9},{9,8},{10,11... | collective-permute-start | bytes 1966088 | tf_op jit(solution)/shard_map/ppermute | solution.py:20
  111.1 11.6 %collective-permute-start.3 = (bf16[32,40,128]{2,1,0:T(8,128)(2,1)S(1)}, bf16[32,40,128]{2,1,0:T(8,128)(2,1)S(1)}, u32[]{:S(2)}, u32[]{:S(2)}) collective-permute-start(bf16[32,40,128]{2,1,0:T(8,128)(2,1)S(1)} %shard_map.145), channel_id=1, source_target_pairs={{0,16},{16,0},{1,17},{17,1},{2,18},{18,2},{3,19},{19,3},{4,20},{20... | collective-permute-start | bytes 983048 | tf_op jit(solution)/shard_map/ppermute | solution.py:20
  115.5 27.3 %copy-start.9 = (s32[320,1]{1,0:T(8,128)S(1)}, s32[320,1]{1,0:T(8,128)}, u32[]{:S(2)}) copy-start(s32[320,1]{1,0:T(8,128)} %constant.99.clone.expert_ref) | copy-start | bytes 3844
  115.5 27.3 %copy-start.10 = (bf16[320,32]{1,0:T(8,128)(2,1)S(1)}, bf16[320,32]{1,0:T(8,128)(2,1)}, u32[]{:S(2)}) copy-start(bf16[320,32]{1,0:T(8,128)(2,1)} %constant.101.clone.widen_ref) | copy-start | bytes 61444
  115.5 27.3 %copy-start.11 = (bf16[400,320]{1,0:T(8,128)(2,1)S(1)}, bf16[400,320]{1,0:T(8,128)(2,1)}, u32[]{:S(2)}) copy-start(bf16[400,320]{1,0:T(8,128)(2,1)} %constant.102.clone.pick_ref) | copy-start | bytes 768004
  115.5 27.3 %copy-start.12 = (s32[128,2]{0,1:T(2,128)S(1)}, s32[128,2]{0,1:T(2,128)}, u32[]{:S(2)}) copy-start(s32[128,2]{0,1:T(2,128)} %param.14) | copy-start | bytes 3076
  115.5 27.3 %copy-start.13 = (f32[128,2]{0,1:T(2,128)S(1)}, f32[128,2]{0,1:T(2,128)}, u32[]{:S(2)}) copy-start(f32[128,2]{0,1:T(2,128)} %param.15) | copy-start | bytes 3076

commit v7 on v6

--- a/solution.py
+++ b/solution.py
@@ -133,18 +133,18 @@
     rows, _ = unpacked(block_ref, pick_ref, rank_ref[...], capacity)
     rows = jnp.concatenate(rows, axis=0)
     for weights_ref, out_ref in ((sent_w_ref, sent_ref), (kept_w_ref, kept_ref)):
-        out_ref[...] = jnp.dot(
-            rows, stretched(weights_ref[...]), preferred_element_type=jnp.float32
-        ).astype(jnp.bfloat16)
-
-
-def add_kernel(pieces_ref, out_ref):
+        total = jnp.dot(rows, stretched(weights_ref[...]), preferred_element_type=jnp.float32)
+        out_ref[...] = total.reshape(out_ref.shape).astype(jnp.bfloat16)
+
+
+def add_kernel(pieces_ref, own_ref, pair_ref):
     total = pieces_ref[0].astype(jnp.float32)
     for piece in range(1, pieces_ref.shape[0]):
         total = total + pieces_ref[piece].astype(jnp.float32)
     total = total.astype(jnp.bfloat16)
-    for piece in range(out_ref.shape[0]):
-        out_ref[piece] = total
+    for piece in range(pieces_ref.shape[0]):
+        own_ref[piece] = total[0]
+        pair_ref[piece] = total[1]
 
 
 def route_kernel(
@@ -291,7 +291,8 @@
     cores = core.astype(jnp.int32).reshape(1)
     block_spec = pl.BlockSpec(block.shape, lambda i, c: (0, 0, 0))
     fixed = lambda i, c: (0, 0)
-    product = jax.ShapeDtypeStruct((slots_all, half), bf16)
+    share = slots_side // chips
+    product = jax.ShapeDtypeStruct((chips, 2, share, half), bf16)
 
     def products_of(side, rows, *filled):
         return pl.pallas_call(
@@ -308,7 +309,7 @@
                     pl.BlockSpec(rank_of.shape, fixed),
                 ]
                 + [pl.BlockSpec(memory_space=pl.ANY)] * len(filled),
-                out_specs=[pl.BlockSpec((slots_side, half), lambda i, c: (side, 0))] * 2,
+                out_specs=[pl.BlockSpec((chips, 1, share, half), lambda i, c: (0, side, 0, 0))] * 2,
             ),
             input_output_aliases={6 + i: i for i in range(len(filled))},
             compiler_params=BIG,
@@ -319,14 +320,18 @@
 
     kept, sent = products_of(1, pair_rows, *products_of(0, own_rows))
     on_chip = whole(sum_kernel, product, kept, swap(sent, "c"))
-    pieces = over_x(on_chip.reshape(chips, slots_all // chips, half))
-    near = over_x(
-        whole(add_kernel, jax.ShapeDtypeStruct(pieces.shape, bf16), pieces)
-    ).reshape(slots_all, half)
-    far = swap(near, "c")
-
-    def routes_of(side, near, far):
-        rows_of = lambda i, c: (side, 0)
+    own_piece, pair_piece = whole(
+        add_kernel,
+        (jax.ShapeDtypeStruct((chips, share, half), bf16),) * 2,
+        over_x(on_chip),
+    )
+    pair_near = over_x(pair_piece)
+    own_piece, pair_near = lax.optimization_barrier((own_piece, pair_near))
+    own_near = over_x(own_piece)
+
+    def routes_of(side, near):
+        far = swap(near, "c")
+        near, far = (value.reshape(slots_side, half) for value in (near, far))
         hidden_of = lambda i, c: (side, c[0] ^ i)
         weights_of = lambda i, c: (0, c[0] ^ i)
         return pl.pallas_call(
@@ -336,8 +341,8 @@
                 num_scalar_prefetch=1,
                 grid=(2,),
                 in_specs=[
-                    pl.BlockSpec((slots_side, half), rows_of),
-                    pl.BlockSpec((slots_side, half), rows_of),
+                    pl.BlockSpec((slots_side, half), fixed),
+                    pl.BlockSpec((slots_side, half), fixed),
                     pl.BlockSpec((slots_side, half), hidden_of),
                     pl.BlockSpec((slots_side, half), hidden_of),
                     pl.BlockSpec((feats, half), weights_of),
@@ -352,12 +357,14 @@
                 ],
             ),
             compiler_params=BIG,
+            cost_estimate=cost(
+                4 * slots_side * feats * half, 4 * feats * half + 8 * slots_side * half
+            ),
         )(cores, near, far, gate_rows, up_rows, w_gate[0], w_up[0], put_all, rank_of)
 
-    pair_routes = routes_of(1, near, far)
-    pair_back = swap(pair_routes, "yl")
-    far, _ = lax.optimization_barrier((far, pair_routes))
-    own_routes = routes_of(0, near, far)
+    pair_back = swap(routes_of(1, pair_near), "yl")
+    own_near, pair_back = lax.optimization_barrier((own_near, pair_back))
+    own_routes = routes_of(0, own_near)
     both = whole(sum_kernel, block, own_routes, pair_back)
     returned = over_group(both)
     grad_in, grad_prob = whole(

time: 145 us -> 159 us (1.097)
  local copies, waits for them, and re-layouts: 0.08 us -> 7.27 us
  starting transfers between devices: 30.3 us -> 36.3 us
  blocking collectives: 69.3 us -> 63.5 us
  Pallas kernels: 11 us -> 14.5 us
  waiting for transfers between devices: 28.4 us -> 31 us
    unnamed x30 -> x38, local copies, waits for them, and re-layouts: 0.08 us -> 7.27 us
    all_to_all x2, blocking collectives: 49.3 us -> 42.8 us  [over_x(): return lax.all_to_all(blocks, 'x', split_axis=0, concat_axis=0, tiled=True)]
    all_to_all x0 -> x1, waiting for transfers between devices: none -> 4.57 us  [over_x(): return lax.all_to_all(blocks, 'x', split_axis=0, concat_axis=0, tiled=True)]
    all_to_all x0 -> x1, starting transfers between devices: none -> 4.08 us  [over_x(): return lax.all_to_all(blocks, 'x', split_axis=0, concat_axis=0, tiled=True)]
    pallas_call x2, Pallas kernels: 4.4 us -> 6.86 us  [routes_of(): pl.pallas_call(functools.partial(route_kernel, capacity), out_shape=block...]
    ppermute x4 -> x5, starting transfers between devices: 8.63 us -> 10.5 us  [swap(): return lax.ppermute(value, axis, ((0, 1), (1, 0)))]
    ppermute x4 -> x5, waiting for transfers between devices: 18.2 us -> 16.3 us  [swap(): return lax.ppermute(value, axis, ((0, 1), (1, 0)))]
  transfers between devices with their start and end apart: 5 -> 7, of which waited for: 5 -> 6; matrix products, arithmetic and copies ran while one was open for 3% -> 3% of each run, Pallas kernels for 2% -> 3%
where the time goes in v7:
time: 159 us; the launch traced here: 158 us
  blocking collectives  63.5 us (40%)
  starting transfers between devices  36.3 us (23%)
  waiting for transfers between devices  31 us (19%)
  Pallas kernels  14.5 us (9%)
  local copies, waits for them, and re-layouts  7.27 us (5%)
  matrix products  4.62 us (3%)
    all_to_all x2, blocking collectives, over_x(): return lax.all_to_all(blocks, 'x', split_axis=0, concat_axis=0, tiled=True)  42.8 us
    all_to_all x1, starting transfers between devices, over_group(): lax.all_to_all(blocks, NODE, split_axis=0, concat_axis=0, tiled=True, axi...  21.7 us
    all_to_all x1, blocking collectives, over_group(): lax.all_to_all(blocks, NODE, split_axis=0, concat_axis=0, tiled=True, axi...  20.6 us
    ppermute x5, waiting for transfers between devices, swap(): return lax.ppermute(value, axis, ((0, 1), (1, 0)))  16.3 us
    ppermute x5, starting transfers between devices, swap(): return lax.ppermute(value, axis, ((0, 1), (1, 0)))  10.5 us
    all_to_all x1, waiting for transfers between devices, over_group(): lax.all_to_all(blocks, NODE, split_axis=0, concat_axis=0, tiled=True, axi...  10.1 us
    unnamed x38, local copies, waits for them, and re-layouts  7.27 us
    pallas_call x2, Pallas kernels, routes_of(): pl.pallas_call(functools.partial(route_kernel, capacity), out_shape=block...  6.86 us
  transfers between devices with their start and end apart: 7, of which 6 were waited for; matrix products, arithmetic and copies ran while one was open for 3% of the time, Pallas kernels for 3%

profile of v7, /device:TPU:16, one launch (start us, length us, event | category | flops | bytes accessed | tf_op | source)
XLA Modules:
  0.0 158.2 jit_solution(18276428822074263589)
XLA Ops:
  0.6 2.9 %shard_map.140 = bf16[32,40,128]{2,1,0:T(8,128)(2,1)} custom-call(s32[2,128]{1,0:T(2,128)} %bitcast.30, bf16[448,128]{1,0:T(8,128)(2,1)} %bitcast.33, bf16[320,32]{1,0:T(8,128)(2,1)} %constant.101.clone.widen_ref, s32[320,1]{1,0:T(8,128)} %constant.99.clone.expert_ref, s32[320,1]{1,0:T(8,128)} %constant.100.clone.rank_ref, bf16[320,320]{1,0:T(8,128)(2,1)} %constant.109.put_ref), custom_call_target="tpu_custom_call" | custom-call | tf_op jit(solution)/shard_map/pallas_call | solution.py:238
  3.6 21.7 %all-to-all-start = ((bf16[32,40,128]{2,1,0:T(8,128)(2,1)}), bf16[32,40,128]{2,1,0:T(8,128)(2,1)S(1)}, u32[]{:S(2)}, u32[]{:S(2)}) async-start(bf16[32,40,128]{2,1,0:T(8,128)(2,1)} %shard_map.140), calls=%async_computation | async-start | bytes 655360 | tf_op jit(solution)/shard_map/all_to_all | solution.py:40
  25.3 2.3 %fusion.3.up_ref = bf16[640,1024]{1,0:T(8,128)(2,1)} fusion(bf16[1,1024,640]{2,1,0:T(8,128)(2,1)S(1)} %copy-done, s32[640]{0:T(1024)S(1)} %fusion.17), kind=kOutput, calls=%fused_computation.4 | convolution fusion | flops 839925760 | bytes 2624000 | tf_op jit(solution)/shard_map/dot_general | solution.py:24
  27.6 2.3 %fusion.2.gate_ref = bf16[640,1024]{1,0:T(8,128)(2,1)} fusion(bf16[1,1024,640]{2,1,0:T(8,128)(2,1)S(1)} %copy-done.18, s32[640]{0:T(1024)S(1)} %fusion.17), kind=kOutput, calls=%fused_computation.3 | convolution fusion | flops 839925760 | bytes 2624000 | tf_op jit(solution)/shard_map/dot_general | solution.py:24
  30.0 10.1 %all-to-all-done.block_ref = bf16[32,40,128]{2,1,0:T(8,128)(2,1)S(1)} async-done(((bf16[32,40,128]{2,1,0:T(8,128)(2,1)}), bf16[32,40,128]{2,1,0:T(8,128)(2,1)S(1)}, u32[]{:S(2)}, u32[]{:S(2)}) %all-to-all-start) | async-done | bytes 327712 | tf_op jit(solution)/shard_map/all_to_all | solution.py:40
  40.1 2.6 %collective-permute-start = (bf16[32,40,128]{2,1,0:T(8,128)(2,1)S(1)}, bf16[32,40,128]{2,1,0:T(8,128)(2,1)S(1)}, u32[]{:S(2)}, u32[]{:S(2)}) collective-permute-start(bf16[32,40,128]{2,1,0:T(8,128)(2,1)S(1)} %all-to-all-done.block_ref), channel_id=1, source_target_pairs={{0,16},{16,0},{1,17},{17,1},{2,18},{18,2},{3,19},{19,3},{4,20},{20... | collective-permute-start | bytes 983048 | tf_op jit(solution)/shard_map/ppermute | solution.py:20
  43.5 6.9 %collective-permute-done.block_ref = bf16[32,40,128]{2,1,0:T(8,128)(2,1)S(1)} collective-permute-done((bf16[32,40,128]{2,1,0:T(8,128)(2,1)S(1)}, bf16[32,40,128]{2,1,0:T(8,128)(2,1)S(1)}, u32[]{:S(2)}, u32[]{:S(2)}) %collective-permute-start) | collective-permute-done | bytes 327712 | tf_op jit(solution)/shard_map/ppermute | solution.py:20
  51.3 1.9 %collective-permute-start.1 = (bf16[8,2,40,512]{3,2,1,0:T(8,128)(2,1)S(1)}, bf16[8,2,40,512]{3,2,1,0:T(8,128)(2,1)S(1)}, u32[]{:S(2)}, u32[]{:S(2)}) collective-permute-start(bf16[8,2,40,512]{3,2,1,0:T(8,128)(2,1)S(1)} %get-tuple-element.21), channel_id=1, source_target_pairs={{0,1},{1,0},{2,3},{3,2},{4,5},{5,4},{6,7},{7,6},{8,9},{9,8},{10,11... | collective-permute-start | bytes 1966088 | tf_op jit(solution)/shard_map/ppermute | solution.py:20
  53.2 2.1 %collective-permute-done.1.right_ref = bf16[8,2,40,512]{3,2,1,0:T(8,128)(2,1)S(1)} collective-permute-done((bf16[8,2,40,512]{3,2,1,0:T(8,128)(2,1)S(1)}, bf16[8,2,40,512]{3,2,1,0:T(8,128)(2,1)S(1)}, u32[]{:S(2)}, u32[]{:S(2)}) %collective-permute-start.1) | collective-permute-done | bytes 655392 | tf_op jit(solution)/shard_map/ppermute | solution.py:20
  55.4 27.2 %all_to_all.25.pieces_ref = bf16[8,2,40,512]{3,2,1,0:T(8,128)(2,1)S(1)} all-to-all(bf16[8,2,40,512]{3,2,1,0:T(8,128)(2,1)S(1)} %shard_map.143), channel_id=1, replica_groups=mesh['z'=8,'yh'=4,'yl'=2,'x'=8,'c'=2] {'x'}, dimensions={0} | all-to-all | bytes 1310720 | tf_op jit(solution)/shard_map/all_to_all | solution.py:30
  82.7 15.7 %all_to_all.26 = bf16[8,40,512]{2,1,0:T(8,128)(2,1)} all-to-all(bf16[8,40,512]{2,1,0:T(8,128)(2,1)S(1)} %get-tuple-element.23), channel_id=1, replica_groups=mesh['z'=8,'yh'=4,'yl'=2,'x'=8,'c'=2] {'x'}, dimensions={0} | all-to-all | bytes 655360 | tf_op jit(solution)/shard_map/all_to_all | solution.py:30
  98.4 1.9 %collective-permute-start.2 = (bf16[8,40,512]{2,1,0:T(8,128)(2,1)}, bf16[8,40,512]{2,1,0:T(8,128)(2,1)}, u32[]{:S(2)}, u32[]{:S(2)}) collective-permute-start(bf16[8,40,512]{2,1,0:T(8,128)(2,1)} %all_to_all.26), channel_id=1, source_target_pairs={{0,1},{1,0},{2,3},{3,2},{4,5},{5,4},{6,7},{7,6},{8,9},{9,8},{10,11... | collective-permute-start | bytes 983048 | tf_op jit(solution)/shard_map/ppermute | solution.py:20
  100.3 4.1 %all-to-all-start.3 = ((bf16[8,40,512]{2,1,0:T(8,128)(2,1)}), bf16[8,40,512]{2,1,0:T(8,128)(2,1)}, u32[]{:S(2)}, u32[]{:S(2)}) async-start(bf16[8,40,512]{2,1,0:T(8,128)(2,1)} %copy-done.14), calls=%async_computation.3 | async-start | bytes 655360 | tf_op jit(solution)/shard_map/all_to_all | solution.py:30
  105.7 1.3 copy-done.5
  108.0 3.8 %shard_map.145 = bf16[32,40,128]{2,1,0:T(8,128)(2,1)} custom-call(s32[1]{0:T(128)} %bitcast.core_ref, bf16[320,512]{1,0:T(8,128)(2,1)} %bitcast.8.near_ref, bf16[320,512]{1,0:T(8,128)(2,1)} %bitcast.9.far_ref, bf16[640,1024]{1,0:T(8,128)(2,1)S(1)} %copy-done.5, bf16[640,1024]{1,0:T(8,128)(2,1)S(1)} %copy-done.3, bf16[448,1024]{1,0:T(8,128)(2,1)S(1)} %bitcast.25, ...), custom_call_target="tpu_custom_call" | custom-call | flops 587202560 | bytes 4456448 | tf_op jit(solution)/shard_map/pallas_call | solution.py:337
  111.8 2.2 %collective-permute-start.3 = (bf16[32,40,128]{2,1,0:T(8,128)(2,1)}, bf16[32,40,128]{2,1,0:T(8,128)(2,1)}, u32[]{:S(2)}, u32[]{:S(2)}) collective-permute-start(bf16[32,40,128]{2,1,0:T(8,128)(2,1)} %shard_map.145), channel_id=1, source_target_pairs={{0,16},{16,0},{1,17},{17,1},{2,18},{18,2},{3,19},{19,3},{4,20},{20... | collective-permute-start | bytes 983048 | tf_op jit(solution)/shard_map/ppermute | solution.py:20
  114.0 4.6 %all-to-all-done.3 = bf16[8,40,512]{2,1,0:T(8,128)(2,1)} async-done(((bf16[8,40,512]{2,1,0:T(8,128)(2,1)}), bf16[8,40,512]{2,1,0:T(8,128)(2,1)}, u32[]{:S(2)}, u32[]{:S(2)}) %all-to-all-start.3) | async-done | bytes 327712 | tf_op jit(solution)/shard_map/all_to_all | solution.py:30
  118.6 5.5 %collective-permute-done.3.right_ref = bf16[32,40,128]{2,1,0:T(8,128)(2,1)} collective-permute-done((bf16[32,40,128]{2,1,0:T(8,128)(2,1)}, bf16[32,40,128]{2,1,0:T(8,128)(2,1)}, u32[]{:S(2)}, u32[]{:S(2)}) %collective-permute-start.3) | collective-permute-done | bytes 327712 | tf_op jit(solution)/shard_map/ppermute | solution.py:20
  124.1 1.9 %collective-permute-start.4 = (bf16[8,40,512]{2,1,0:T(8,128)(2,1)}, bf16[8,40,512]{2,1,0:T(8,128)(2,1)S(1)}, u32[]{:S(2)}, u32[]{:S(2)}) collective-permute-start(bf16[8,40,512]{2,1,0:T(8,128)(2,1)} %all-to-all-done.3), channel_id=1, source_target_pairs={{0,1},{1,0},{2,3},{3,2},{4,5},{5,4},{6,7},{7,6},{8,9},{9,8},{10,11... | collective-permute-start | bytes 983048 | tf_op jit(solution)/shard_map/ppermute | solution.py:20
  126.1 1.8 %collective-permute-done.4 = bf16[8,40,512]{2,1,0:T(8,128)(2,1)S(1)} collective-permute-done((bf16[8,40,512]{2,1,0:T(8,128)(2,1)}, bf16[8,40,512]{2,1,0:T(8,128)(2,1)S(1)}, u32[]{:S(2)}, u32[]{:S(2)}) %collective-permute-start.4) | collective-permute-done | bytes 327712 | tf_op jit(solution)/shard_map/ppermute | solution.py:20
  127.9 1.3 copy-done.4
  131.5 3.0 %shard_map.146.left_ref = bf16[32,40,128]{2,1,0:T(8,128)(2,1)S(1)} custom-call(s32[1]{0:T(128)} %bitcast.core_ref, bf16[320,512]{1,0:T(8,128)(2,1)} %bitcast.12.near_ref, bf16[320,512]{1,0:T(8,128)(2,1)S(1)} %bitcast.29, bf16[640,1024]{1,0:T(8,128)(2,1)S(1)} %copy-done.6, bf16[640,1024]{1,0:T(8,128)(2,1)S(1)} %copy-done.4, bf16[448,1024]{1,0:T(8,128)(2,1)S(1)} %bitcast.26, ...), custom_call_target="tpu_custom_call" | custom-call | flops 587202560 | bytes 4456448 | tf_op jit(solution)/shard_map/pallas_call | solution.py:337
  135.7 20.6 %all_to_all.27.back_ref = bf16[32,40,128]{2,1,0:T(8,128)(2,1)S(1)} all-to-all(bf16[32,40,128]{2,1,0:T(8,128)(2,1)S(1)} %shard_map.147), channel_id=1, replica_groups={{0,32,80,112,128,160,208,240,256,288,336,368,384,416,464,496,512,544,59..., dimensions={0} | all-to-all | bytes 655360 | tf_op jit(solution)/shard_map/all_to_all | solution.py:40
  156.4 1.8 %shard_map.148 = (bf16[448,128]{1,0:T(8,128)(2,1)}, bf16[2,128]{1,0:T(2,128)(2,1)}) custom-call(bf16[32,40,128]{2,1,0:T(8,128)(2,1)S(1)} %all_to_all.27.back_ref, s32[2,128]{1,0:T(2,128)S(1)} %bitcast.31, f32[2,128]{1,0:T(2,128)S(1)} %bitcast.32, bf16[320,32]{1,0:T(8,128)(2,1)S(1)} %copy-done.13, s32[320,1]{1,0:T(8,128)S(1)} %copy-done.12, ...), custom_call_target="tpu_custom_call" | custom-call | tf_op jit(solution)/shard_map/pallas_call | solution.py:238
  (43 shorter events, 7.6 us)
Async XLA Ops:
  0.6 24.7 %copy-start = (bf16[1,1024,640]{2,1,0:T(8,128)(2,1)S(1)}, bf16[1,1024,640]{2,1,0:T(8,128)(2,1)}, u32[]{:S(2)}) copy-start(bf16[1,1024,640]{2,1,0:T(8,128)(2,1)} %param.17) | copy-start | bytes 3932164
  3.6 36.5 %all-to-all-start = ((bf16[32,40,128]{2,1,0:T(8,128)(2,1)}), bf16[32,40,128]{2,1,0:T(8,128)(2,1)S(1)}, u32[]{:S(2)}, u32[]{:S(2)}) async-start(bf16[32,40,128]{2,1,0:T(8,128)(2,1)} %shard_map.140), calls=%async_computation | async-start | bytes 655360 | tf_op jit(solution)/shard_map/all_to_all | solution.py:40
  25.3 2.3 %copy-start.18 = (bf16[1,1024,640]{2,1,0:T(8,128)(2,1)S(1)}, bf16[1,1024,640]{2,1,0:T(8,128)(2,1)}, u32[]{:S(2)}) copy-start(bf16[1,1024,640]{2,1,0:T(8,128)(2,1)} %param.16) | copy-start | bytes 3932164
  27.6 15.1 %copy-start.1 = (bf16[1,1024,448]{1,2,0:T(8,128)(2,1)S(1)}, bf16[1,1024,448]{1,2,0:T(8,128)(2,1)}, u32[]{:S(2)}) copy-start(bf16[1,1024,448]{1,2,0:T(8,128)(2,1)} %param.20) | copy-start | bytes 2752516
  27.6 15.1 %copy-start.2 = (s32[320,1]{1,0:T(8,128)S(1)}, s32[320,1]{1,0:T(8,128)}, u32[]{:S(2)}) copy-start(s32[320,1]{1,0:T(8,128)} %constant.100.clone.rank_ref) | copy-start | bytes 3844
  27.6 15.1 %copy-start.11 = (bf16[320,320]{1,0:T(8,128)(2,1)S(1)}, bf16[320,320]{1,0:T(8,128)(2,1)}, u32[]{:S(2)}) copy-start(bf16[320,320]{1,0:T(8,128)(2,1)} %constant.110.pick_ref) | copy-start | bytes 614404
  40.1 10.4 %collective-permute-start = (bf16[32,40,128]{2,1,0:T(8,128)(2,1)S(1)}, bf16[32,40,128]{2,1,0:T(8,128)(2,1)S(1)}, u32[]{:S(2)}, u32[]{:S(2)}) collective-permute-start(bf16[32,40,128]{2,1,0:T(8,128)(2,1)S(1)} %all-to-all-done.block_ref), channel_id=1, source_target_pairs={{0,16},{16,0},{1,17},{17,1},{2,18},{18,2},{3,19},{19,3},{4,20},{20... | collective-permute-start | bytes 983048 | tf_op jit(solution)/shard_map/ppermute | solution.py:20
  51.3 4.0 %collective-permute-start.1 = (bf16[8,2,40,512]{3,2,1,0:T(8,128)(2,1)S(1)}, bf16[8,2,40,512]{3,2,1,0:T(8,128)(2,1)S(1)}, u32[]{:S(2)}, u32[]{:S(2)}) collective-permute-start(bf16[8,2,40,512]{3,2,1,0:T(8,128)(2,1)S(1)} %get-tuple-element.21), channel_id=1, source_target_pairs={{0,1},{1,0},{2,3},{3,2},{4,5},{5,4},{6,7},{7,6},{8,9},{9,8},{10,11... | collective-permute-start | bytes 1966088 | tf_op jit(solution)/shard_map/ppermute | solution.py:20
  82.6 21.8 %copy-start.7 = (bf16[1,448,1024]{2,1,0:T(8,128)(2,1)S(1)}, bf16[1,448,1024]{2,1,0:T(8,128)(2,1)}, u32[]{:S(2)}) copy-start(bf16[1,448,1024]{2,1,0:T(8,128)(2,1)} %param.18) | copy-start | bytes 2752516
  82.6 21.8 %copy-start.8 = (bf16[1,448,1024]{2,1,0:T(8,128)(2,1)S(1)}, bf16[1,448,1024]{2,1,0:T(8,128)(2,1)}, u32[]{:S(2)}) copy-start(bf16[1,448,1024]{2,1,0:T(8,128)(2,1)} %param.19) | copy-start | bytes 2752516
  82.7 15.7 %copy-start.14 = (bf16[8,40,512]{2,1,0:T(8,128)(2,1)}, bf16[8,40,512]{2,1,0:T(8,128)(2,1)S(1)}, u32[]{:S(2)}) copy-start(bf16[8,40,512]{2,1,0:T(8,128)(2,1)S(1)} %get-tuple-element.24) | copy-start | bytes 983044
  98.4 6.0 %collective-permute-start.2 = (bf16[8,40,512]{2,1,0:T(8,128)(2,1)}, bf16[8,40,512]{2,1,0:T(8,128)(2,1)}, u32[]{:S(2)}, u32[]{:S(2)}) collective-permute-start(bf16[8,40,512]{2,1,0:T(8,128)(2,1)} %all_to_all.26), channel_id=1, source_target_pairs={{0,1},{1,0},{2,3},{3,2},{4,5},{5,4},{6,7},{7,6},{8,9},{9,8},{10,11... | collective-permute-start | bytes 983048 | tf_op jit(solution)/shard_map/ppermute | solution.py:20
  100.3 18.3 %all-to-all-start.3 = ((bf16[8,40,512]{2,1,0:T(8,128)(2,1)}), bf16[8,40,512]{2,1,0:T(8,128)(2,1)}, u32[]{:S(2)}, u32[]{:S(2)}) async-start(bf16[8,40,512]{2,1,0:T(8,128)(2,1)} %copy-done.14), calls=%async_computation.3 | async-start | bytes 655360 | tf_op jit(solution)/shard_map/all_to_all | solution.py:30
  104.4 1.3 copy-start.3
  105.7 1.3 copy-start.5
  111.8 12.3 %collective-permute-start.3 = (bf16[32,40,128]{2,1,0:T(8,128)(2,1)}, bf16[32,40,128]{2,1,0:T(8,128)(2,1)}, u32[]{:S(2)}, u32[]{:S(2)}) collective-permute-start(bf16[32,40,128]{2,1,0:T(8,128)(2,1)} %shard_map.145), channel_id=1, source_target_pairs={{0,16},{16,0},{1,17},{17,1},{2,18},{18,2},{3,19},{19,3},{4,20},{20... | collective-permute-start | bytes 983048 | tf_op jit(solution)/shard_map/ppermute | solution.py:20
  124.1 3.7 %collective-permute-start.4 = (bf16[8,40,512]{2,1,0:T(8,128)(2,1)}, bf16[8,40,512]{2,1,0:T(8,128)(2,1)S(1)}, u32[]{:S(2)}, u32[]{:S(2)}) collective-permute-start(bf16[8,40,512]{2,1,0:T(8,128)(2,1)} %all-to-all-done.3), channel_id=1, source_target_pairs={{0,1},{1,0},{2,3},{3,2},{4,5},{5,4},{6,7},{7,6},{8,9},{9,8},{10,11... | collective-permute-start | bytes 983048 | tf_op jit(solution)/shard_map/ppermute | solution.py:20
  127.9 1.3 copy-start.4
  129.2 1.3 copy-start.6
  134.5 21.8 %copy-start.12 = (s32[320,1]{1,0:T(8,128)S(1)}, s32[320,1]{1,0:T(8,128)}, u32[]{:S(2)}) copy-start(s32[320,1]{1,0:T(8,128)} %constant.99.clone.expert_ref) | copy-start | bytes 3844
  134.5 21.8 %copy-start.13 = (bf16[320,32]{1,0:T(8,128)(2,1)S(1)}, bf16[320,32]{1,0:T(8,128)(2,1)}, u32[]{:S(2)}) copy-start(bf16[320,32]{1,0:T(8,128)(2,1)} %constant.101.clone.widen_ref) | copy-start | bytes 61444
  134.5 21.8 %copy-start.15 = (bf16[400,320]{1,0:T(8,128)(2,1)S(1)}, bf16[400,320]{1,0:T(8,128)(2,1)}, u32[]{:S(2)}) copy-start(bf16[400,320]{1,0:T(8,128)(2,1)} %constant.102.clone.pick_ref) | copy-start | bytes 768004
  134.6 21.8 %copy-start.16 = (s32[128,2]{0,1:T(2,128)S(1)}, s32[128,2]{0,1:T(2,128)}, u32[]{:S(2)}) copy-start(s32[128,2]{0,1:T(2,128)} %param.14) | copy-start | bytes 3076
  134.6 21.8 %copy-start.17 = (f32[128,2]{0,1:T(2,128)S(1)}, f32[128,2]{0,1:T(2,128)}, u32[]{:S(2)}) copy-start(f32[128,2]{0,1:T(2,128)} %param.15) | copy-start | bytes 3076
  (2 other events, 1.9 us)

commit v8 on v6

--- a/solution.py
+++ b/solution.py
@@ -58,12 +58,16 @@
     return (lane < LANES // 2) == (rank < capacity // 2)
 
 
-def unpacked(block_ref, pick_ref, rank, capacity):
+def unpacked(block_ref, pick_ref, rank, capacity, places=None):
     span = BATCH * capacity
     features, probs = [], []
-    for batch in range(block_ref.shape[0] // BATCH):
-        rows = block_ref[batch * BATCH : (batch + 1) * BATCH].astype(jnp.float32)
-        rows = rows.reshape(BATCH * PACKED, LANES).astype(jnp.bfloat16)
+    for batch in range((len(places) if places else block_ref.shape[0]) // BATCH):
+        here = slice(batch * BATCH, (batch + 1) * BATCH)
+        if places:
+            rows = jnp.concatenate([block_ref[n].astype(jnp.float32) for n in places[here]], axis=0)
+        else:
+            rows = block_ref[here].astype(jnp.float32).reshape(BATCH * PACKED, LANES)
+        rows = rows.astype(jnp.bfloat16)
         picked = jnp.dot(pick_ref[...], rows, preferred_element_type=jnp.float32)
         own = rank[batch * span : (batch + 1) * span]
         tail = jnp.where(tail_lanes(own, capacity), picked[3 * span : 4 * span], 0.0)
@@ -93,9 +97,13 @@
         packed = jnp.dot(
             put_ref[:, : stacked.shape[0]], stacked, preferred_element_type=jnp.float32
         )
-        out_ref[batch * BATCH : (batch + 1) * BATCH] = packed.reshape(
-            BATCH, PACKED, LANES
-        ).astype(jnp.bfloat16)
+        packed = packed.reshape(BATCH, PACKED, LANES).astype(jnp.bfloat16)
+        here = slice(batch * BATCH, (batch + 1) * BATCH)
+        if len(out_ref.shape) == 3:
+            out_ref[here] = packed
+        else:
+            for node in range(out_ref.shape[1]):
+                out_ref[here, node] = packed
 
 
 def slot_masks(routes, widen, expert, rank):
@@ -127,11 +135,22 @@
 
 
 def down_kernel(
-    capacity, core_ref, block_ref, kept_w_ref, sent_w_ref, pick_ref, rank_ref, *refs
+    capacity,
+    turns,
+    where_ref,
+    block_ref,
+    kept_w_ref,
+    sent_w_ref,
+    pick_ref,
+    rank_ref,
+    kept_ref,
+    sent_ref,
 ):
-    kept_ref, sent_ref = refs[-2:]
-    rows, _ = unpacked(block_ref, pick_ref, rank_ref[...], capacity)
-    rows = jnp.concatenate(rows, axis=0)
+    sides = []
+    for side in range(2):
+        places = [2 * p + (where_ref[1] ^ (turn ^ side)) for p, turn in enumerate(turns)]
+        sides += unpacked(block_ref, pick_ref, rank_ref[...], capacity, places)[0]
+    rows = jnp.concatenate(sides, axis=0)
     for weights_ref, out_ref in ((sent_w_ref, sent_ref), (kept_w_ref, kept_ref)):
         out_ref[...] = jnp.dot(
             rows, stretched(weights_ref[...]), preferred_element_type=jnp.float32
@@ -265,7 +284,7 @@
     routes = route_expert.T
     outgoing = whole(
         functools.partial(dispatch_kernel, capacity),
-        block,
+        jax.ShapeDtypeStruct((experts, 2, PACKED, LANES), bf16),
         routes,
         grad_out.T,
         widen,
@@ -274,7 +293,9 @@
         put_all[:, : 4 * kinds.shape[1]],
         params=FULL,
     )
-    own_rows = over_group(outgoing)
+    arrived = lax.all_to_all(
+        outgoing.reshape(2 * experts, PACKED, LANES), NODE, split_axis=0, concat_axis=0, tiled=True
+    )
 
     slot = jnp.arange(slots_all, dtype=jnp.int32)[:, None]
     place = jnp.arange(slots_all, dtype=jnp.int32)[None, :]
@@ -285,39 +306,36 @@
     gate_rows = times_transposed(order, saved_gate[0]).astype(bf16)
     up_rows = times_transposed(order, saved_up[0]).astype(bf16)
     down = w_down[0].T
-    own_rows, gate_rows, up_rows = lax.optimization_barrier((own_rows, gate_rows, up_rows))
-
-    pair_rows = swap(own_rows, "yl")
+    arrived, gate_rows, up_rows = lax.optimization_barrier((arrived, gate_rows, up_rows))
+
     cores = core.astype(jnp.int32).reshape(1)
     block_spec = pl.BlockSpec(block.shape, lambda i, c: (0, 0, 0))
     fixed = lambda i, c: (0, 0)
     product = jax.ShapeDtypeStruct((slots_all, half), bf16)
-
-    def products_of(side, rows, *filled):
-        return pl.pallas_call(
-            functools.partial(down_kernel, capacity),
-            out_shape=(product, product),
-            grid_spec=pltpu.PrefetchScalarGridSpec(
-                num_scalar_prefetch=1,
-                grid=(1,),
-                in_specs=[
-                    block_spec,
-                    pl.BlockSpec((feats, half), lambda i, c: (0, c[0])),
-                    pl.BlockSpec((feats, half), lambda i, c: (0, 1 - c[0])),
-                    pl.BlockSpec(pick_rows.shape, fixed),
-                    pl.BlockSpec(rank_of.shape, fixed),
-                ]
-                + [pl.BlockSpec(memory_space=pl.ANY)] * len(filled),
-                out_specs=[pl.BlockSpec((slots_side, half), lambda i, c: (side, 0))] * 2,
-            ),
-            input_output_aliases={6 + i: i for i in range(len(filled))},
-            compiler_params=BIG,
-            cost_estimate=cost(
-                2 * slots_side * feats * half, 2 * feats * half + 3 * slots_side * half
-            ),
-        )(cores, rows, down, down, pick_rows, rank_of, *filled)
-
-    kept, sent = products_of(1, pair_rows, *products_of(0, own_rows))
+    kept, sent = pl.pallas_call(
+        functools.partial(down_kernel, capacity, tuple(turned(p) for p in range(experts))),
+        out_shape=(product, product),
+        grid_spec=pltpu.PrefetchScalarGridSpec(
+            num_scalar_prefetch=1,
+            grid=(1,),
+            in_specs=[
+                pl.BlockSpec(arrived.shape, lambda i, c: (0, 0, 0)),
+                pl.BlockSpec((feats, half), lambda i, c: (0, c[0])),
+                pl.BlockSpec((feats, half), lambda i, c: (0, 1 - c[0])),
+                pl.BlockSpec(pick_rows.shape, fixed),
+                pl.BlockSpec(rank_of.shape, fixed),
+            ],
+            out_specs=[pl.BlockSpec((slots_all, half), fixed)] * 2,
+        ),
+        compiler_params=BIG,
+    )(
+        jnp.stack([core, group]).astype(jnp.int32),
+        arrived,
+        down,
+        down,
+        pick_rows,
+        rank_of,
+    )
     on_chip = whole(sum_kernel, product, kept, swap(sent, "c"))
     pieces = over_x(on_chip.reshape(chips, slots_all // chips, half))
     near = over_x(

time: 145 us -> 146 us (level)
  local copies, waits for them, and re-layouts: 0.08 us -> 2.26 us
    all_to_all x1, waiting for transfers between devices: 10.2 us -> 18 us  [shards(): lax.all_to_all(outgoing.reshape(2 * experts, PACKED, LANES), NODE, split_...]
    ppermute x4 -> x3, waiting for transfers between devices: 18.2 us -> 10.8 us  [swap(): return lax.ppermute(value, axis, ((0, 1), (1, 0)))]
    unnamed x30 -> x28, local copies, waits for them, and re-layouts: 0.08 us -> 2.26 us
    ppermute x4 -> x3, starting transfers between devices: 8.63 us -> 6.49 us  [swap(): return lax.ppermute(value, axis, ((0, 1), (1, 0)))]
    all_to_all x1, starting transfers between devices: 21.7 us -> 23.3 us  [shards(): lax.all_to_all(outgoing.reshape(2 * experts, PACKED, LANES), NODE, split_...]
  transfers between devices with their start and end apart: 5 -> 4, of which waited for: 5 -> 4; matrix products, arithmetic and copies ran while one was open for 3% -> 3% of each run, Pallas kernels for 2% -> 2%
where the time goes in v8:
time: 146 us; the launch traced here: 145 us
  blocking collectives  68.4 us (47%)
  starting transfers between devices  29.8 us (20%)
  waiting for transfers between devices  28.8 us (20%)
  Pallas kernels  11.5 us (8%)
  matrix products  3.55 us (2%)
  local copies, waits for them, and re-layouts  2.26 us (2%)
    all_to_all x2, blocking collectives, over_x(): return lax.all_to_all(blocks, 'x', split_axis=0, concat_axis=0, tiled=True)  49.3 us
    all_to_all x1, starting transfers between devices, shards(): lax.all_to_all(outgoing.reshape(2 * experts, PACKED, LANES), NODE, split_...  23.3 us
    all_to_all x1, blocking collectives, over_group(): lax.all_to_all(blocks, NODE, split_axis=0, concat_axis=0, tiled=True, axi...  19.1 us
    all_to_all x1, waiting for transfers between devices, shards(): lax.all_to_all(outgoing.reshape(2 * experts, PACKED, LANES), NODE, split_...  18 us
    ppermute x3, waiting for transfers between devices, swap(): return lax.ppermute(value, axis, ((0, 1), (1, 0)))  10.8 us
    ppermute x3, starting transfers between devices, swap(): return lax.ppermute(value, axis, ((0, 1), (1, 0)))  6.49 us
    pallas_call x5, Pallas kernels, whole(): pl.pallas_call(kernel, out_shape=out_shape, compiler_params=params, cost_...  5.15 us
    pallas_call x2, Pallas kernels, routes_of(): pl.pallas_call(functools.partial(route_kernel, capacity), out_shape=block...  4.41 us
  transfers between devices with their start and end apart: 4, of which 4 were waited for; matrix products, arithmetic and copies ran while one was open for 3% of the time, Pallas kernels for 2%

profile of v8, /device:TPU:16, one launch (start us, length us, event | category | flops | bytes accessed | tf_op | source)
XLA Modules:
  0.0 145.2 jit_solution(4363100801005247653)
XLA Ops:
  0.6 3.0 %shard_map.140 = bf16[32,2,40,128]{3,2,1,0:T(8,128)(2,1)} custom-call(s32[2,128]{1,0:T(2,128)} %bitcast.31, bf16[448,128]{1,0:T(8,128)(2,1)} %bitcast.35, bf16[320,32]{1,0:T(8,128)(2,1)} %constant.101.clone.widen_ref, s32[320,1]{1,0:T(8,128)} %constant.99.clone.expert_ref, s32[320,1]{1,0:T(8,128)} %constant.100.clone.rank_ref, ...), custom_call_target="tpu_custom_call" | custom-call | tf_op jit(solution)/shard_map/pallas_call | solution.py:257
  3.7 23.3 %all-to-all-start = ((bf16[64,40,128]{2,1,0:T(8,128)(2,1)}), bf16[64,40,128]{2,1,0:T(8,128)(2,1)S(1)}, u32[]{:S(2)}, u32[]{:S(2)}) async-start(bf16[64,40,128]{2,1,0:T(8,128)(2,1)} %bitcast.34), calls=%async_computation | async-start | bytes 1310720 | tf_op jit(solution)/shard_map/all_to_all | solution.py:296
  27.0 0.1 pad_add_fusion.where_ref
  27.1 1.2 fusion.3.up_ref
  28.5 2.3 %fusion.2.gate_ref = bf16[640,1024]{1,0:T(8,128)(2,1)} fusion(bf16[1,1024,640]{2,1,0:T(8,128)(2,1)S(1)} %copy-done.13, s32[640]{0:T(1024)S(1)} %fusion.17), kind=kOutput, calls=%fused_computation.3 | convolution fusion | flops 839925760 | bytes 2624000 | tf_op jit(solution)/shard_map/dot_general | solution.py:24
  30.8 18.0 %all-to-all-done.block_ref = bf16[64,40,128]{2,1,0:T(8,128)(2,1)S(1)} async-done(((bf16[64,40,128]{2,1,0:T(8,128)(2,1)}), bf16[64,40,128]{2,1,0:T(8,128)(2,1)S(1)}, u32[]{:S(2)}, u32[]{:S(2)}) %all-to-all-start) | async-done | bytes 655392 | tf_op jit(solution)/shard_map/all_to_all | solution.py:296
  48.8 1.2 copy-done.3
  49.9 0.9 copy-done.10
  50.9 1.9 %shard_map.141 = (bf16[640,512]{1,0:T(8,128)(2,1)S(1)}, bf16[640,512]{1,0:T(8,128)(2,1)S(1)}) custom-call(s32[2]{0:T(128)S(1)} %pad_add_fusion.where_ref, bf16[64,40,128]{2,1,0:T(8,128)(2,1)S(1)} %all-to-all-done.block_ref, bf16[448,1024]{1,0:T(8,128)(2,1)S(1)} %bitcast.24, bf16[448,1024]{1,0:T(8,128)(2,1)S(1)} %bitcast.25, bf16[320,320]{1,0:T(8,128)(2,1)S(1)} %copy-done.10, ...), custom_call_target="tpu_custom_call" | custom-call | tf_op jit(solution)/shard_map/pallas_call | solution.py:315
  52.8 1.9 %collective-permute-start = (bf16[640,512]{1,0:T(8,128)(2,1)S(1)}, bf16[640,512]{1,0:T(8,128)(2,1)S(1)}, u32[]{:S(2)}, u32[]{:S(2)}) collective-permute-start(bf16[640,512]{1,0:T(8,128)(2,1)S(1)} %get-tuple-element.12), channel_id=1, source_target_pairs={{0,1},{1,0},{2,3},{3,2},{4,5},{5,4},{6,7},{7,6},{8,9},{9,8},{10,11... | collective-permute-start | bytes 1966088 | tf_op jit(solution)/shard_map/ppermute | solution.py:20
  54.7 2.1 %collective-permute-done.right_ref = bf16[640,512]{1,0:T(8,128)(2,1)S(1)} collective-permute-done((bf16[640,512]{1,0:T(8,128)(2,1)S(1)}, bf16[640,512]{1,0:T(8,128)(2,1)S(1)}, u32[]{:S(2)}, u32[]{:S(2)}) %collective-permute-start) | collective-permute-done | bytes 655392 | tf_op jit(solution)/shard_map/ppermute | solution.py:20
  56.8 0.2 shard_map.142
  56.9 27.3 %all_to_all.20.pieces_ref = bf16[8,80,512]{2,1,0:T(8,128)(2,1)S(1)} all-to-all(bf16[8,80,512]{2,1,0:T(8,128)(2,1)S(1)} %bitcast.30), channel_id=1, replica_groups=mesh['z'=8,'yh'=4,'yl'=2,'x'=8,'c'=2] {'x'}, dimensions={0} | all-to-all | bytes 1310720 | tf_op jit(solution)/shard_map/all_to_all | solution.py:30
  84.2 0.1 shard_map.143
  84.3 22.0 %all_to_all.21 = bf16[8,80,512]{2,1,0:T(8,128)(2,1)S(1)} all-to-all(bf16[8,80,512]{2,1,0:T(8,128)(2,1)S(1)} %shard_map.143), channel_id=1, replica_groups=mesh['z'=8,'yh'=4,'yl'=2,'x'=8,'c'=2] {'x'}, dimensions={0} | all-to-all | bytes 1310720 | tf_op jit(solution)/shard_map/all_to_all | solution.py:30
  106.4 1.9 %collective-permute-start.1 = (bf16[640,512]{1,0:T(8,128)(2,1)S(1)}, bf16[640,512]{1,0:T(8,128)(2,1)S(1)}, u32[]{:S(2)}, u32[]{:S(2)}) collective-permute-start(bf16[640,512]{1,0:T(8,128)(2,1)S(1)} %bitcast.21), channel_id=1, source_target_pairs={{0,1},{1,0},{2,3},{3,2},{4,5},{5,4},{6,7},{7,6},{8,9},{9,8},{10,11... | collective-permute-start | bytes 1966088 | tf_op jit(solution)/shard_map/ppermute | solution.py:20
  108.3 2.1 %collective-permute-done.1.far_ref = bf16[640,512]{1,0:T(8,128)(2,1)S(1)} collective-permute-done((bf16[640,512]{1,0:T(8,128)(2,1)S(1)}, bf16[640,512]{1,0:T(8,128)(2,1)S(1)}, u32[]{:S(2)}, u32[]{:S(2)}) %collective-permute-start.1) | collective-permute-done | bytes 655392 | tf_op jit(solution)/shard_map/ppermute | solution.py:20
  110.4 2.2 %shard_map.144 = bf16[32,40,128]{2,1,0:T(8,128)(2,1)S(1)} custom-call(s32[1]{0:T(128)} %bitcast.core_ref, bf16[640,512]{1,0:T(8,128)(2,1)S(1)} %bitcast.22, bf16[640,512]{1,0:T(8,128)(2,1)S(1)} %collective-permute-done.1.far_ref, bf16[640,1024]{1,0:T(8,128)(2,1)S(1)} %copy-done.1, bf16[640,1024]{1,0:T(8,128)(2,1)S(1)} %fusion.3.up_ref, ...), custom_call_target="tpu_custom_call" | custom-call | tf_op jit(solution)/shard_map/pallas_call | solution.py:350
  112.6 2.7 %collective-permute-start.2 = (bf16[32,40,128]{2,1,0:T(8,128)(2,1)S(1)}, bf16[32,40,128]{2,1,0:T(8,128)(2,1)S(1)}, u32[]{:S(2)}, u32[]{:S(2)}) collective-permute-start(bf16[32,40,128]{2,1,0:T(8,128)(2,1)S(1)} %shard_map.144), channel_id=1, source_target_pairs={{0,16},{16,0},{1,17},{17,1},{2,18},{18,2},{3,19},{19,3},{4,20},{20... | collective-permute-start | bytes 983048 | tf_op jit(solution)/shard_map/ppermute | solution.py:20
  115.2 2.2 %shard_map.145.left_ref = bf16[32,40,128]{2,1,0:T(8,128)(2,1)S(1)} custom-call(s32[1]{0:T(128)} %bitcast.core_ref, bf16[640,512]{1,0:T(8,128)(2,1)S(1)} %bitcast.23, bf16[640,512]{1,0:T(8,128)(2,1)S(1)} %collective-permute-done.1.far_ref, bf16[640,1024]{1,0:T(8,128)(2,1)S(1)} %copy-done.1, bf16[640,1024]{1,0:T(8,128)(2,1)S(1)} %fusion.3.up_ref, ...), custom_call_target="tpu_custom_call" | custom-call | tf_op jit(solution)/shard_map/pallas_call | solution.py:350
  117.5 6.7 %collective-permute-done.2.right_ref = bf16[32,40,128]{2,1,0:T(8,128)(2,1)S(1)} collective-permute-done((bf16[32,40,128]{2,1,0:T(8,128)(2,1)S(1)}, bf16[32,40,128]{2,1,0:T(8,128)(2,1)S(1)}, u32[]{:S(2)}, u32[]{:S(2)}) %collective-permute-start.2) | collective-permute-done | bytes 327712 | tf_op jit(solution)/shard_map/ppermute | solution.py:20
  124.2 0.1 shard_map.146
  124.3 19.1 %all_to_all.22.back_ref = bf16[32,40,128]{2,1,0:T(8,128)(2,1)S(1)} all-to-all(bf16[32,40,128]{2,1,0:T(8,128)(2,1)S(1)} %shard_map.146), channel_id=1, replica_groups={{0,32,80,112,128,160,208,240,256,288,336,368,384,416,464,496,512,544,59..., dimensions={0} | all-to-all | bytes 655360 | tf_op jit(solution)/shard_map/all_to_all | solution.py:40
  143.4 1.8 %shard_map.147 = (bf16[448,128]{1,0:T(8,128)(2,1)}, bf16[2,128]{1,0:T(2,128)(2,1)}) custom-call(bf16[32,40,128]{2,1,0:T(8,128)(2,1)S(1)} %all_to_all.22.back_ref, s32[2,128]{1,0:T(2,128)S(1)} %bitcast.32, f32[2,128]{1,0:T(2,128)S(1)} %bitcast.33, bf16[320,32]{1,0:T(8,128)(2,1)S(1)} %copy-done.8, s32[320,1]{1,0:T(8,128)S(1)} %copy-done.7, ...), custom_call_target="tpu_custom_call" | custom-call | tf_op jit(solution)/shard_map/pallas_call | solution.py:257
  (27 shorter events, 0.2 us)
Async XLA Ops:
  0.6 26.5 %copy-start = (bf16[1,1024,640]{2,1,0:T(8,128)(2,1)S(1)}, bf16[1,1024,640]{2,1,0:T(8,128)(2,1)}, u32[]{:S(2)}) copy-start(bf16[1,1024,640]{2,1,0:T(8,128)(2,1)} %param.17) | copy-start | bytes 3932164
  3.7 45.1 %all-to-all-start = ((bf16[64,40,128]{2,1,0:T(8,128)(2,1)}), bf16[64,40,128]{2,1,0:T(8,128)(2,1)S(1)}, u32[]{:S(2)}, u32[]{:S(2)}) async-start(bf16[64,40,128]{2,1,0:T(8,128)(2,1)} %bitcast.34), calls=%async_computation | async-start | bytes 1310720 | tf_op jit(solution)/shard_map/all_to_all | solution.py:296
  27.1 1.3 copy-start.13
  28.5 20.3 %copy-start.2 = (s32[320,1]{1,0:T(8,128)S(1)}, s32[320,1]{1,0:T(8,128)}, u32[]{:S(2)}) copy-start(s32[320,1]{1,0:T(8,128)} %constant.100.clone.rank_ref) | copy-start | bytes 3844
  48.8 1.2 copy-start.3
  49.9 0.9 copy-start.10
  52.8 4.0 %collective-permute-start = (bf16[640,512]{1,0:T(8,128)(2,1)S(1)}, bf16[640,512]{1,0:T(8,128)(2,1)S(1)}, u32[]{:S(2)}, u32[]{:S(2)}) collective-permute-start(bf16[640,512]{1,0:T(8,128)(2,1)S(1)} %get-tuple-element.12), channel_id=1, source_target_pairs={{0,1},{1,0},{2,3},{3,2},{4,5},{5,4},{6,7},{7,6},{8,9},{9,8},{10,11... | collective-permute-start | bytes 1966088 | tf_op jit(solution)/shard_map/ppermute | solution.py:20
  56.9 53.4 %copy-start.5 = (bf16[1,448,1024]{2,1,0:T(8,128)(2,1)S(1)}, bf16[1,448,1024]{2,1,0:T(8,128)(2,1)}, u32[]{:S(2)}) copy-start(bf16[1,448,1024]{2,1,0:T(8,128)(2,1)} %param.19) | copy-start | bytes 2752516
  84.2 26.1 %copy-start.1 = (bf16[640,1024]{1,0:T(8,128)(2,1)S(1)}, bf16[640,1024]{1,0:T(8,128)(2,1)}, u32[]{:S(2)}) copy-start(bf16[640,1024]{1,0:T(8,128)(2,1)} %fusion.2.gate_ref) | copy-start | bytes 3932164
  84.2 26.1 %copy-start.4 = (bf16[1,448,1024]{2,1,0:T(8,128)(2,1)S(1)}, bf16[1,448,1024]{2,1,0:T(8,128)(2,1)}, u32[]{:S(2)}) copy-start(bf16[1,448,1024]{2,1,0:T(8,128)(2,1)} %param.18) | copy-start | bytes 2752516
  84.2 26.1 %copy-start.6 = (bf16[320,400]{1,0:T(8,128)(2,1)S(1)}, bf16[320,400]{1,0:T(8,128)(2,1)}, u32[]{:S(2)}) copy-start(bf16[320,400]{1,0:T(8,128)(2,1)} %constant.103.clone.put_ref) | copy-start | bytes 768004
  106.4 4.0 %collective-permute-start.1 = (bf16[640,512]{1,0:T(8,128)(2,1)S(1)}, bf16[640,512]{1,0:T(8,128)(2,1)S(1)}, u32[]{:S(2)}, u32[]{:S(2)}) collective-permute-start(bf16[640,512]{1,0:T(8,128)(2,1)S(1)} %bitcast.21), channel_id=1, source_target_pairs={{0,1},{1,0},{2,3},{3,2},{4,5},{5,4},{6,7},{7,6},{8,9},{9,8},{10,11... | collective-permute-start | bytes 1966088 | tf_op jit(solution)/shard_map/ppermute | solution.py:20
  112.6 11.6 %collective-permute-start.2 = (bf16[32,40,128]{2,1,0:T(8,128)(2,1)S(1)}, bf16[32,40,128]{2,1,0:T(8,128)(2,1)S(1)}, u32[]{:S(2)}, u32[]{:S(2)}) collective-permute-start(bf16[32,40,128]{2,1,0:T(8,128)(2,1)S(1)} %shard_map.144), channel_id=1, source_target_pairs={{0,16},{16,0},{1,17},{17,1},{2,18},{18,2},{3,19},{19,3},{4,20},{20... | collective-permute-start | bytes 983048 | tf_op jit(solution)/shard_map/ppermute | solution.py:20
  117.5 25.9 %copy-start.7 = (s32[320,1]{1,0:T(8,128)S(1)}, s32[320,1]{1,0:T(8,128)}, u32[]{:S(2)}) copy-start(s32[320,1]{1,0:T(8,128)} %constant.99.clone.expert_ref) | copy-start | bytes 3844
  117.5 25.9 %copy-start.8 = (bf16[320,32]{1,0:T(8,128)(2,1)S(1)}, bf16[320,32]{1,0:T(8,128)(2,1)}, u32[]{:S(2)}) copy-start(bf16[320,32]{1,0:T(8,128)(2,1)} %constant.101.clone.widen_ref) | copy-start | bytes 61444
  117.5 25.9 %copy-start.9 = (bf16[400,320]{1,0:T(8,128)(2,1)S(1)}, bf16[400,320]{1,0:T(8,128)(2,1)}, u32[]{:S(2)}) copy-start(bf16[400,320]{1,0:T(8,128)(2,1)} %constant.102.clone.pick_ref) | copy-start | bytes 768004
  117.5 25.9 %copy-start.11 = (s32[128,2]{0,1:T(2,128)S(1)}, s32[128,2]{0,1:T(2,128)}, u32[]{:S(2)}) copy-start(s32[128,2]{0,1:T(2,128)} %param.14) | copy-start | bytes 3076
  117.5 25.9 %copy-start.12 = (f32[128,2]{0,1:T(2,128)S(1)}, f32[128,2]{0,1:T(2,128)}, u32[]{:S(2)}) copy-start(f32[128,2]{0,1:T(2,128)} %param.15) | copy-start | bytes 3076

commit v9 on v8

--- a/solution.py
+++ b/solution.py
@@ -141,11 +141,19 @@
     block_ref,
     kept_w_ref,
     sent_w_ref,
-    pick_ref,
     rank_ref,
     kept_ref,
     sent_ref,
+    pick_ref,
 ):
+    span = BATCH * capacity
+    rank = rank_ref[: 4 * span]
+    row = lax.broadcasted_iota(jnp.int32, rank.shape, 0)
+    kind = sum((row >= span * k).astype(jnp.int32) for k in range(1, 4))
+    fold = jnp.where((kind == 3) & (rank >= capacity // 2), capacity // 2, 0)
+    target = (row - span * kind - rank) * (PACKED // capacity) + capacity * kind + rank - fold
+    lane = lax.broadcasted_iota(jnp.int32, pick_ref.shape, 1)
+    pick_ref[...] = jnp.where(lane == target, 1.0, 0.0).astype(jnp.bfloat16)
     sides = []
     for side in range(2):
         places = [2 * p + (where_ref[1] ^ (turn ^ side)) for p, turn in enumerate(turns)]
@@ -277,7 +285,6 @@
     widen = jnp.asarray(numbers // capacity == np.arange(experts)[None, :], bf16)
     kinds = packing(capacity)
     pick_all = jnp.asarray(kinds.reshape(-1, kinds.shape[2]), bf16)
-    pick_rows = pick_all[: 4 * kinds.shape[1]]
     put_all = jnp.asarray(kinds.reshape(-1, kinds.shape[2]).T, bf16)
     block = jax.ShapeDtypeStruct((experts, PACKED, LANES), bf16)
 
@@ -322,10 +329,10 @@
                 pl.BlockSpec(arrived.shape, lambda i, c: (0, 0, 0)),
                 pl.BlockSpec((feats, half), lambda i, c: (0, c[0])),
                 pl.BlockSpec((feats, half), lambda i, c: (0, 1 - c[0])),
-                pl.BlockSpec(pick_rows.shape, fixed),
                 pl.BlockSpec(rank_of.shape, fixed),
             ],
             out_specs=[pl.BlockSpec((slots_all, half), fixed)] * 2,
+            scratch_shapes=[pltpu.VMEM((4 * kinds.shape[1], kinds.shape[2]), bf16)],
         ),
         compiler_params=BIG,
     )(
@@ -333,7 +340,6 @@
         arrived,
         down,
         down,
-        pick_rows,
         rank_of,
     )
     on_chip = whole(sum_kernel, product, kept, swap(sent, "c"))

time: 146 us -> 145 us (level)
  no operation moved by 1% of the time
where the time goes in v9:
time: 145 us; the launch traced here: 144 us
  blocking collectives  68.4 us (47%)
  starting transfers between devices  29.8 us (21%)
  waiting for transfers between devices  28.8 us (20%)
  Pallas kernels  11.5 us (8%)
  matrix products  3.55 us (2%)
    all_to_all x2, blocking collectives, over_x(): return lax.all_to_all(blocks, 'x', split_axis=0, concat_axis=0, tiled=True)  49.3 us
    all_to_all x1, starting transfers between devices, shards(): lax.all_to_all(outgoing.reshape(2 * experts, PACKED, LANES), NODE, split_...  23.3 us
    all_to_all x1, blocking collectives, over_group(): lax.all_to_all(blocks, NODE, split_axis=0, concat_axis=0, tiled=True, axi...  19 us
    all_to_all x1, waiting for transfers between devices, shards(): lax.all_to_all(outgoing.reshape(2 * experts, PACKED, LANES), NODE, split_...  18 us
    ppermute x3, waiting for transfers between devices, swap(): return lax.ppermute(value, axis, ((0, 1), (1, 0)))  10.8 us
    ppermute x3, starting transfers between devices, swap(): return lax.ppermute(value, axis, ((0, 1), (1, 0)))  6.5 us
    pallas_call x5, Pallas kernels, whole(): pl.pallas_call(kernel, out_shape=out_shape, compiler_params=params, cost_...  5.15 us
    pallas_call x2, Pallas kernels, routes_of(): pl.pallas_call(functools.partial(route_kernel, capacity), out_shape=block...  4.41 us
  transfers between devices with their start and end apart: 4, of which 4 were waited for; matrix products, arithmetic and copies ran while one was open for 3% of the time, Pallas kernels for 2%

profile of v9, /device:TPU:16, one launch (start us, length us, event | category | flops | bytes accessed | tf_op | source)
XLA Modules:
  0.0 144.3 jit_solution(3074892325086749848)
XLA Ops:
  0.6 3.0 %shard_map.140 = bf16[32,2,40,128]{3,2,1,0:T(8,128)(2,1)} custom-call(s32[2,128]{1,0:T(2,128)} %bitcast.31, bf16[448,128]{1,0:T(8,128)(2,1)} %bitcast.35, bf16[320,32]{1,0:T(8,128)(2,1)} %constant.101.clone.widen_ref, s32[320,1]{1,0:T(8,128)} %constant.99.clone.expert_ref, s32[320,1]{1,0:T(8,128)} %constant.100.clone.rank_ref, ...), custom_call_target="tpu_custom_call" | custom-call | tf_op jit(solution)/shard_map/pallas_call | solution.py:265
  3.7 23.3 %all-to-all-start = ((bf16[64,40,128]{2,1,0:T(8,128)(2,1)}), bf16[64,40,128]{2,1,0:T(8,128)(2,1)S(1)}, u32[]{:S(2)}, u32[]{:S(2)}) async-start(bf16[64,40,128]{2,1,0:T(8,128)(2,1)} %bitcast.34), calls=%async_computation | async-start | bytes 1310720 | tf_op jit(solution)/shard_map/all_to_all | solution.py:303
  27.0 0.1 pad_add_fusion.where_ref
  27.1 1.2 fusion.3.up_ref
  28.4 0.1 copy-done.12
  28.5 2.3 %fusion.2.gate_ref = bf16[640,1024]{1,0:T(8,128)(2,1)} fusion(bf16[1,1024,640]{2,1,0:T(8,128)(2,1)S(1)} %copy-done.12, s32[640]{0:T(1024)S(1)} %fusion.17), kind=kOutput, calls=%fused_computation.3 | convolution fusion | flops 839925760 | bytes 2624000 | tf_op jit(solution)/shard_map/dot_general | solution.py:24
  30.8 18.0 %all-to-all-done.block_ref = bf16[64,40,128]{2,1,0:T(8,128)(2,1)S(1)} async-done(((bf16[64,40,128]{2,1,0:T(8,128)(2,1)}), bf16[64,40,128]{2,1,0:T(8,128)(2,1)S(1)}, u32[]{:S(2)}, u32[]{:S(2)}) %all-to-all-start) | async-done | bytes 655392 | tf_op jit(solution)/shard_map/all_to_all | solution.py:303
  48.8 1.2 copy-done.3
  49.9 2.0 %shard_map.141 = (bf16[640,512]{1,0:T(8,128)(2,1)S(1)}, bf16[640,512]{1,0:T(8,128)(2,1)S(1)}) custom-call(s32[2]{0:T(128)S(1)} %pad_add_fusion.where_ref, bf16[64,40,128]{2,1,0:T(8,128)(2,1)S(1)} %all-to-all-done.block_ref, bf16[448,1024]{1,0:T(8,128)(2,1)S(1)} %bitcast.24, bf16[448,1024]{1,0:T(8,128)(2,1)S(1)} %bitcast.25, s32[320,1]{1,0:T(8,128)S(1)} %copy-done.2), custom_call_target="tpu_custom_call" | custom-call | tf_op jit(solution)/shard_map/pallas_call | solution.py:322
  51.9 1.9 %collective-permute-start = (bf16[640,512]{1,0:T(8,128)(2,1)S(1)}, bf16[640,512]{1,0:T(8,128)(2,1)S(1)}, u32[]{:S(2)}, u32[]{:S(2)}) collective-permute-start(bf16[640,512]{1,0:T(8,128)(2,1)S(1)} %get-tuple-element.12), channel_id=1, source_target_pairs={{0,1},{1,0},{2,3},{3,2},{4,5},{5,4},{6,7},{7,6},{8,9},{9,8},{10,11... | collective-permute-start | bytes 1966088 | tf_op jit(solution)/shard_map/ppermute | solution.py:20
  53.8 2.1 %collective-permute-done.right_ref = bf16[640,512]{1,0:T(8,128)(2,1)S(1)} collective-permute-done((bf16[640,512]{1,0:T(8,128)(2,1)S(1)}, bf16[640,512]{1,0:T(8,128)(2,1)S(1)}, u32[]{:S(2)}, u32[]{:S(2)}) %collective-permute-start) | collective-permute-done | bytes 655392 | tf_op jit(solution)/shard_map/ppermute | solution.py:20
  55.9 0.2 shard_map.142
  56.1 27.3 %all_to_all.20.pieces_ref = bf16[8,80,512]{2,1,0:T(8,128)(2,1)S(1)} all-to-all(bf16[8,80,512]{2,1,0:T(8,128)(2,1)S(1)} %bitcast.30), channel_id=1, replica_groups=mesh['z'=8,'yh'=4,'yl'=2,'x'=8,'c'=2] {'x'}, dimensions={0} | all-to-all | bytes 1310720 | tf_op jit(solution)/shard_map/all_to_all | solution.py:30
  83.4 0.1 shard_map.143
  83.5 22.0 %all_to_all.21 = bf16[8,80,512]{2,1,0:T(8,128)(2,1)S(1)} all-to-all(bf16[8,80,512]{2,1,0:T(8,128)(2,1)S(1)} %shard_map.143), channel_id=1, replica_groups=mesh['z'=8,'yh'=4,'yl'=2,'x'=8,'c'=2] {'x'}, dimensions={0} | all-to-all | bytes 1310720 | tf_op jit(solution)/shard_map/all_to_all | solution.py:30
  105.5 1.9 %collective-permute-start.1 = (bf16[640,512]{1,0:T(8,128)(2,1)S(1)}, bf16[640,512]{1,0:T(8,128)(2,1)S(1)}, u32[]{:S(2)}, u32[]{:S(2)}) collective-permute-start(bf16[640,512]{1,0:T(8,128)(2,1)S(1)} %bitcast.21), channel_id=1, source_target_pairs={{0,1},{1,0},{2,3},{3,2},{4,5},{5,4},{6,7},{7,6},{8,9},{9,8},{10,11... | collective-permute-start | bytes 1966088 | tf_op jit(solution)/shard_map/ppermute | solution.py:20
  107.4 2.1 %collective-permute-done.1.far_ref = bf16[640,512]{1,0:T(8,128)(2,1)S(1)} collective-permute-done((bf16[640,512]{1,0:T(8,128)(2,1)S(1)}, bf16[640,512]{1,0:T(8,128)(2,1)S(1)}, u32[]{:S(2)}, u32[]{:S(2)}) %collective-permute-start.1) | collective-permute-done | bytes 655392 | tf_op jit(solution)/shard_map/ppermute | solution.py:20
  109.5 2.2 %shard_map.144 = bf16[32,40,128]{2,1,0:T(8,128)(2,1)S(1)} custom-call(s32[1]{0:T(128)} %bitcast.core_ref, bf16[640,512]{1,0:T(8,128)(2,1)S(1)} %bitcast.22, bf16[640,512]{1,0:T(8,128)(2,1)S(1)} %collective-permute-done.1.far_ref, bf16[640,1024]{1,0:T(8,128)(2,1)S(1)} %copy-done.1, bf16[640,1024]{1,0:T(8,128)(2,1)S(1)} %fusion.3.up_ref, ...), custom_call_target="tpu_custom_call" | custom-call | tf_op jit(solution)/shard_map/pallas_call | solution.py:356
  111.7 2.7 %collective-permute-start.2 = (bf16[32,40,128]{2,1,0:T(8,128)(2,1)S(1)}, bf16[32,40,128]{2,1,0:T(8,128)(2,1)S(1)}, u32[]{:S(2)}, u32[]{:S(2)}) collective-permute-start(bf16[32,40,128]{2,1,0:T(8,128)(2,1)S(1)} %shard_map.144), channel_id=1, source_target_pairs={{0,16},{16,0},{1,17},{17,1},{2,18},{18,2},{3,19},{19,3},{4,20},{20... | collective-permute-start | bytes 983048 | tf_op jit(solution)/shard_map/ppermute | solution.py:20
  114.4 2.2 %shard_map.145.left_ref = bf16[32,40,128]{2,1,0:T(8,128)(2,1)S(1)} custom-call(s32[1]{0:T(128)} %bitcast.core_ref, bf16[640,512]{1,0:T(8,128)(2,1)S(1)} %bitcast.23, bf16[640,512]{1,0:T(8,128)(2,1)S(1)} %collective-permute-done.1.far_ref, bf16[640,1024]{1,0:T(8,128)(2,1)S(1)} %copy-done.1, bf16[640,1024]{1,0:T(8,128)(2,1)S(1)} %fusion.3.up_ref, ...), custom_call_target="tpu_custom_call" | custom-call | tf_op jit(solution)/shard_map/pallas_call | solution.py:356
  116.6 6.7 %collective-permute-done.2.right_ref = bf16[32,40,128]{2,1,0:T(8,128)(2,1)S(1)} collective-permute-done((bf16[32,40,128]{2,1,0:T(8,128)(2,1)S(1)}, bf16[32,40,128]{2,1,0:T(8,128)(2,1)S(1)}, u32[]{:S(2)}, u32[]{:S(2)}) %collective-permute-start.2) | collective-permute-done | bytes 327712 | tf_op jit(solution)/shard_map/ppermute | solution.py:20
  123.3 0.1 shard_map.146
  123.4 19.0 %all_to_all.22.back_ref = bf16[32,40,128]{2,1,0:T(8,128)(2,1)S(1)} all-to-all(bf16[32,40,128]{2,1,0:T(8,128)(2,1)S(1)} %shard_map.146), channel_id=1, replica_groups={{0,32,80,112,128,160,208,240,256,288,336,368,384,416,464,496,512,544,59..., dimensions={0} | all-to-all | bytes 655360 | tf_op jit(solution)/shard_map/all_to_all | solution.py:40
  142.5 1.8 %shard_map.147 = (bf16[448,128]{1,0:T(8,128)(2,1)}, bf16[2,128]{1,0:T(2,128)(2,1)}) custom-call(bf16[32,40,128]{2,1,0:T(8,128)(2,1)S(1)} %all_to_all.22.back_ref, s32[2,128]{1,0:T(2,128)S(1)} %bitcast.32, f32[2,128]{1,0:T(2,128)S(1)} %bitcast.33, bf16[320,32]{1,0:T(8,128)(2,1)S(1)} %copy-done.8, s32[320,1]{1,0:T(8,128)S(1)} %copy-done.7, ...), custom_call_target="tpu_custom_call" | custom-call | tf_op jit(solution)/shard_map/pallas_call | solution.py:265
  (25 shorter events, 0.1 us)
Async XLA Ops:
  0.6 26.5 %copy-start = (bf16[1,1024,640]{2,1,0:T(8,128)(2,1)S(1)}, bf16[1,1024,640]{2,1,0:T(8,128)(2,1)}, u32[]{:S(2)}) copy-start(bf16[1,1024,640]{2,1,0:T(8,128)(2,1)} %param.17) | copy-start | bytes 3932164
  3.7 45.1 %all-to-all-start = ((bf16[64,40,128]{2,1,0:T(8,128)(2,1)}), bf16[64,40,128]{2,1,0:T(8,128)(2,1)S(1)}, u32[]{:S(2)}, u32[]{:S(2)}) async-start(bf16[64,40,128]{2,1,0:T(8,128)(2,1)} %bitcast.34), calls=%async_computation | async-start | bytes 1310720 | tf_op jit(solution)/shard_map/all_to_all | solution.py:303
  27.1 1.3 copy-start.12
  28.5 20.3 %copy-start.2 = (s32[320,1]{1,0:T(8,128)S(1)}, s32[320,1]{1,0:T(8,128)}, u32[]{:S(2)}) copy-start(s32[320,1]{1,0:T(8,128)} %constant.100.clone.rank_ref) | copy-start | bytes 3844
  48.8 1.2 copy-start.3
  51.9 4.0 %collective-permute-start = (bf16[640,512]{1,0:T(8,128)(2,1)S(1)}, bf16[640,512]{1,0:T(8,128)(2,1)S(1)}, u32[]{:S(2)}, u32[]{:S(2)}) collective-permute-start(bf16[640,512]{1,0:T(8,128)(2,1)S(1)} %get-tuple-element.12), channel_id=1, source_target_pairs={{0,1},{1,0},{2,3},{3,2},{4,5},{5,4},{6,7},{7,6},{8,9},{9,8},{10,11... | collective-permute-start | bytes 1966088 | tf_op jit(solution)/shard_map/ppermute | solution.py:20
  56.0 53.4 %copy-start.5 = (bf16[1,448,1024]{2,1,0:T(8,128)(2,1)S(1)}, bf16[1,448,1024]{2,1,0:T(8,128)(2,1)}, u32[]{:S(2)}) copy-start(bf16[1,448,1024]{2,1,0:T(8,128)(2,1)} %param.19) | copy-start | bytes 2752516
  83.4 26.1 %copy-start.1 = (bf16[640,1024]{1,0:T(8,128)(2,1)S(1)}, bf16[640,1024]{1,0:T(8,128)(2,1)}, u32[]{:S(2)}) copy-start(bf16[640,1024]{1,0:T(8,128)(2,1)} %fusion.2.gate_ref) | copy-start | bytes 3932164
  83.4 26.1 %copy-start.4 = (bf16[1,448,1024]{2,1,0:T(8,128)(2,1)S(1)}, bf16[1,448,1024]{2,1,0:T(8,128)(2,1)}, u32[]{:S(2)}) copy-start(bf16[1,448,1024]{2,1,0:T(8,128)(2,1)} %param.18) | copy-start | bytes 2752516
  83.4 26.1 %copy-start.6 = (bf16[320,400]{1,0:T(8,128)(2,1)S(1)}, bf16[320,400]{1,0:T(8,128)(2,1)}, u32[]{:S(2)}) copy-start(bf16[320,400]{1,0:T(8,128)(2,1)} %constant.103.clone.put_ref) | copy-start | bytes 768004
  105.5 4.0 %collective-permute-start.1 = (bf16[640,512]{1,0:T(8,128)(2,1)S(1)}, bf16[640,512]{1,0:T(8,128)(2,1)S(1)}, u32[]{:S(2)}, u32[]{:S(2)}) collective-permute-start(bf16[640,512]{1,0:T(8,128)(2,1)S(1)} %bitcast.21), channel_id=1, source_target_pairs={{0,1},{1,0},{2,3},{3,2},{4,5},{5,4},{6,7},{7,6},{8,9},{9,8},{10,11... | collective-permute-start | bytes 1966088 | tf_op jit(solution)/shard_map/ppermute | solution.py:20
  111.7 11.6 %collective-permute-start.2 = (bf16[32,40,128]{2,1,0:T(8,128)(2,1)S(1)}, bf16[32,40,128]{2,1,0:T(8,128)(2,1)S(1)}, u32[]{:S(2)}, u32[]{:S(2)}) collective-permute-start(bf16[32,40,128]{2,1,0:T(8,128)(2,1)S(1)} %shard_map.144), channel_id=1, source_target_pairs={{0,16},{16,0},{1,17},{17,1},{2,18},{18,2},{3,19},{19,3},{4,20},{20... | collective-permute-start | bytes 983048 | tf_op jit(solution)/shard_map/ppermute | solution.py:20
  116.6 25.9 %copy-start.7 = (s32[320,1]{1,0:T(8,128)S(1)}, s32[320,1]{1,0:T(8,128)}, u32[]{:S(2)}) copy-start(s32[320,1]{1,0:T(8,128)} %constant.99.clone.expert_ref) | copy-start | bytes 3844
  116.6 25.9 %copy-start.8 = (bf16[320,32]{1,0:T(8,128)(2,1)S(1)}, bf16[320,32]{1,0:T(8,128)(2,1)}, u32[]{:S(2)}) copy-start(bf16[320,32]{1,0:T(8,128)(2,1)} %constant.101.clone.widen_ref) | copy-start | bytes 61444
  116.6 25.9 %copy-start.9 = (bf16[400,320]{1,0:T(8,128)(2,1)S(1)}, bf16[400,320]{1,0:T(8,128)(2,1)}, u32[]{:S(2)}) copy-start(bf16[400,320]{1,0:T(8,128)(2,1)} %constant.102.clone.pick_ref) | copy-start | bytes 768004
  116.6 25.9 %copy-start.10 = (s32[128,2]{0,1:T(2,128)S(1)}, s32[128,2]{0,1:T(2,128)}, u32[]{:S(2)}) copy-start(s32[128,2]{0,1:T(2,128)} %param.14) | copy-start | bytes 3076
  116.6 25.9 %copy-start.11 = (f32[128,2]{0,1:T(2,128)S(1)}, f32[128,2]{0,1:T(2,128)}, u32[]{:S(2)}) copy-start(f32[128,2]{0,1:T(2,128)} %param.15) | copy-start | bytes 3076
